TPU v7x, 32 devices: a whole 2x2x4 slice. The times are simulated.
32 devices in a mesh: dp: 2 (over y), expert: 16 (over z, x, core).
Axes of the slice: x: 2, y: 2, z: 4, core: 2. Of those that a mesh axis runs over, the one named last changes fastest.
Arguments:
- tokens: bfloat16 [768, 4096], P(('dp', 'expert')), may hold values from -6 to 6
- out_grad: bfloat16 [768, 4096], P(('dp', 'expert')), may hold values from -6 to 6
- routes: int32 [768, 8], P(('dp', 'expert')), may hold values from 0 to 15, all different within a row; in each aligned block of 24 rows (0 to 23, 24 to 47, ...) at most 18 rows name the same one
- gates: bfloat16 [768, 8], P(('dp', 'expert')), may hold values from 0.099609375 to 0.5
- w_gate: bfloat16 [16, 768, 4096], P('expert', 'dp'), may hold values from -0.09375 to 0.09375
- w_up: bfloat16 [16, 768, 4096], P('expert', 'dp'), may hold values from -0.09375 to 0.09375
- w_down: bfloat16 [16, 768, 4096], P('expert', 'dp'), may hold values from -0.21875 to 0.21875
Outputs:
- d_tokens: bfloat16 [768, 4096], P(('dp', 'expert'))
- d_gate: bfloat16 [16, 768, 4096], P('expert', 'dp')
- d_up: bfloat16 [16, 768, 4096], P('expert', 'dp')
- d_down: bfloat16 [16, 768, 4096], P('expert', 'dp')
Inputs may be any that keep to these rules, and one draw needn't show every extreme that they name: `routes`: each row names 8 different experts. Within the 24 rows of one device no expert is named by more than 18 rows, and in every draw some expert is named by exactly 18 rows of some device.
All inputs are finite; a program needn't handle non-finite values.
Results may differ from a plain program's by a relative error of at most 0.015.
Values may be sent and summed in bfloat16 or wider, within the bound.
No kernel may reach another device: no remote copies, remote signals or barrier semaphores. Data moves between devices by JAX's collectives and lax.ppermute only.
A program may use at most 128 MiB of HBM per device.

v0:
```python
from functools import partial

import jax
import jax.numpy as jnp
from jax import lax
from jax.sharding import PartitionSpec as P


def cell_match(routes, experts, capacity):
    expert_ids = jnp.arange(experts, dtype=jnp.int32)
    onehot = (routes[:, :, None] == expert_ids).astype(jnp.int32)
    chosen = jnp.sum(onehot, axis=1)
    earlier = jnp.cumsum(chosen, axis=0) - chosen
    slot_index = jnp.sum(onehot * earlier[:, None, :], axis=2)
    target = routes * capacity + slot_index
    cell_ids = jnp.arange(experts * capacity, dtype=jnp.int32)
    return target[:, :, None] == cell_ids


def placement(matches, experts, capacity):
    return jnp.any(matches, axis=1).reshape(-1, experts, capacity).astype(jnp.bfloat16)


def weighting(matches, gates, experts, capacity):
    spread = jnp.where(matches, gates.astype(jnp.float32)[:, :, None], 0.0)
    return jnp.sum(spread, axis=1).reshape(-1, experts, capacity)


def per_device(tokens, out_grad, routes, gates, w_gate, w_up, w_down):
    tok_rows, features = tokens.shape
    top_count = routes.shape[1]
    experts = lax.axis_size("expert")
    groups = lax.axis_size("dp")
    capacity = max(2, min(tok_rows, 3 * tok_rows * top_count // (2 * experts)))
    match_fn = partial(cell_match, experts=experts, capacity=capacity)
    place_fn = partial(placement, experts=experts, capacity=capacity)
    weight_fn = partial(weighting, experts=experts, capacity=capacity)
    own_match = match_fn(routes)
    own_place = place_fn(own_match)
    own_weight = weight_fn(own_match, gates)
    input_send = jnp.einsum(
        "tec,td->ecd", own_place, tokens, preferred_element_type=jnp.float32
    ).astype(jnp.bfloat16)
    grad_send = jnp.einsum(
        "tec,td->ecd", own_weight, out_grad.astype(jnp.float32), precision=lax.Precision.HIGHEST
    ).astype(jnp.bfloat16)
    input_recv, grad_recv = (
        lax.all_to_all(input_send, "expert", split_axis=0, concat_axis=0, tiled=True),
        lax.all_to_all(grad_send, "expert", split_axis=0, concat_axis=0, tiled=True),
    )
    input_recv = input_recv.reshape(experts, 1, capacity, features)
    grad_recv = grad_recv.reshape(experts, 1, capacity, features)
    input_slots, grad_slots = (
        lax.all_gather(input_recv, "dp", axis=1, tiled=True),
        lax.all_gather(grad_recv, "dp", axis=1, tiled=True),
    )
    input_rows = input_slots.reshape(-1, features)
    grad_rows = grad_slots.reshape(-1, features)
    gate_w = w_gate[0]
    up_w = w_up[0]
    down_w = w_down[0]
    gate_pre = jnp.einsum("rd,fd->rf", input_rows, gate_w, preferred_element_type=jnp.float32)
    up_pre = jnp.einsum("rd,fd->rf", input_rows, up_w, preferred_element_type=jnp.float32)
    sigmoid_gate = jax.nn.sigmoid(gate_pre)
    silu_gate = gate_pre * sigmoid_gate
    hidden = (silu_gate * up_pre).astype(jnp.bfloat16)
    d_hidden = jnp.einsum("rd,fd->rf", grad_rows, down_w, preferred_element_type=jnp.float32)
    d_up_act = (d_hidden * silu_gate).astype(jnp.bfloat16)
    d_gate_act = (
        d_hidden * up_pre * sigmoid_gate * (1.0 + gate_pre * (1.0 - sigmoid_gate))
    ).astype(jnp.bfloat16)
    grad_down = jnp.einsum(
        "rf,rd->fd", hidden, grad_rows, preferred_element_type=jnp.float32
    ).astype(jnp.bfloat16)
    grad_gate = jnp.einsum(
        "rf,rd->fd", d_gate_act, input_rows, preferred_element_type=jnp.float32
    ).astype(jnp.bfloat16)
    grad_up = jnp.einsum(
        "rf,rd->fd", d_up_act, input_rows, preferred_element_type=jnp.float32
    ).astype(jnp.bfloat16)
    partial_sum = jnp.einsum("rf,fd->rd", d_gate_act, gate_w, preferred_element_type=jnp.float32)
    partial_sum = partial_sum + jnp.einsum(
        "rf,fd->rd", d_up_act, up_w, preferred_element_type=jnp.float32
    )
    rounded = partial_sum.astype(jnp.bfloat16).reshape(experts, groups, capacity, features)
    held = lax.optimization_barrier(rounded).astype(jnp.float32)
    slot_total = lax.psum_scatter(
        held.astype(jnp.bfloat16), "dp", scatter_dimension=1, tiled=True
    ).astype(jnp.float32)
    returned = lax.all_to_all(
        slot_total[:, 0].astype(jnp.bfloat16), "expert", split_axis=0, concat_axis=0, tiled=True
    ).astype(jnp.float32)
    summed = jnp.einsum(
        "tec,ecd->td", own_place.astype(jnp.float32), returned, precision=lax.Precision.HIGHEST
    )
    return (summed.astype(jnp.bfloat16), grad_gate[None], grad_up[None], grad_down[None])


def solution(mesh):
    in_specs = (
        P(("dp", "expert"), None),
        P(("dp", "expert"), None),
        P(("dp", "expert"), None),
        P(("dp", "expert"), None),
        P("expert", "dp", None),
        P("expert", "dp", None),
        P("expert", "dp", None),
    )
    out_specs = (
        P(("dp", "expert"), None),
        P("expert", "dp", None),
        P("expert", "dp", None),
        P("expert", "dp", None),
    )
    return jax.shard_map(
        per_device, mesh=mesh, in_specs=in_specs, out_specs=out_specs, check_vma=False
    )
```

profile of v0, /device:TPU:11, one launch (start us, length us, event | category | flops | bytes accessed | tf_op | source)
XLA Modules:
  0.0 446.9 jit_solution(10988848814832716835)
XLA Ops:
  7.2 0.9 convert_reduce_fusion
  8.2 0.7 select_reduce_fusion.1
  9.0 0.7 multiply_add_fusion
  9.7 0.8 copy.38
  10.5 0.2 select_reduce_fusion
  10.8 5.0 %convolution_convert_fusion.4 = bf16[16,18,4096]{2,1,0:T(8,128)(2,1)} fusion(bf16[24,4096]{1,0:T(8,128)(2,1)} %param.8, f32[24,16,18]{2,1,0:T(8,128)S(1)} %reshape.43), kind=kOutput, calls=%fused_computation.5 | convolution fusion | flops 340918272 | bytes 2583552 | tf_op jit(solution)/shard_map/tec,td->ecd/dot_general | solution.py:44
  15.8 6.6 %all-to-all-start = ((bf16[16,18,4096]{2,1,0:T(8,128)(2,1)}), bf16[16,18,4096]{2,1,0:T(8,128)(2,1)}, u32[]{:S(2)}, u32[]{:S(2)}) async-start(bf16[16,18,4096]{2,1,0:T(8,128)(2,1)} %convolution_convert_fusion.4), calls=%async_computation | async-start | bytes 6291456 | tf_op jit(solution)/shard_map/all_to_all | solution.py:49
  22.4 0.2 fusion.14
  22.7 69.6 %all-to-all-done = bf16[16,18,4096]{2,1,0:T(8,128)(2,1)} async-done(((bf16[16,18,4096]{2,1,0:T(8,128)(2,1)}), bf16[16,18,4096]{2,1,0:T(8,128)(2,1)}, u32[]{:S(2)}, u32[]{:S(2)}) %all-to-all-start) | async-done | bytes 2359328 | tf_op jit(solution)/shard_map/all_to_all | solution.py:49
  92.3 4.6 %copy.40 = bf16[16,18,4096]{2,0,1:T(8,128)(2,1)} copy(bf16[16,18,4096]{2,1,0:T(8,128)(2,1)} %all-to-all-done) | data formatting | bytes 4718592 | tf_op jit(solution)/shard_map/all_to_all | solution.py:49
  97.0 1.0 convolution_convert_fusion.3
  98.0 74.5 %all_to_all.15 = bf16[16,18,4096]{2,1,0:T(8,128)(2,1)S(1)} all-to-all(bf16[16,18,4096]{2,1,0:T(8,128)(2,1)S(1)} %convolution_convert_fusion.3), channel_id=1, replica_groups=mesh['dp'=2,'expert'=16] {'expert'}, dimensions={0} | all-to-all | bytes 4718592 | tf_op jit(solution)/shard_map/all_to_all | solution.py:48
  172.5 2.7 copy.43
  175.3 7.3 %copy.41 = bf16[16,36,4096]{2,1,0:T(8,128)(2,1)} copy(bf16[16,36,4096]{2,0,1:T(8,128)(2,1)} %all-gather.5.cloned.1.call-done) | data formatting | bytes 9437184 | tf_op jit(solution)/shard_map/all_gather | solution.py:55
  182.6 7.6 %reshape.45 = bf16[576,4096]{1,0:T(8,128)(2,1)} reshape(bf16[16,36,4096]{2,1,0:T(8,128)(2,1)} %copy.41) | data formatting | bytes 9437184 | tf_op jit(solution)/shard_map/reshape | solution.py:58
  190.2 47.6 %all-gather.7.cloned.1.call-done = bf16[16,36,4096]{2,0,1:T(8,128)(2,1)} async-done(((bf16[16,18,4096]{2,0,1:T(8,128)(2,1)}), bf16[16,36,4096]{2,0,1:T(8,128)(2,1)}) %all-gather.7.cloned.1.call-update) | async-done | bytes 4718608 | tf_op jit(solution)/shard_map/all_gather | solution.py:54
  237.8 7.3 %copy.44 = bf16[16,36,4096]{2,1,0:T(8,128)(2,1)} copy(bf16[16,36,4096]{2,0,1:T(8,128)(2,1)} %all-gather.7.cloned.1.call-done) | data formatting | bytes 9437184 | tf_op jit(solution)/shard_map/all_gather | solution.py:54
  245.1 7.2 %reshape.47 = bf16[576,4096]{1,0:T(8,128)(2,1)} reshape(bf16[16,36,4096]{2,1,0:T(8,128)(2,1)} %copy.44) | data formatting | bytes 9437184 | tf_op jit(solution)/shard_map/reshape | solution.py:57
  252.3 4.8 %fusion.6 = f32[576,384]{1,0:T(8,128)S(1)} fusion(bf16[576,4096]{1,0:T(8,128)(2,1)} %reshape.47, bf16[1,384,4096]{2,1,0:T(8,128)(2,1)S(1)} %copy-done), kind=kOutput, calls=%fused_computation.13 | convolution fusion | flops 1811939328 | bytes 8749056 | tf_op jit(solution)/shard_map/rd,fd->rf/dot_general | solution.py:62
  257.2 2.6 fusion.9
  259.8 2.8 multiply_convert_fusion.1
  262.7 2.6 fusion.4
  265.3 4.3 add_convert_fusion
  269.7 7.6 %reshape.48 = bf16[16,2,18,4096]{3,2,1,0:T(8,128)(2,1)} reshape(bf16[576,4096]{1,0:T(8,128)(2,1)} %add_convert_fusion) | data formatting | bytes 9437184 | tf_op jit(solution)/shard_map/reshape | solution.py:85
  277.2 6.2 %copy.45 = bf16[16,2,18,4096]{3,2,0,1:T(8,128)(2,1)} copy(bf16[16,2,18,4096]{3,2,1,0:T(8,128)(2,1)} %reshape.48) | data formatting | bytes 9437184 | tf_op jit(solution)/shard_map/optimization_barrier | solution.py:86
  283.5 77.2 %reduce-scatter.2.cloned.1.call-done = bf16[16,1,18,4096]{3,2,0,1:T(8,128)(2,1)} async-done(((bf16[16,2,18,4096]{3,2,0,1:T(8,128)(2,1)}), bf16[16,1,18,4096]{3,2,0,1:T(8,128)(2,1)}) %reduce-scatter.2.cloned.1.call-update) | async-done | bytes 2359312 | tf_op jit(solution)/shard_map/reduce_scatter | solution.py:87
  360.7 6.4 %all-to-all-start.2 = ((bf16[16,18,4096]{2,1,0:T(8,128)(2,1)}), bf16[16,18,4096]{2,1,0:T(8,128)(2,1)}, u32[]{:S(2)}, u32[]{:S(2)}) async-start(bf16[16,18,4096]{2,1,0:T(8,128)(2,1)} %bitcast.47), calls=%async_computation.3 | async-start | bytes 6291456 | tf_op jit(solution)/shard_map/all_to_all | solution.py:90
  367.1 6.8 %fusion.1 = bf16[1,384,4096]{2,1,0:T(8,128)(2,1)} fusion(bf16[576,384]{1,0:T(8,128)(2,1)S(1)} %copy-done.4, bf16[576,4096]{1,0:T(8,128)(2,1)} %reshape.47), kind=kOutput, calls=%fused_computation.7 | convolution fusion | flops 1813512192 | bytes 8306688 | tf_op jit(solution)/shard_map/rf,rd->fd/dot_general | solution.py:78
  373.9 6.8 %fusion = bf16[1,384,4096]{2,1,0:T(8,128)(2,1)} fusion(bf16[576,384]{1,0:T(8,128)(2,1)S(1)} %copy-done.7, bf16[576,4096]{1,0:T(8,128)(2,1)} %reshape.47), kind=kOutput, calls=%fused_computation.6 | convolution fusion | flops 1813512192 | bytes 8306688 | tf_op jit(solution)/shard_map/rf,rd->fd/dot_general | solution.py:75
  380.7 4.1 fusion.2
  384.8 52.2 %all-to-all-done.2 = bf16[16,18,4096]{2,1,0:T(8,128)(2,1)} async-done(((bf16[16,18,4096]{2,1,0:T(8,128)(2,1)}), bf16[16,18,4096]{2,1,0:T(8,128)(2,1)}, u32[]{:S(2)}, u32[]{:S(2)}) %all-to-all-start.2) | async-done | bytes 2359328 | tf_op jit(solution)/shard_map/all_to_all | solution.py:90
  437.1 3.3 fusion.3
  (52 shorter events, 0.9 us)
Async XLA Ops:
  7.2 245.2 %copy-start = (bf16[1,384,4096]{2,1,0:T(8,128)(2,1)S(1)}, bf16[1,384,4096]{2,1,0:T(8,128)(2,1)}, u32[]{:S(2)}) copy-start(bf16[1,384,4096]{2,1,0:T(8,128)(2,1)} %param.11) | copy-start | bytes 9437188
  15.8 76.6 %all-to-all-start = ((bf16[16,18,4096]{2,1,0:T(8,128)(2,1)}), bf16[16,18,4096]{2,1,0:T(8,128)(2,1)}, u32[]{:S(2)}, u32[]{:S(2)}) async-start(bf16[16,18,4096]{2,1,0:T(8,128)(2,1)} %convolution_convert_fusion.4), calls=%async_computation | async-start | bytes 6291456 | tf_op jit(solution)/shard_map/all_to_all | solution.py:49
  22.3 74.7 %copy-start.8 = (bf16[24,4096]{1,0:T(8,128)(2,1)S(1)}, bf16[24,4096]{1,0:T(8,128)(2,1)}, u32[]{:S(2)}) copy-start(bf16[24,4096]{1,0:T(8,128)(2,1)} %param.7) | copy-start | bytes 589828
  22.3 153.0 %all-gather.5.cloned.1.call-start = ((), (), s32[]{:S(2)}) async-start(), calls=%async_computation.5 | async-start | bytes 7077888 | tf_op jit(solution)/shard_map/all_gather | solution.py:55
  96.9 140.9 %all-gather.7.cloned.1.call-start = ((), (), s32[]{:S(2)}) async-start(), calls=%async_computation.6 | async-start | bytes 7077888 | tf_op jit(solution)/shard_map/all_gather | solution.py:54
  175.2 185.5 %reduce-scatter.2.cloned.1.call-start = ((), (), s32[]{:S(2)}) async-start(), calls=%async_computation.4 | async-start | bytes 9437184 | tf_op jit(solution)/shard_map/reduce_scatter | solution.py:87
  252.3 4.8 %copy-start.2 = (bf16[576,4096]{1,0:T(8,128)(2,1)S(1)}, bf16[576,4096]{1,0:T(8,128)(2,1)}, u32[]{:S(2)}) copy-start(bf16[576,4096]{1,0:T(8,128)(2,1)} %reshape.47) | copy-start | bytes 14155780
  252.3 4.8 %copy-start.5 = (bf16[1,384,4096]{2,1,0:T(8,128)(2,1)S(1)}, bf16[1,384,4096]{2,1,0:T(8,128)(2,1)}, u32[]{:S(2)}) copy-start(bf16[1,384,4096]{2,1,0:T(8,128)(2,1)} %param.12) | copy-start | bytes 9437188
  252.3 7.5 %slice-start = ((s8[4718592]{0:T(1024)(128)(4,1)}), s8[4194304]{0:T(1024)(128)(4,1)S(1)}, s32[]{:S(2)}) async-start(s8[4718592]{0:T(1024)(128)(4,1)} %bitcast.43), calls=%async_computation.7 | async-start | bytes 8388608
  257.1 2.7 copy-start.10
  257.1 2.7 slice-start.1
  257.2 2.7 copy-start.9
  259.8 2.8 copy-start.12
  262.7 2.6 copy-start.6
  262.7 2.6 copy-start.3
  283.5 83.6 %copy-start.4 = (bf16[576,384]{1,0:T(8,128)(2,1)S(1)}, bf16[576,384]{1,0:T(8,128)(2,1)}, u32[]{:S(2)}) copy-start(bf16[576,384]{1,0:T(8,128)(2,1)} %copy-done.3) | copy-start | bytes 1327108
  360.7 76.4 %all-to-all-start.2 = ((bf16[16,18,4096]{2,1,0:T(8,128)(2,1)}), bf16[16,18,4096]{2,1,0:T(8,128)(2,1)}, u32[]{:S(2)}, u32[]{:S(2)}) async-start(bf16[16,18,4096]{2,1,0:T(8,128)(2,1)} %bitcast.47), calls=%async_computation.3 | async-start | bytes 6291456 | tf_op jit(solution)/shard_map/all_to_all | solution.py:90
  367.1 6.8 %copy-start.7 = (bf16[576,384]{1,0:T(8,128)(2,1)S(1)}, bf16[576,384]{1,0:T(8,128)(2,1)}, u32[]{:S(2)}) copy-start(bf16[576,384]{1,0:T(8,128)(2,1)} %copy-done.6) | copy-start | bytes 1327108
  367.1 13.6 %slice-start.2 = ((s8[4718592]{0:T(1024)(128)(4,1)}), s8[4194304]{0:T(1024)(128)(4,1)S(1)}, s32[]{:S(2)}) async-start(s8[4718592]{0:T(1024)(128)(4,1)} %bitcast.45), calls=%async_computation.9 | async-start | bytes 8388608
  373.9 6.8 %slice-start.3 = ((s8[4718592]{0:T(1024)(128)(4,1)}), s8[524288]{0:T(1024)(128)(4,1)S(1)}, s32[]{:S(2)}) async-start(s8[4718592]{0:T(1024)(128)(4,1)} %bitcast.45), calls=%async_computation.10 | async-start | bytes 1048576
  373.9 6.8 %copy-start.11 = (f32[576,384]{1,0:T(8,128)S(1)}, f32[576,384]{1,0:T(8,128)}, u32[]{:S(2)}) copy-start(f32[576,384]{1,0:T(8,128)} %copy-done.10) | copy-start | bytes 2654212
  373.9 6.8 %copy-start.13 = (f32[576,384]{1,0:T(8,128)S(1)}, f32[576,384]{1,0:T(8,128)}, u32[]{:S(2)}) copy-start(f32[576,384]{1,0:T(8,128)} %copy-done.12) | copy-start | bytes 2654212
  380.7 59.7 %copy-start.1 = (bf16[1,384,4096]{2,1,0:T(8,128)(2,1)S(1)}, bf16[1,384,4096]{2,1,0:T(8,128)(2,1)}, u32[]{:S(2)}) copy-start(bf16[1,384,4096]{2,1,0:T(8,128)(2,1)} %param.11) | copy-start | bytes 9437188
Sparse Core Ops, SparseCore 0:
  97.1 62.1 all-gather.4
  175.3 62.4 all-gather.6
  283.6 77.0 reduce-scatter.1
where the time goes:
time: 448 us; the launch traced here: 447 us
  waiting for transfers between devices  247 us (55%)
  blocking collectives  74.5 us (17%)
  local copies, waits for them, and re-layouts  51.9 us (12%)
  matrix products  44.1 us (10%)
  between operations  14 us (3%)
  starting transfers between devices  13.1 us (3%)
    reduce_scatter x1, waiting for transfers between devices, per_device(): lax.psum_scatter(held.astype(jnp.bfloat16), 'dp', scatter_dimension=1, ti...  77.2 us
    all_to_all x1, blocking collectives, per_device(): lax.all_to_all(input_send, 'expert', split_axis=0, concat_axis=0, tiled=T...  74.5 us
    all_to_all x1, waiting for transfers between devices, per_device(): lax.all_to_all(grad_send, 'expert', split_axis=0, concat_axis=0, tiled=True)  69.6 us
    all_to_all x1, waiting for transfers between devices, per_device(): lax.all_to_all(slot_total[:, 0].astype(jnp.bfloat16), 'expert', split_axi...  52.2 us
    all_gather x1, waiting for transfers between devices, per_device(): lax.all_gather(input_recv, 'dp', axis=1, tiled=True)  47.6 us
  transfers between devices with their start and end apart: 5, of which 4 were waited for; matrix products, arithmetic and copies ran while one was open for 8% of the time, Pallas kernels for 0%

commit v1 on v0

--- a/solution.py
+++ b/solution.py
@@ -26,7 +26,7 @@
     return jnp.sum(spread, axis=1).reshape(-1, experts, capacity)
 
 
-def per_device(tokens, out_grad, routes, gates, w_gate, w_up, w_down):
+def slot_plan(tokens, out_grad, routes, gates, w_gate, w_up, w_down):
     tok_rows, features = tokens.shape
     top_count = routes.shape[1]
     experts = lax.axis_size("expert")
@@ -96,6 +96,107 @@
     return (summed.astype(jnp.bfloat16), grad_gate[None], grad_up[None], grad_down[None])
 
 
+def swapped(x, axis, bits):
+    count = lax.axis_size(axis)
+    return lax.ppermute(x, axis, [(i, i ^ bits) for i in range(count)])
+
+
+def gate_of_expert(routes, gates, experts):
+    hit = routes[:, :, None] == jnp.arange(experts, dtype=jnp.int32)
+    return jnp.sum(jnp.where(hit, gates[:, :, None], 0), axis=1).astype(jnp.bfloat16)
+
+
+def dense_plan(tokens, out_grad, routes, gates, w_gate, w_up, w_down):
+    rows, features = tokens.shape
+    half = features // 2
+    experts = lax.axis_size("expert")
+    layers = experts // 4
+    over_core = partial(swapped, axis="expert", bits=1)
+    over_x = partial(swapped, axis="expert", bits=2)
+    over_y = partial(swapped, axis="dp", bits=1)
+
+    def over_z(x, step):
+        return swapped(x, "expert", 4 * step) if step else x
+
+    def summed(x, y):
+        return (x.astype(jnp.float32) + y.astype(jnp.float32)).astype(jnp.bfloat16)
+
+    scales = gate_of_expert(routes, gates, experts)[None]
+    for move in (over_core, over_x, over_y):
+        scales = jnp.concatenate([scales, move(scales)])
+    scales = jnp.stack([over_z(scales, step) for step in range(layers)])
+    own = jnp.arange(experts, dtype=jnp.int32) == lax.axis_index("expert")
+    scales = jnp.sum(jnp.where(own, scales.astype(jnp.float32), 0.0), axis=-1)
+    scales = scales.reshape(layers, -1, 1)
+
+    gate_w = w_gate[0]
+    up_w = w_up[0]
+    down_w = w_down[0]
+    mine = jnp.stack([tokens, out_grad])
+    inputs, grads, hiddens, gate_acts, up_acts = [], [], [], [], []
+    total = None
+    for step in range(layers):
+        here = over_z(mine, step)
+        from_x = over_x(here)
+        from_y = over_y(here)
+        from_xy = jnp.concatenate(
+            [over_x(from_y[:, :, :half]), over_y(from_x[:, :, half:])], axis=2
+        )
+        lane = jnp.stack([here, from_x, from_y, from_xy], axis=1)
+        both = jnp.stack([lane, over_core(lane)], axis=2)
+        both = both.reshape(2, -1, features)
+        x_rows, g_rows = both[0], both[1]
+        scale = scales[step]
+        gate_pre = jnp.einsum("rd,fd->rf", x_rows, gate_w, preferred_element_type=jnp.float32)
+        up_pre = jnp.einsum("rd,fd->rf", x_rows, up_w, preferred_element_type=jnp.float32)
+        d_hidden = scale * jnp.einsum("rd,fd->rf", g_rows, down_w, preferred_element_type=jnp.float32)
+        sigmoid_gate = jax.nn.sigmoid(gate_pre)
+        silu_gate = gate_pre * sigmoid_gate
+        hidden = (scale * silu_gate * up_pre).astype(jnp.bfloat16)
+        d_up_act = (d_hidden * silu_gate).astype(jnp.bfloat16)
+        d_gate_act = (
+            d_hidden * up_pre * sigmoid_gate * (1.0 + gate_pre * (1.0 - sigmoid_gate))
+        ).astype(jnp.bfloat16)
+        part = jnp.einsum("rf,fd->rd", d_gate_act, gate_w, preferred_element_type=jnp.float32)
+        part = part + jnp.einsum("rf,fd->rd", d_up_act, up_w, preferred_element_type=jnp.float32)
+        part = part.astype(jnp.bfloat16).reshape(4, 2, rows, features)
+        lane_sum = summed(part[:, 0], over_core(part[:, 1]))
+        left, right = lane_sum[:, :, :half], lane_sum[:, :, half:]
+        left = summed(left[0::2], over_x(left[1::2]))
+        right = summed(right[:2], over_y(right[2:]))
+        left = summed(left[0], over_y(left[1]))
+        right = summed(right[0], over_x(right[1]))
+        back = over_z(jnp.concatenate([left, right], axis=1), step).astype(jnp.float32)
+        total = back if total is None else total + back
+        inputs.append(x_rows)
+        grads.append(g_rows)
+        hiddens.append(hidden)
+        gate_acts.append(d_gate_act)
+        up_acts.append(d_up_act)
+
+    def weight_grad(acts, sides):
+        return jnp.einsum(
+            "rf,rd->fd", acts, sides, preferred_element_type=jnp.float32
+        ).astype(jnp.bfloat16)[None]
+
+    all_inputs = jnp.concatenate(inputs)
+    return (
+        total.astype(jnp.bfloat16),
+        weight_grad(jnp.concatenate(gate_acts), all_inputs),
+        weight_grad(jnp.concatenate(up_acts), all_inputs),
+        weight_grad(jnp.concatenate(hiddens), jnp.concatenate(grads)),
+    )
+
+
+def per_device(tokens, out_grad, routes, gates, w_gate, w_up, w_down):
+    tok_rows, top_count = routes.shape
+    experts = lax.axis_size("expert")
+    capacity = max(2, min(tok_rows, 3 * tok_rows * top_count // (2 * experts)))
+    crowded = 2 * capacity >= tok_rows and lax.axis_size("dp") == 2 and experts in (4, 8, 16)
+    plan = dense_plan if crowded else slot_plan
+    return plan(tokens, out_grad, routes, gates, w_gate, w_up, w_down)
+
+
 def solution(mesh):
     in_specs = (
         P(("dp", "expert"), None),

time: 448 us -> 192 us (0.43)
  the two profiles are of different devices: /device:TPU:11 before, /device:TPU:0 now
where the time goes in v1:
time: 192 us; the launch traced here: 191 us
  waiting for transfers between devices  74.5 us (39%)
  starting transfers between devices  51.8 us (27%)
  matrix products  37.6 us (20%)
  other arithmetic  16.1 us (8%)
  local copies, waits for them, and re-layouts  9.26 us (5%)
    ppermute x52, waiting for transfers between devices, swapped(): return lax.ppermute(x, axis, [(i, i ^ bits) for i in range(count)])  74.5 us
    ppermute x52, starting transfers between devices, swapped(): return lax.ppermute(x, axis, [(i, i ^ bits) for i in range(count)])  51.8 us
    dot_general x3, matrix products, weight_grad(): jnp.einsum('rf,rd->fd', acts, sides, preferred_element_type=jnp.float32)  12.1 us
    dot_general x4, matrix products, dense_plan(): jnp.einsum('rd,fd->rf', x_rows, up_w, preferred_element_type=jnp.float32)  7.86 us
    another operation x8, other arithmetic, dense_plan(): both = jnp.stack([lane, over_core(lane)], axis=2)  6.21 us
    dot_general x4, matrix products, dense_plan(): jnp.einsum('rd,fd->rf', x_rows, gate_w, preferred_element_type=jnp.float32)  4.73 us
    dot_general x4, matrix products, dense_plan(): jnp.einsum('rd,fd->rf', g_rows, down_w, preferred_element_type=jnp.float32)  4.73 us
    dot_general x4, matrix products, dense_plan(): jnp.einsum('rf,fd->rd', d_up_act, up_w, preferred_element_type=jnp.float32)  4.3 us
  transfers between devices with their start and end apart: 52, of which 25 were waited for; matrix products, arithmetic and copies ran while one was open for 31% of the time, Pallas kernels for 0%

profile of v1, /device:TPU:0, one launch (start us, length us, event | category | flops | bytes accessed | tf_op | source)
XLA Modules:
  0.0 190.8 jit_solution(6775076818035548959)
XLA Ops:
  2.9 2.8 %collective-permute-start.1 = (bf16[2,24,16]{1,2,0:T(8,128)(2,1)S(1)}, bf16[2,24,16]{1,2,0:T(8,128)(2,1)S(1)}, u32[]{:S(2)}, u32[]{:S(2)}) collective-permute-start(bf16[2,24,16]{1,2,0:T(8,128)(2,1)S(1)} %pad_maximum_fusion.17), channel_id=1, source_target_pairs={{0,2},{1,3},{2,0},{3,1},{4,6},{5,7},{6,4},{7,5},{8,10},{9,11},{10,... | collective-permute-start | bytes 4616 | tf_op jit(solution)/shard_map/ppermute | solution.py:101
  5.7 1.8 fusion.115
  9.7 9.3 %collective-permute-done.2 = bf16[4,24,16]{1,2,0:T(8,128)(2,1)S(1)} collective-permute-done((bf16[4,24,16]{1,2,0:T(8,128)(2,1)S(1)}, bf16[4,24,16]{1,2,0:T(8,128)(2,1)S(1)}, u32[]{:S(2)}, u32[]{:S(2)}) %collective-permute-start.2) | collective-permute-done | bytes 3104 | tf_op jit(solution)/shard_map/ppermute | solution.py:101
  19.6 2.6 %collective-permute-start.4 = (bf16[8,24,16]{1,2,0:T(8,128)(2,1)}, bf16[8,24,16]{1,2,0:T(8,128)(2,1)}, u32[]{:S(2)}, u32[]{:S(2)}) collective-permute-start(bf16[8,24,16]{1,2,0:T(8,128)(2,1)} %get-tuple-element.35), channel_id=1, source_target_pairs={{0,8},{1,9},{2,10},{3,11},{4,12},{5,13},{6,14},{7,15},{8,0},{9,1},... | collective-permute-start | bytes 18440 | tf_op jit(solution)/shard_map/ppermute | solution.py:101
  22.2 1.6 collective-permute-start.3
  24.7 2.8 %collective-permute-start.28 = (bf16[2,24,4096]{2,1,0:T(8,128)(2,1)}, bf16[2,24,4096]{2,1,0:T(8,128)(2,1)}, u32[]{:S(2)}, u32[]{:S(2)}) collective-permute-start(bf16[2,24,4096]{2,1,0:T(8,128)(2,1)} %get-tuple-element.33), channel_id=1, source_target_pairs={{0,8},{1,9},{2,10},{3,11},{4,12},{5,13},{6,14},{7,15},{8,0},{9,1},... | collective-permute-start | bytes 1179656 | tf_op jit(solution)/shard_map/ppermute | solution.py:101
  27.5 1.8 collective-permute-start.16
  31.3 1.6 slice.281
  33.5 1.6 slice.282
  37.5 16.4 %collective-permute-done.28 = bf16[2,24,4096]{2,1,0:T(8,128)(2,1)} collective-permute-done((bf16[2,24,4096]{2,1,0:T(8,128)(2,1)}, bf16[2,24,4096]{2,1,0:T(8,128)(2,1)}, u32[]{:S(2)}, u32[]{:S(2)}) %collective-permute-start.28) | collective-permute-done | bytes 393248 | tf_op jit(solution)/shard_map/ppermute | solution.py:101
  60.5 5.6 %collective-permute-done.30 = bf16[2,24,4096]{2,1,0:T(8,128)(2,1)S(1)} collective-permute-done((bf16[2,24,4096]{2,1,0:T(8,128)(2,1)}, bf16[2,24,4096]{2,1,0:T(8,128)(2,1)S(1)}, u32[]{:S(2)}, u32[]{:S(2)}) %collective-permute-start.30) | collective-permute-done | bytes 393248 | tf_op jit(solution)/shard_map/ppermute | solution.py:101
  68.3 4.4 %collective-permute-done.18 = bf16[2,24,4096]{2,1,0:T(8,128)(2,1)S(1)} collective-permute-done((bf16[2,24,4096]{2,1,0:T(8,128)(2,1)}, bf16[2,24,4096]{2,1,0:T(8,128)(2,1)S(1)}, u32[]{:S(2)}, u32[]{:S(2)}) %collective-permute-start.18) | collective-permute-done | bytes 393248 | tf_op jit(solution)/shard_map/ppermute | solution.py:101
  79.0 2.5 %collective-permute-done.31 = bf16[2,24,2048]{2,1,0:T(8,128)(2,1)S(1)} collective-permute-done((bf16[2,24,2048]{2,1,0:T(8,128)(2,1)S(1)}, bf16[2,24,2048]{2,1,0:T(8,128)(2,1)S(1)}, u32[]{:S(2)}, u32[]{:S(2)}) %collective-permute-start.31) | collective-permute-done | bytes 196640 | tf_op jit(solution)/shard_map/ppermute | solution.py:101
  83.9 1.9 collective-permute-done.19
  90.3 1.6 copy-done.1
  95.0 1.9 %multiply_convert_fusion.3 = (bf16[192,384]{1,0:T(8,128)(2,1)}, bf16[192,384]{1,0:T(8,128)(2,1)S(1)}, bf16[192,384]{1,0:T(8,128)(2,1)S(1)}) fusion(f32[192]{0:T(256)S(1)} %copy-done.6, f32[192,384]{1,0:T(8,128)S(1)} %fusion.34, f32[192,384]{1,0:T(8,128)S(1)} %fusion.64, bf16[192,4096]{1,0:T(8,128)(2,1)S(1)} %bitcast.255, bf16[1,384,4096]{2,1,0:T(8,128)(2,1)S(1)} %copy-done), kind=kOutput, calls=%fused_computation.137 | convolution fusion | flops 605159424 | bytes 5751552 | tf_op jit(solution)/shard_map/rd,fd->rf/dot_general | solution.py:151
  107.2 2.0 %multiply_convert_fusion.2 = (bf16[192,384]{1,0:T(8,128)(2,1)}, bf16[192,384]{1,0:T(8,128)(2,1)S(1)}, bf16[192,384]{1,0:T(8,128)(2,1)S(1)}) fusion(f32[192]{0:T(256)S(1)} %mul.157, f32[192,384]{1,0:T(8,128)S(1)} %fusion.30, f32[192,384]{1,0:T(8,128)S(1)} %fusion.67, bf16[192,4096]{1,0:T(8,128)(2,1)S(1)} %bitcast.263, bf16[1,384,4096]{2,1,0:T(8,128)(2,1)S(1)} %copy-done), kind=kOutput, calls=%fused_computation.136 | convolution fusion | flops 605159424 | bytes 5751552 | tf_op jit(solution)/shard_map/rd,fd->rf/dot_general | solution.py:151
  111.3 2.0 %multiply_convert_fusion.1 = (bf16[192,384]{1,0:T(8,128)(2,1)}, bf16[192,384]{1,0:T(8,128)(2,1)S(1)}, bf16[192,384]{1,0:T(8,128)(2,1)S(1)}) fusion(f32[192]{0:T(256)S(1)} %mul.166, f32[192,384]{1,0:T(8,128)S(1)} %fusion.26, f32[192,384]{1,0:T(8,128)S(1)} %fusion.70, bf16[192,4096]{1,0:T(8,128)(2,1)S(1)} %bitcast.259, bf16[1,384,4096]{2,1,0:T(8,128)(2,1)S(1)} %copy-done), kind=kOutput, calls=%fused_computation.135 | convolution fusion | flops 605159424 | bytes 5751552 | tf_op jit(solution)/shard_map/rd,fd->rf/dot_general | solution.py:151
  115.5 2.0 %multiply_convert_fusion = (bf16[192,384]{1,0:T(8,128)(2,1)}, bf16[192,384]{1,0:T(8,128)(2,1)S(1)}, bf16[192,384]{1,0:T(8,128)(2,1)}) fusion(f32[192]{0:T(256)S(1)} %mul.175, f32[192,384]{1,0:T(8,128)S(1)} %fusion.22, f32[192,384]{1,0:T(8,128)S(1)} %fusion.73, bf16[192,4096]{1,0:T(8,128)(2,1)S(1)} %bitcast.267, bf16[1,384,4096]{2,1,0:T(8,128)(2,1)S(1)} %copy-done), kind=kOutput, calls=%fused_computation.134 | convolution fusion | flops 605159424 | bytes 5751552 | tf_op jit(solution)/shard_map/rd,fd->rf/dot_general | solution.py:151
  117.5 4.0 %fusion.11 = bf16[1,384,4096]{2,1,0:T(8,128)(2,1)} fusion(bf16[192,4096]{1,0:T(8,128)(2,1)S(1)} %bitcast.268, bf16[192,4096]{1,0:T(8,128)(2,1)S(1)} %bitcast.260, bf16[192,4096]{1,0:T(8,128)(2,1)S(1)} %bitcast.264, bf16[192,4096]{1,0:T(8,128)(2,1)S(1)} %bitcast.256, bf16[192,384]{1,0:T(8,128)(2,1)S(1)} %get-tuple-element.30, ...), kind=kOutput, calls=%fused_computation.16 | convolution fusion | flops 2445017088 | bytes 10027008 | tf_op jit(solution)/shard_map/rf,rd->fd/dot_general | solution.py:178
  127.4 4.0 %fusion.12 = bf16[1,384,4096]{2,1,0:T(8,128)(2,1)} fusion(bf16[192,4096]{1,0:T(8,128)(2,1)S(1)} %bitcast.269, bf16[192,4096]{1,0:T(8,128)(2,1)S(1)} %bitcast.261, bf16[192,4096]{1,0:T(8,128)(2,1)S(1)} %bitcast.265, bf16[192,4096]{1,0:T(8,128)(2,1)S(1)} %bitcast.257, bf16[192,384]{1,0:T(8,128)(2,1)S(1)} %copy-done.3, ...), kind=kOutput, calls=%fused_computation.17 | convolution fusion | flops 2445017088 | bytes 10027008 | tf_op jit(solution)/shard_map/rf,rd->fd/dot_general | solution.py:178
  133.5 4.0 %fusion.13 = bf16[1,384,4096]{2,1,0:T(8,128)(2,1)} fusion(bf16[192,4096]{1,0:T(8,128)(2,1)S(1)} %bitcast.275, bf16[192,4096]{1,0:T(8,128)(2,1)S(1)} %bitcast.271, bf16[192,4096]{1,0:T(8,128)(2,1)S(1)} %bitcast.273, bf16[192,4096]{1,0:T(8,128)(2,1)S(1)} %bitcast.277, bf16[192,384]{1,0:T(8,128)(2,1)S(1)} %copy-done.10, bf16[192,384]{1,0:T(8,128)(2,1)S(1)} %copy-done.9, ...), kind=kOutput, calls=%fused_computation.18 | convolution fusion | flops 2445017088 | bytes 10027008 | tf_op jit(solution)/shard_map/rf,rd->fd/dot_general | solution.py:178
  138.2 1.6 collective-permute-done.14
  140.5 4.7 %collective-permute-done.12 = bf16[2,24,2048]{2,1,0:T(8,128)(2,1)S(1)} collective-permute-done((bf16[2,24,2048]{2,1,0:T(8,128)(2,1)S(1)}, bf16[2,24,2048]{2,1,0:T(8,128)(2,1)S(1)}, u32[]{:S(2)}, u32[]{:S(2)}) %collective-permute-start.12) | collective-permute-done | bytes 196640 | tf_op jit(solution)/shard_map/ppermute | solution.py:101
  145.3 1.6 collective-permute-start.13
  153.2 3.0 %collective-permute-done.25 = bf16[2,24,2048]{2,1,0:T(8,128)(2,1)S(1)} collective-permute-done((bf16[2,24,2048]{2,1,0:T(8,128)(2,1)S(1)}, bf16[2,24,2048]{2,1,0:T(8,128)(2,1)S(1)}, u32[]{:S(2)}, u32[]{:S(2)}) %collective-permute-start.25) | collective-permute-done | bytes 196640 | tf_op jit(solution)/shard_map/ppermute | solution.py:101
  158.4 2.0 %collective-permute-done.37 = bf16[2,24,2048]{2,1,0:T(8,128)(2,1)S(1)} collective-permute-done((bf16[2,24,2048]{2,1,0:T(8,128)(2,1)S(1)}, bf16[2,24,2048]{2,1,0:T(8,128)(2,1)S(1)}, u32[]{:S(2)}, u32[]{:S(2)}) %collective-permute-start.37) | collective-permute-done | bytes 196640 | tf_op jit(solution)/shard_map/ppermute | solution.py:101
  164.3 1.5 collective-permute-done.47
  166.0 1.6 collective-permute-done.26
  169.0 6.6 %collective-permute-start.27 = (bf16[24,4096]{1,0:T(8,128)(2,1)S(1)}, bf16[24,4096]{1,0:T(8,128)(2,1)S(1)}, u32[]{:S(2)}, u32[]{:S(2)}) collective-permute-start(bf16[24,4096]{1,0:T(8,128)(2,1)S(1)} %pad_maximum_fusion.12), channel_id=1, source_target_pairs={{0,4},{1,5},{2,6},{3,7},{4,0},{5,1},{6,2},{7,3},{8,12},{9,13},{10,... | collective-permute-start | bytes 589832 | tf_op jit(solution)/shard_map/ppermute | solution.py:101
  175.7 2.8 %collective-permute-start.39 = (bf16[24,4096]{1,0:T(8,128)(2,1)S(1)}, bf16[24,4096]{1,0:T(8,128)(2,1)S(1)}, u32[]{:S(2)}, u32[]{:S(2)}) collective-permute-start(bf16[24,4096]{1,0:T(8,128)(2,1)S(1)} %pad_maximum_fusion.13), channel_id=1, source_target_pairs={{0,8},{1,9},{2,10},{3,11},{4,12},{5,13},{6,14},{7,15},{8,0},{9,1},... | collective-permute-start | bytes 589832 | tf_op jit(solution)/shard_map/ppermute | solution.py:101
  180.2 9.8 %collective-permute-done.39 = bf16[24,4096]{1,0:T(8,128)(2,1)S(1)} collective-permute-done((bf16[24,4096]{1,0:T(8,128)(2,1)S(1)}, bf16[24,4096]{1,0:T(8,128)(2,1)S(1)}, u32[]{:S(2)}, u32[]{:S(2)}) %collective-permute-start.39) | collective-permute-done | bytes 196640 | tf_op jit(solution)/shard_map/ppermute | solution.py:101
  (203 shorter events, 75.9 us)
Async XLA Ops:
  7.5 23.8 %collective-permute-start.7 = (bf16[2,24,4096]{2,1,0:T(8,128)(2,1)}, bf16[2,24,4096]{2,1,0:T(8,128)(2,1)}, u32[]{:S(2)}, u32[]{:S(2)}) collective-permute-start(bf16[2,24,4096]{2,1,0:T(8,128)(2,1)} %get-tuple-element.33), channel_id=1, source_target_pairs={{0,16},{16,0},{1,17},{17,1},{2,18},{18,2},{3,19},{19,3},{4,20},{20... | collective-permute-start | bytes 1179656 | tf_op jit(solution)/shard_map/ppermute | solution.py:101
  9.0 24.4 %collective-permute-start.6 = (bf16[2,24,4096]{2,1,0:T(8,128)(2,1)}, bf16[2,24,4096]{2,1,0:T(8,128)(2,1)}, u32[]{:S(2)}, u32[]{:S(2)}) collective-permute-start(bf16[2,24,4096]{2,1,0:T(8,128)(2,1)} %get-tuple-element.33), channel_id=1, source_target_pairs={{0,2},{1,3},{2,0},{3,1},{4,6},{5,7},{6,4},{7,5},{8,10},{9,11},{10,... | collective-permute-start | bytes 1179656 | tf_op jit(solution)/shard_map/ppermute | solution.py:101
  24.7 29.1 %collective-permute-start.28 = (bf16[2,24,4096]{2,1,0:T(8,128)(2,1)}, bf16[2,24,4096]{2,1,0:T(8,128)(2,1)}, u32[]{:S(2)}, u32[]{:S(2)}) collective-permute-start(bf16[2,24,4096]{2,1,0:T(8,128)(2,1)} %get-tuple-element.33), channel_id=1, source_target_pairs={{0,8},{1,9},{2,10},{3,11},{4,12},{5,13},{6,14},{7,15},{8,0},{9,1},... | collective-permute-start | bytes 1179656 | tf_op jit(solution)/shard_map/ppermute | solution.py:101
  27.5 27.9 %collective-permute-start.16 = (bf16[2,24,4096]{2,1,0:T(8,128)(2,1)}, bf16[2,24,4096]{2,1,0:T(8,128)(2,1)}, u32[]{:S(2)}, u32[]{:S(2)}) collective-permute-start(bf16[2,24,4096]{2,1,0:T(8,128)(2,1)} %get-tuple-element.33), channel_id=1, source_target_pairs={{0,4},{1,5},{2,6},{3,7},{4,0},{5,1},{6,2},{7,3},{8,12},{9,13},{10,... | collective-permute-start | bytes 1179656 | tf_op jit(solution)/shard_map/ppermute | solution.py:101
  30.2 25.7 %collective-permute-start.40 = (bf16[2,24,4096]{2,1,0:T(8,128)(2,1)}, bf16[2,24,4096]{2,1,0:T(8,128)(2,1)}, u32[]{:S(2)}, u32[]{:S(2)}) collective-permute-start(bf16[2,24,4096]{2,1,0:T(8,128)(2,1)} %get-tuple-element.33), channel_id=1, source_target_pairs={{0,12},{1,13},{2,14},{3,15},{4,8},{5,9},{6,10},{7,11},{8,4},{9,5},... | collective-permute-start | bytes 1179656 | tf_op jit(solution)/shard_map/ppermute | solution.py:101
  32.9 23.5 %collective-permute-start.8 = (bf16[2,24,2048]{2,1,0:T(8,128)(2,1)}, bf16[2,24,2048]{2,1,0:T(8,128)(2,1)}, u32[]{:S(2)}, u32[]{:S(2)}) collective-permute-start(bf16[2,24,2048]{2,1,0:T(8,128)(2,1)} %slice.281), channel_id=1, source_target_pairs={{0,2},{1,3},{2,0},{3,1},{4,6},{5,7},{6,4},{7,5},{8,10},{9,11},{10,... | collective-permute-start | bytes 589832 | tf_op jit(solution)/shard_map/ppermute | solution.py:101
  35.1 22.9 %collective-permute-start.9 = (bf16[2,24,2048]{2,1,0:T(8,128)(2,1)}, bf16[2,24,2048]{2,1,0:T(8,128)(2,1)}, u32[]{:S(2)}, u32[]{:S(2)}) collective-permute-start(bf16[2,24,2048]{2,1,0:T(8,128)(2,1)} %slice.282), channel_id=1, source_target_pairs={{0,16},{16,0},{1,17},{17,1},{2,18},{18,2},{3,19},{19,3},{4,20},{20... | collective-permute-start | bytes 589832 | tf_op jit(solution)/shard_map/ppermute | solution.py:101
  53.9 12.3 %collective-permute-start.30 = (bf16[2,24,4096]{2,1,0:T(8,128)(2,1)}, bf16[2,24,4096]{2,1,0:T(8,128)(2,1)S(1)}, u32[]{:S(2)}, u32[]{:S(2)}) collective-permute-start(bf16[2,24,4096]{2,1,0:T(8,128)(2,1)} %collective-permute-done.28), channel_id=1, source_target_pairs={{0,16},{16,0},{1,17},{17,1},{2,18},{18,2},{3,19},{19,3},{4,20},{20... | collective-permute-start | bytes 1179656 | tf_op jit(solution)/shard_map/ppermute | solution.py:101
  55.4 12.3 %collective-permute-start.29 = (bf16[2,24,4096]{2,1,0:T(8,128)(2,1)}, bf16[2,24,4096]{2,1,0:T(8,128)(2,1)S(1)}, u32[]{:S(2)}, u32[]{:S(2)}) collective-permute-start(bf16[2,24,4096]{2,1,0:T(8,128)(2,1)} %collective-permute-done.28), channel_id=1, source_target_pairs={{0,2},{1,3},{2,0},{3,1},{4,6},{5,7},{6,4},{7,5},{8,10},{9,11},{10,... | collective-permute-start | bytes 1179656 | tf_op jit(solution)/shard_map/ppermute | solution.py:101
  55.9 16.7 %collective-permute-start.18 = (bf16[2,24,4096]{2,1,0:T(8,128)(2,1)}, bf16[2,24,4096]{2,1,0:T(8,128)(2,1)S(1)}, u32[]{:S(2)}, u32[]{:S(2)}) collective-permute-start(bf16[2,24,4096]{2,1,0:T(8,128)(2,1)} %collective-permute-done.16), channel_id=1, source_target_pairs={{0,16},{16,0},{1,17},{17,1},{2,18},{18,2},{3,19},{19,3},{4,20},{20... | collective-permute-start | bytes 1179656 | tf_op jit(solution)/shard_map/ppermute | solution.py:101
  56.4 19.1 %collective-permute-start.17 = (bf16[2,24,4096]{2,1,0:T(8,128)(2,1)}, bf16[2,24,4096]{2,1,0:T(8,128)(2,1)S(1)}, u32[]{:S(2)}, u32[]{:S(2)}) collective-permute-start(bf16[2,24,4096]{2,1,0:T(8,128)(2,1)} %collective-permute-done.16), channel_id=1, source_target_pairs={{0,2},{1,3},{2,0},{3,1},{4,6},{5,7},{6,4},{7,5},{8,10},{9,11},{10,... | collective-permute-start | bytes 1179656 | tf_op jit(solution)/shard_map/ppermute | solution.py:101
  57.9 18.9 %collective-permute-start.42 = (bf16[2,24,4096]{2,1,0:T(8,128)(2,1)}, bf16[2,24,4096]{2,1,0:T(8,128)(2,1)S(1)}, u32[]{:S(2)}, u32[]{:S(2)}) collective-permute-start(bf16[2,24,4096]{2,1,0:T(8,128)(2,1)} %collective-permute-done.40), channel_id=1, source_target_pairs={{0,16},{16,0},{1,17},{17,1},{2,18},{18,2},{3,19},{19,3},{4,20},{20... | collective-permute-start | bytes 1179656 | tf_op jit(solution)/shard_map/ppermute | solution.py:101
  66.1 12.0 %collective-permute-start.41 = (bf16[2,24,4096]{2,1,0:T(8,128)(2,1)}, bf16[2,24,4096]{2,1,0:T(8,128)(2,1)S(1)}, u32[]{:S(2)}, u32[]{:S(2)}) collective-permute-start(bf16[2,24,4096]{2,1,0:T(8,128)(2,1)} %collective-permute-done.40), channel_id=1, source_target_pairs={{0,2},{1,3},{2,0},{3,1},{4,6},{5,7},{6,4},{7,5},{8,10},{9,11},{10,... | collective-permute-start | bytes 1179656 | tf_op jit(solution)/shard_map/ppermute | solution.py:101
  67.7 13.9 %collective-permute-start.31 = (bf16[2,24,2048]{2,1,0:T(8,128)(2,1)S(1)}, bf16[2,24,2048]{2,1,0:T(8,128)(2,1)S(1)}, u32[]{:S(2)}, u32[]{:S(2)}) collective-permute-start(bf16[2,24,2048]{2,1,0:T(8,128)(2,1)S(1)} %slice.309), channel_id=1, source_target_pairs={{0,2},{1,3},{2,0},{3,1},{4,6},{5,7},{6,4},{7,5},{8,10},{9,11},{10,... | collective-permute-start | bytes 589832 | tf_op jit(solution)/shard_map/ppermute | solution.py:101
  72.7 9.4 %collective-permute-start.32 = (bf16[2,24,2048]{2,1,0:T(8,128)(2,1)S(1)}, bf16[2,24,2048]{2,1,0:T(8,128)(2,1)S(1)}, u32[]{:S(2)}, u32[]{:S(2)}) collective-permute-start(bf16[2,24,2048]{2,1,0:T(8,128)(2,1)S(1)} %slice.310), channel_id=1, source_target_pairs={{0,16},{16,0},{1,17},{17,1},{2,18},{18,2},{3,19},{19,3},{4,20},{20... | collective-permute-start | bytes 589832 | tf_op jit(solution)/shard_map/ppermute | solution.py:101
  75.6 14.4 %collective-permute-start.10 = (bf16[2,4,24,4096]{3,2,1,0:T(8,128)(2,1)S(1)}, bf16[2,4,24,4096]{3,2,1,0:T(8,128)(2,1)S(1)}, u32[]{:S(2)}, u32[]{:S(2)}) collective-permute-start(bf16[2,4,24,4096]{3,2,1,0:T(8,128)(2,1)S(1)} %get-tuple-element.13), channel_id=1, source_target_pairs={{0,1},{1,0},{2,3},{3,2},{4,5},{5,4},{6,7},{7,6},{8,9},{9,8},{10,11... | collective-permute-start | bytes 4718600 | tf_op jit(solution)/shard_map/ppermute | solution.py:101
  85.8 14.7 %collective-permute-start.33 = (bf16[2,4,24,4096]{3,2,0,1:T(8,128)(2,1)S(1)}, bf16[2,4,24,4096]{3,2,0,1:T(8,128)(2,1)S(1)}, u32[]{:S(2)}, u32[]{:S(2)}) collective-permute-start(bf16[2,4,24,4096]{3,2,0,1:T(8,128)(2,1)S(1)} %get-tuple-element.17), channel_id=1, source_target_pairs={{0,1},{1,0},{2,3},{3,2},{4,5},{5,4},{6,7},{7,6},{8,9},{9,8},{10,11... | collective-permute-start | bytes 4718600 | tf_op jit(solution)/shard_map/ppermute | solution.py:101
  87.1 14.0 %collective-permute-start.21 = (bf16[2,4,24,4096]{3,2,0,1:T(8,128)(2,1)S(1)}, bf16[2,4,24,4096]{3,2,0,1:T(8,128)(2,1)S(1)}, u32[]{:S(2)}, u32[]{:S(2)}) collective-permute-start(bf16[2,4,24,4096]{3,2,0,1:T(8,128)(2,1)S(1)} %get-tuple-element.15), channel_id=1, source_target_pairs={{0,1},{1,0},{2,3},{3,2},{4,5},{5,4},{6,7},{7,6},{8,9},{9,8},{10,11... | collective-permute-start | bytes 4718600 | tf_op jit(solution)/shard_map/ppermute | solution.py:101
  90.0 14.1 %collective-permute-start.45 = (bf16[2,4,24,4096]{3,2,0,1:T(8,128)(2,1)S(1)}, bf16[2,4,24,4096]{3,2,0,1:T(8,128)(2,1)S(1)}, u32[]{:S(2)}, u32[]{:S(2)}) collective-permute-start(bf16[2,4,24,4096]{3,2,0,1:T(8,128)(2,1)S(1)} %get-tuple-element.19), channel_id=1, source_target_pairs={{0,1},{1,0},{2,3},{3,2},{4,5},{5,4},{6,7},{7,6},{8,9},{9,8},{10,11... | collective-permute-start | bytes 4718600 | tf_op jit(solution)/shard_map/ppermute | solution.py:101
  100.0 31.4 %collective-permute-start.11 = (bf16[4,24,4096]{2,1,0:T(8,128)(2,1)}, bf16[4,24,4096]{2,1,0:T(8,128)(2,1)}, u32[]{:S(2)}, u32[]{:S(2)}) collective-permute-start(bf16[4,24,4096]{2,1,0:T(8,128)(2,1)} %slice_bitcast_fusion.6), channel_id=1, source_target_pairs={{0,1},{1,0},{2,3},{3,2},{4,5},{5,4},{6,7},{7,6},{8,9},{9,8},{10,11... | collective-permute-start | bytes 2359304 | tf_op jit(solution)/shard_map/ppermute | solution.py:101
  123.6 23.3 %collective-permute-start.22 = (bf16[4,24,4096]{2,1,0:T(8,128)(2,1)S(1)}, bf16[4,24,4096]{2,1,0:T(8,128)(2,1)}, u32[]{:S(2)}, u32[]{:S(2)}) collective-permute-start(bf16[4,24,4096]{2,1,0:T(8,128)(2,1)S(1)} %slice_bitcast_fusion.4), channel_id=1, source_target_pairs={{0,1},{1,0},{2,3},{3,2},{4,5},{5,4},{6,7},{7,6},{8,9},{9,8},{10,11... | collective-permute-start | bytes 2359304 | tf_op jit(solution)/shard_map/ppermute | solution.py:101
  124.8 24.4 %collective-permute-start.34 = (bf16[4,24,4096]{2,1,0:T(8,128)(2,1)S(1)}, bf16[4,24,4096]{2,1,0:T(8,128)(2,1)S(1)}, u32[]{:S(2)}, u32[]{:S(2)}) collective-permute-start(bf16[4,24,4096]{2,1,0:T(8,128)(2,1)S(1)} %slice_bitcast_fusion.2), channel_id=1, source_target_pairs={{0,1},{1,0},{2,3},{3,2},{4,5},{5,4},{6,7},{7,6},{8,9},{9,8},{10,11... | collective-permute-start | bytes 2359304 | tf_op jit(solution)/shard_map/ppermute | solution.py:101
  126.8 22.6 %collective-permute-start.46 = (bf16[4,24,4096]{2,1,0:T(8,128)(2,1)S(1)}, bf16[4,24,4096]{2,1,0:T(8,128)(2,1)S(1)}, u32[]{:S(2)}, u32[]{:S(2)}) collective-permute-start(bf16[4,24,4096]{2,1,0:T(8,128)(2,1)S(1)} %slice_bitcast_fusion), channel_id=1, source_target_pairs={{0,1},{1,0},{2,3},{3,2},{4,5},{5,4},{6,7},{7,6},{8,9},{9,8},{10,11... | collective-permute-start | bytes 2359304 | tf_op jit(solution)/shard_map/ppermute | solution.py:101
  145.3 33.8 %collective-permute-start.13 = (bf16[24,2048]{1,0:T(8,128)(2,1)S(1)}, bf16[24,2048]{1,0:T(8,128)(2,1)S(1)}, u32[]{:S(2)}, u32[]{:S(2)}) collective-permute-start(bf16[24,2048]{1,0:T(8,128)(2,1)S(1)} %slice_bitcast_fusion.22), channel_id=1, source_target_pairs={{0,16},{16,0},{1,17},{17,1},{2,18},{18,2},{3,19},{19,3},{4,20},{20... | collective-permute-start | bytes 294920 | tf_op jit(solution)/shard_map/ppermute | solution.py:101
  150.5 9.9 %collective-permute-start.37 = (bf16[2,24,2048]{2,1,0:T(8,128)(2,1)S(1)}, bf16[2,24,2048]{2,1,0:T(8,128)(2,1)S(1)}, u32[]{:S(2)}, u32[]{:S(2)}) collective-permute-start(bf16[2,24,2048]{2,1,0:T(8,128)(2,1)S(1)} %slice.319), channel_id=1, source_target_pairs={{0,16},{16,0},{1,17},{17,1},{2,18},{18,2},{3,19},{19,3},{4,20},{20... | collective-permute-start | bytes 589832 | tf_op jit(solution)/shard_map/ppermute | solution.py:101
  151.7 10.3 %collective-permute-start.35 = (bf16[2,24,2048]{2,1,0:T(8,128)(2,1)S(1)}, bf16[2,24,2048]{2,1,0:T(8,128)(2,1)S(1)}, u32[]{:S(2)}, u32[]{:S(2)}) collective-permute-start(bf16[2,24,2048]{2,1,0:T(8,128)(2,1)S(1)} %slice.257), channel_id=1, source_target_pairs={{0,2},{1,3},{2,0},{3,1},{4,6},{5,7},{6,4},{7,5},{8,10},{9,11},{10,... | collective-permute-start | bytes 589832 | tf_op jit(solution)/shard_map/ppermute | solution.py:101
  165.9 9.8 %collective-permute-start.36 = (bf16[24,2048]{1,0:T(8,128)(2,1)S(1)}, bf16[24,2048]{1,0:T(8,128)(2,1)S(1)}, u32[]{:S(2)}, u32[]{:S(2)}) collective-permute-start(bf16[24,2048]{1,0:T(8,128)(2,1)S(1)} %slice_bitcast_fusion.14), channel_id=1, source_target_pairs={{0,16},{16,0},{1,17},{17,1},{2,18},{18,2},{3,19},{19,3},{4,20},{20... | collective-permute-start | bytes 294920 | tf_op jit(solution)/shard_map/ppermute | solution.py:101
  167.6 10.8 %collective-permute-start.50 = (bf16[24,2048]{1,0:T(8,128)(2,1)S(1)}, bf16[24,2048]{1,0:T(8,128)(2,1)S(1)}, u32[]{:S(2)}, u32[]{:S(2)}) collective-permute-start(bf16[24,2048]{1,0:T(8,128)(2,1)S(1)} %slice_bitcast_fusion.8), channel_id=1, source_target_pairs={{0,2},{1,3},{2,0},{3,1},{4,6},{5,7},{6,4},{7,5},{8,10},{9,11},{10,... | collective-permute-start | bytes 294920 | tf_op jit(solution)/shard_map/ppermute | solution.py:101
  167.8 10.7 %collective-permute-start.48 = (bf16[24,2048]{1,0:T(8,128)(2,1)S(1)}, bf16[24,2048]{1,0:T(8,128)(2,1)S(1)}, u32[]{:S(2)}, u32[]{:S(2)}) collective-permute-start(bf16[24,2048]{1,0:T(8,128)(2,1)S(1)} %slice_bitcast_fusion.10), channel_id=1, source_target_pairs={{0,16},{16,0},{1,17},{17,1},{2,18},{18,2},{3,19},{19,3},{4,20},{20... | collective-permute-start | bytes 294920 | tf_op jit(solution)/shard_map/ppermute | solution.py:101
  169.0 11.2 %collective-permute-start.27 = (bf16[24,4096]{1,0:T(8,128)(2,1)S(1)}, bf16[24,4096]{1,0:T(8,128)(2,1)S(1)}, u32[]{:S(2)}, u32[]{:S(2)}) collective-permute-start(bf16[24,4096]{1,0:T(8,128)(2,1)S(1)} %pad_maximum_fusion.12), channel_id=1, source_target_pairs={{0,4},{1,5},{2,6},{3,7},{4,0},{5,1},{6,2},{7,3},{8,12},{9,13},{10,... | collective-permute-start | bytes 589832 | tf_op jit(solution)/shard_map/ppermute | solution.py:101
  175.7 14.3 %collective-permute-start.39 = (bf16[24,4096]{1,0:T(8,128)(2,1)S(1)}, bf16[24,4096]{1,0:T(8,128)(2,1)S(1)}, u32[]{:S(2)}, u32[]{:S(2)}) collective-permute-start(bf16[24,4096]{1,0:T(8,128)(2,1)S(1)} %pad_maximum_fusion.13), channel_id=1, source_target_pairs={{0,8},{1,9},{2,10},{3,11},{4,12},{5,13},{6,14},{7,15},{8,0},{9,1},... | collective-permute-start | bytes 589832 | tf_op jit(solution)/shard_map/ppermute | solution.py:101
  178.6 11.4 %collective-permute-start.51 = (bf16[24,4096]{1,0:T(8,128)(2,1)S(1)}, bf16[24,4096]{1,0:T(8,128)(2,1)S(1)}, u32[]{:S(2)}, u32[]{:S(2)}) collective-permute-start(bf16[24,4096]{1,0:T(8,128)(2,1)S(1)} %pad_maximum_fusion.14), channel_id=1, source_target_pairs={{0,12},{1,13},{2,14},{3,15},{4,8},{5,9},{6,10},{7,11},{8,4},{9,5},... | collective-permute-start | bytes 589832 | tf_op jit(solution)/shard_map/ppermute | solution.py:101
  (31 other events, 248.0 us)

commit v2 on v0

--- a/solution.py
+++ b/solution.py
@@ -26,7 +26,7 @@
     return jnp.sum(spread, axis=1).reshape(-1, experts, capacity)
 
 
-def per_device(tokens, out_grad, routes, gates, w_gate, w_up, w_down):
+def slot_plan(tokens, out_grad, routes, gates, w_gate, w_up, w_down):
     tok_rows, features = tokens.shape
     top_count = routes.shape[1]
     experts = lax.axis_size("expert")
@@ -96,6 +96,170 @@
     return (summed.astype(jnp.bfloat16), grad_gate[None], grad_up[None], grad_down[None])
 
 
+def swapped(x, axis, bits):
+    count = lax.axis_size(axis)
+    return lax.ppermute(x, axis, [(i, i ^ bits) for i in range(count)])
+
+
+over_core = partial(swapped, axis="expert", bits=1)
+over_x = partial(swapped, axis="expert", bits=2)
+over_z = partial(swapped, axis="expert", bits=4)
+over_far_z = partial(swapped, axis="expert", bits=8)
+over_y = partial(swapped, axis="dp", bits=1)
+together = lax.optimization_barrier
+LANES = 128
+
+
+def gate_of_expert(routes, gates, experts):
+    hit = routes[:, :, None] == jnp.arange(experts, dtype=jnp.int32)
+    return jnp.sum(jnp.where(hit, gates[:, :, None], 0), axis=1).astype(jnp.bfloat16)
+
+
+def summed(*terms):
+    total = terms[0].astype(jnp.float32)
+    for term in terms[1:]:
+        total = total + term.astype(jnp.float32)
+    return total.astype(jnp.bfloat16)
+
+
+def rows_of(*pieces):
+    return jnp.concatenate(pieces, axis=0)
+
+
+def first_sends(part):
+    half = part.shape[-1] // 2
+    return part[..., :half], part[..., half:]
+
+
+def dense_plan(tokens, out_grad, routes, gates, w_gate, w_up, w_down):
+    rows, features = tokens.shape
+    experts = lax.axis_size("expert")
+    half = features // 2
+    gate_w, up_w, down_w = w_gate[0], w_up[0], w_down[0]
+    own = jnp.arange(LANES, dtype=jnp.int32) == lax.axis_index("expert")
+
+    def expert_rows(near, far, near_other, far_other):
+        x_rows = rows_of(near[0], far[0], near_other[0], far_other[0])[:, :features]
+        g_rows = rows_of(near[1], far[1], near_other[1], far_other[1])
+        scale = g_rows[:, features:].astype(jnp.float32)
+        scale = jnp.sum(jnp.where(own, scale, 0.0), axis=-1, keepdims=True)
+        g_rows = g_rows[:, :features]
+        gate_pre = jnp.einsum("rd,fd->rf", x_rows, gate_w, preferred_element_type=jnp.float32)
+        up_pre = jnp.einsum("rd,fd->rf", x_rows, up_w, preferred_element_type=jnp.float32)
+        d_hidden = scale * jnp.einsum("rd,fd->rf", g_rows, down_w, preferred_element_type=jnp.float32)
+        sigmoid_gate = jax.nn.sigmoid(gate_pre)
+        silu_gate = gate_pre * sigmoid_gate
+        hidden = (scale * silu_gate * up_pre).astype(jnp.bfloat16)
+        d_up_act = (d_hidden * silu_gate).astype(jnp.bfloat16)
+        d_gate_act = (
+            d_hidden * up_pre * sigmoid_gate * (1.0 + gate_pre * (1.0 - sigmoid_gate))
+        ).astype(jnp.bfloat16)
+        part = jnp.einsum("rf,fd->rd", d_gate_act, gate_w, preferred_element_type=jnp.float32)
+        part = part + jnp.einsum("rf,fd->rd", d_up_act, up_w, preferred_element_type=jnp.float32)
+        part = part.astype(jnp.bfloat16).reshape(2, 8, rows, features)
+        return part, (x_rows, g_rows, hidden, d_gate_act, d_up_act)
+
+    def near_of(mine, from_x, from_y, from_z):
+        return jnp.concatenate([mine, from_x, from_y, from_z], axis=1)
+
+    def far_of(second_x, second_y, second_z, third_x, third_y):
+        return jnp.stack(
+            [
+                rows_of(second_y[0], second_y[1], second_z[0], third_y),
+                rows_of(second_x[0], second_z[1], second_x[1], third_x),
+            ]
+        )
+
+    def firsts(mine):
+        return over_x(mine), over_y(mine), over_z(mine)
+
+    def seconds(from_x, from_y, from_z):
+        return (
+            over_x(jnp.stack([from_y[1], from_z[1]])),
+            over_y(jnp.stack([from_x[0], from_z[0]])),
+            over_z(jnp.stack([from_x[0], from_y[1]])),
+        )
+
+    def thirds(second_z):
+        return over_x(second_z[1]), over_y(second_z[0])
+
+    scales = gate_of_expert(routes, gates, experts)
+    scales = jnp.pad(scales, ((0, 0), (0, LANES - experts)))
+    mine = jnp.stack([jnp.pad(tokens, ((0, 0), (0, LANES))), jnp.concatenate([out_grad, scales], axis=1)])
+    first = firsts(mine)
+    distant = over_far_z(mine)
+    first = together(first)
+    second = seconds(*first)
+    near = near_of(mine, *first)
+    near_other = over_core(near)
+    second, near_other, distant = together((second, near_other, distant))
+    first2 = firsts(distant)
+    third = thirds(second[2])
+    first2, third = together((first2, third))
+    second2 = seconds(*first2)
+    far = far_of(*second, *third)
+    far_other = over_core(far)
+    near2 = near_of(distant, *first2)
+    near2_other = over_core(near2)
+    part, kept = expert_rows(near, far, near_other, far_other)
+    second2, near2_other, part = together((second2, near2_other, part))
+    third2 = thirds(second2[2])
+    part_other = over_core(part[1])
+    third2, part_other = together((third2, part_other))
+    far2 = far_of(*second2, *third2)
+    far2_other = over_core(far2)
+
+    def lane_sums(part, part_other):
+        own, x, y, z, xy, yz, xz, xyz = (summed(part[i], part_other[i]) for i in range(8))
+        opening = over_x(xyz[:, half:]), over_y(xyz[:, :half])
+        middle = over_x(jnp.stack([xy[:, half:], xz[:, half:]])), over_y(jnp.stack([xy[:, :half], yz[:, :half]]))
+        return (own, x, y, z, yz[:, half:], xz[:, :half]), opening, middle
+
+    def sent_z(sums, opening):
+        return over_z(jnp.concatenate([summed(sums[5], opening[1]), summed(sums[4], opening[0])], axis=1))
+
+    def last_sends(sums, middle, from_z):
+        _, x, y, z, _, _ = sums
+        from_x, from_y = middle
+        x = jnp.concatenate([summed(x[:, :half], from_y[0], from_z[:, :half]), x[:, half:]], axis=1)
+        y = jnp.concatenate([y[:, :half], summed(y[:, half:], from_x[0], from_z[:, half:])], axis=1)
+        z = jnp.concatenate([summed(z[:, :half], from_y[1]), summed(z[:, half:], from_x[1])], axis=1)
+        return over_x(x), over_y(y), over_z(z)
+
+    sums, opening, middle = lane_sums(part[0], part_other)
+    opening, far2_other = together((opening, far2_other))
+    from_z = sent_z(sums, opening)
+    part2, kept2 = expert_rows(near2, far2, near2_other, far2_other)
+    middle, from_z, part2 = together((middle, from_z, part2))
+    part2_other = over_core(part2[1])
+    last = last_sends(sums, middle, from_z)
+    last, part2_other = together((last, part2_other))
+    near_total = summed(sums[0], *last)
+    sums2, opening2, middle2 = lane_sums(part2[0], part2_other)
+    from_z2 = sent_z(sums2, opening2)
+    last2 = last_sends(sums2, middle2, from_z2)
+    d_tokens = summed(near_total, over_far_z(summed(sums2[0], *last2)))
+
+    def weight_grad(at, side):
+        return jnp.einsum(
+            "rf,rd->fd",
+            rows_of(kept[at], kept2[at]),
+            rows_of(kept[side], kept2[side]),
+            preferred_element_type=jnp.float32,
+        ).astype(jnp.bfloat16)[None]
+
+    return d_tokens, weight_grad(3, 0), weight_grad(4, 0), weight_grad(2, 1)
+
+
+def per_device(tokens, out_grad, routes, gates, w_gate, w_up, w_down):
+    tok_rows, top_count = routes.shape
+    experts = lax.axis_size("expert")
+    capacity = max(2, min(tok_rows, 3 * tok_rows * top_count // (2 * experts)))
+    crowded = 2 * capacity >= tok_rows and lax.axis_size("dp") == 2 and experts == 16
+    plan = dense_plan if crowded else slot_plan
+    return plan(tokens, out_grad, routes, gates, w_gate, w_up, w_down)
+
+
 def solution(mesh):
     in_specs = (
         P(("dp", "expert"), None),

time: 448 us -> 152 us (0.34)
  the two profiles are of different devices: /device:TPU:11 before, /device:TPU:0 now
where the time goes in v2:
time: 152 us
  waiting for transfers between devices  53.9 us (35%)
  starting transfers between devices  43.4 us (29%)
  matrix products  32 us (21%)
  other arithmetic  12.7 us (8%)
  local copies, waits for them, and re-layouts  8.55 us (6%)
    ppermute x40, waiting for transfers between devices, swapped(): return lax.ppermute(x, axis, [(i, i ^ bits) for i in range(count)])  53.9 us
    ppermute x40, starting transfers between devices, swapped(): return lax.ppermute(x, axis, [(i, i ^ bits) for i in range(count)])  43.4 us
    dot_general x3, matrix products, weight_grad(): jnp.einsum('rf,rd->fd', rows_of(kept[at], kept2[at]), rows_of(kept[side],...  12.1 us
    dot_general x2, matrix products, expert_rows(): jnp.einsum('rd,fd->rf', x_rows, up_w, preferred_element_type=jnp.float32)  5.39 us
    convert_element_type x10, other arithmetic, summed(): return total.astype(jnp.bfloat16)  5 us
    dot_general x2, matrix products, expert_rows(): jnp.einsum('rf,fd->rd', d_up_act, up_w, preferred_element_type=jnp.float32)  3.73 us
    dot_general x2, matrix products, expert_rows(): jnp.einsum('rd,fd->rf', g_rows, down_w, preferred_element_type=jnp.float32)  3.62 us
    dot_general x2, matrix products, expert_rows(): jnp.einsum('rf,fd->rd', d_gate_act, gate_w, preferred_element_type=jnp.fl...  3.6 us
  transfers between devices with their start and end apart: 40, of which 18 were waited for; matrix products, arithmetic and copies ran while one was open for 30% of the time, Pallas kernels for 0%

profile of v2, /device:TPU:0, one launch (start us, length us, event | category | flops | bytes accessed | tf_op | source)
XLA Modules:
  0.0 151.9 jit_solution(9905181008986367846)
XLA Ops:
  4.1 3.0 %collective-permute-start.2 = (bf16[2,24,4224]{2,1,0:T(8,128)(2,1)}, bf16[2,24,4224]{2,1,0:T(8,128)(2,1)}, u32[]{:S(2)}, u32[]{:S(2)}) collective-permute-start(bf16[2,24,4224]{2,1,0:T(8,128)(2,1)} %pad_maximum_fusion.10), channel_id=1, source_target_pairs={{0,4},{1,5},{2,6},{3,7},{4,0},{5,1},{6,2},{7,3},{8,12},{9,13},{10,... | collective-permute-start | bytes 1216520 | tf_op jit(solution)/shard_map/ppermute | solution.py:101
  10.1 2.6 %collective-permute-start.7 = (bf16[2,24,4224]{2,1,0:T(8,128)(2,1)}, bf16[2,24,4224]{2,1,0:T(8,128)(2,1)}, u32[]{:S(2)}, u32[]{:S(2)}) collective-permute-start(bf16[2,24,4224]{2,1,0:T(8,128)(2,1)} %pad_maximum_fusion.10), channel_id=1, source_target_pairs={{0,8},{1,9},{2,10},{3,11},{4,12},{5,13},{6,14},{7,15},{8,0},{9,1},... | collective-permute-start | bytes 1216520 | tf_op jit(solution)/shard_map/ppermute | solution.py:101
  12.7 10.2 %collective-permute-done.2 = bf16[2,24,4224]{2,1,0:T(8,128)(2,1)} collective-permute-done((bf16[2,24,4224]{2,1,0:T(8,128)(2,1)}, bf16[2,24,4224]{2,1,0:T(8,128)(2,1)}, u32[]{:S(2)}, u32[]{:S(2)}) %collective-permute-start.2) | collective-permute-done | bytes 405536 | tf_op jit(solution)/shard_map/ppermute | solution.py:101
  27.5 2.7 %collective-permute-start.3 = (bf16[2,24,4224]{2,1,0:T(8,128)(2,1)S(1)}, bf16[2,24,4224]{2,1,0:T(8,128)(2,1)S(1)}, u32[]{:S(2)}, u32[]{:S(2)}) collective-permute-start(bf16[2,24,4224]{2,1,0:T(8,128)(2,1)S(1)} %get-tuple-element.124), channel_id=1, source_target_pairs={{0,2},{1,3},{2,0},{3,1},{4,6},{5,7},{6,4},{7,5},{8,10},{9,11},{10,... | collective-permute-start | bytes 1216520 | tf_op jit(solution)/shard_map/ppermute | solution.py:101
  30.2 2.5 %collective-permute-start.4 = (bf16[2,24,4224]{2,1,0:T(8,128)(2,1)S(1)}, bf16[2,24,4224]{2,1,0:T(8,128)(2,1)S(1)}, u32[]{:S(2)}, u32[]{:S(2)}) collective-permute-start(bf16[2,24,4224]{2,1,0:T(8,128)(2,1)S(1)} %get-tuple-element.125), channel_id=1, source_target_pairs={{0,16},{16,0},{1,17},{17,1},{2,18},{18,2},{3,19},{19,3},{4,20},{20... | collective-permute-start | bytes 1216520 | tf_op jit(solution)/shard_map/ppermute | solution.py:101
  32.9 6.4 %collective-permute-done.5 = bf16[2,24,4224]{2,1,0:T(8,128)(2,1)S(1)} collective-permute-done((bf16[2,24,4224]{2,1,0:T(8,128)(2,1)S(1)}, bf16[2,24,4224]{2,1,0:T(8,128)(2,1)S(1)}, u32[]{:S(2)}, u32[]{:S(2)}) %collective-permute-start.5) | collective-permute-done | bytes 405536 | tf_op jit(solution)/shard_map/ppermute | solution.py:101
  40.2 2.3 %collective-permute-done.4 = bf16[2,24,4224]{2,1,0:T(8,128)(2,1)S(1)} collective-permute-done((bf16[2,24,4224]{2,1,0:T(8,128)(2,1)S(1)}, bf16[2,24,4224]{2,1,0:T(8,128)(2,1)S(1)}, u32[]{:S(2)}, u32[]{:S(2)}) %collective-permute-start.4) | collective-permute-done | bytes 405536 | tf_op jit(solution)/shard_map/ppermute | solution.py:101
  44.2 1.7 %collective-permute-start.9 = (bf16[2,24,4224]{2,1,0:T(8,128)(2,1)}, bf16[2,24,4224]{2,1,0:T(8,128)(2,1)S(1)}, u32[]{:S(2)}, u32[]{:S(2)}) collective-permute-start(bf16[2,24,4224]{2,1,0:T(8,128)(2,1)} %collective-permute-done.7), channel_id=1, source_target_pairs={{0,16},{16,0},{1,17},{17,1},{2,18},{18,2},{3,19},{19,3},{4,20},{20... | collective-permute-start | bytes 1216520 | tf_op jit(solution)/shard_map/ppermute | solution.py:101
  46.6 1.7 %collective-permute-start.11 = (bf16[24,4224]{1,0:T(8,128)(2,1)S(1)}, bf16[24,4224]{1,0:T(8,128)(2,1)S(1)}, u32[]{:S(2)}, u32[]{:S(2)}) collective-permute-start(bf16[24,4224]{1,0:T(8,128)(2,1)S(1)} %get-tuple-element.117), channel_id=1, source_target_pairs={{0,2},{1,3},{2,0},{3,1},{4,6},{5,7},{6,4},{7,5},{8,10},{9,11},{10,... | collective-permute-start | bytes 608264 | tf_op jit(solution)/shard_map/ppermute | solution.py:101
  49.6 9.6 %collective-permute-done.12 = bf16[24,4224]{1,0:T(8,128)(2,1)S(1)} collective-permute-done((bf16[24,4224]{1,0:T(8,128)(2,1)S(1)}, bf16[24,4224]{1,0:T(8,128)(2,1)S(1)}, u32[]{:S(2)}, u32[]{:S(2)}) %collective-permute-start.12) | collective-permute-done | bytes 202784 | tf_op jit(solution)/shard_map/ppermute | solution.py:101
  64.3 3.2 %collective-permute-done.17 = bf16[2,96,4224]{2,1,0:T(8,128)(2,1)S(1)} collective-permute-done((bf16[2,96,4224]{2,1,0:T(8,128)(2,1)S(1)}, bf16[2,96,4224]{2,1,0:T(8,128)(2,1)S(1)}, u32[]{:S(2)}, u32[]{:S(2)}) %collective-permute-start.17) | collective-permute-done | bytes 1622048 | tf_op jit(solution)/shard_map/ppermute | solution.py:101
  67.8 1.8 %fusion.30 = f32[384,384]{1,0:T(8,128)S(1)} fusion(bf16[1,384,4096]{2,1,0:T(8,128)(2,1)S(1)} %copy-done.14, f32[384]{0:T(512)S(1)} %select_reduce_fusion.1, bf16[384,4224]{1,0:T(8,128)(2,1)S(1)} %get-tuple-element.88), kind=kOutput, calls=%fused_computation.36 | convolution fusion | flops 1208107008 | bytes 6883328 | tf_op jit(solution)/shard_map/rd,fd->rf/dot_general | solution.py:149
  69.7 1.8 %fusion.18 = f32[384,384]{1,0:T(8,128)S(1)} fusion(bf16[1,384,4096]{2,1,0:T(8,128)(2,1)S(1)} %copy-done.1, bf16[384,4224]{1,0:T(8,128)(2,1)S(1)} %get-tuple-element.89), kind=kOutput, calls=%fused_computation.19 | convolution fusion | flops 1207959552 | bytes 6881280 | tf_op jit(solution)/shard_map/rd,fd->rf/dot_general | solution.py:147
  71.5 2.7 %multiply_convert_fusion.1 = (bf16[384,384]{1,0:T(8,128)(2,1)}, bf16[384,384]{1,0:T(8,128)(2,1)S(1)}, bf16[384,384]{1,0:T(8,128)(2,1)S(1)}) fusion(f32[384]{0:T(512)S(1)} %select_reduce_fusion.1, f32[384,384]{1,0:T(8,128)S(1)} %fusion.18, f32[384,384]{1,0:T(8,128)S(1)} %fusion.30, bf16[1,384,4096]{2,1,0:T(8,128)(2,1)S(1)} %copy-done, ...), kind=kOutput, calls=%fused_computation.70 | convolution fusion | flops 1210318848 | bytes 8357888 | tf_op jit(solution)/shard_map/rd,fd->rf/dot_general | solution.py:148
  74.2 1.8 %fusion.16 = f32[384,4096]{1,0:T(8,128)S(1)} fusion(bf16[384,384]{1,0:T(8,128)(2,1)S(1)} %get-tuple-element.95, bf16[1,384,4096]{2,1,0:T(8,128)(2,1)S(1)} %copy-done.1), kind=kOutput, calls=%fused_computation.17 | convolution fusion | flops 1207959552 | bytes 9732096 | tf_op jit(solution)/shard_map/rf,fd->rd/dot_general | solution.py:157
  76.0 1.9 %add_convert_fusion.1 = bf16[384,4096]{1,0:T(8,128)(2,1)S(1)} fusion(f32[384,4096]{1,0:T(8,128)S(1)} %fusion.16, bf16[384,384]{1,0:T(8,128)(2,1)S(1)} %get-tuple-element.96, bf16[1,384,4096]{2,1,0:T(8,128)(2,1)S(1)} %copy-done), kind=kOutput, calls=%fused_computation.6 | convolution fusion | flops 1211105280 | bytes 12877824 | tf_op jit(solution)/shard_map/rf,fd->rd/dot_general | solution.py:158
  81.3 3.9 %collective-permute-done.19 = bf16[24,4224]{1,0:T(8,128)(2,1)S(1)} collective-permute-done((bf16[24,4224]{1,0:T(8,128)(2,1)S(1)}, bf16[24,4224]{1,0:T(8,128)(2,1)S(1)}, u32[]{:S(2)}, u32[]{:S(2)}) %collective-permute-start.19) | collective-permute-done | bytes 202784 | tf_op jit(solution)/shard_map/ppermute | solution.py:101
  93.4 3.0 %collective-permute-done.25 = bf16[2,96,4224]{2,1,0:T(8,128)(2,1)S(1)} collective-permute-done((bf16[2,96,4224]{2,1,0:T(8,128)(2,1)S(1)}, bf16[2,96,4224]{2,1,0:T(8,128)(2,1)S(1)}, u32[]{:S(2)}, u32[]{:S(2)}) %collective-permute-start.25) | collective-permute-done | bytes 1622048 | tf_op jit(solution)/shard_map/ppermute | solution.py:101
  98.2 1.8 %fusion.33 = f32[384,384]{1,0:T(8,128)S(1)} fusion(bf16[1,384,4096]{2,1,0:T(8,128)(2,1)S(1)} %copy-done.15, f32[384]{0:T(512)S(1)} %select_reduce_fusion, bf16[384,4224]{1,0:T(8,128)(2,1)S(1)} %get-tuple-element.82), kind=kOutput, calls=%fused_computation.37 | convolution fusion | flops 1208107008 | bytes 6883328 | tf_op jit(solution)/shard_map/rd,fd->rf/dot_general | solution.py:149
  100.0 1.8 %fusion.14 = f32[384,384]{1,0:T(8,128)S(1)} fusion(bf16[1,384,4096]{2,1,0:T(8,128)(2,1)S(1)} %copy-done.1, bf16[384,4224]{1,0:T(8,128)(2,1)S(1)} %get-tuple-element.83), kind=kOutput, calls=%fused_computation.15 | convolution fusion | flops 1207959552 | bytes 6881280 | tf_op jit(solution)/shard_map/rd,fd->rf/dot_general | solution.py:147
  101.8 2.7 %multiply_convert_fusion = (bf16[384,384]{1,0:T(8,128)(2,1)}, bf16[384,384]{1,0:T(8,128)(2,1)S(1)}, bf16[384,384]{1,0:T(8,128)(2,1)S(1)}) fusion(f32[384]{0:T(512)S(1)} %select_reduce_fusion, f32[384,384]{1,0:T(8,128)S(1)} %fusion.14, f32[384,384]{1,0:T(8,128)S(1)} %fusion.33, bf16[1,384,4096]{2,1,0:T(8,128)(2,1)S(1)} %copy-done, ...), kind=kOutput, calls=%fused_computation.69 | convolution fusion | flops 1210318848 | bytes 8357888 | tf_op jit(solution)/shard_map/rd,fd->rf/dot_general | solution.py:148
  104.5 1.8 %fusion.12 = f32[384,4096]{1,0:T(8,128)S(1)} fusion(bf16[384,384]{1,0:T(8,128)(2,1)S(1)} %get-tuple-element.98, bf16[1,384,4096]{2,1,0:T(8,128)(2,1)S(1)} %copy-done.1), kind=kOutput, calls=%fused_computation.13 | convolution fusion | flops 1207959552 | bytes 9732096 | tf_op jit(solution)/shard_map/rf,fd->rd/dot_general | solution.py:157
  106.3 1.9 %add_convert_fusion = bf16[384,4096]{1,0:T(8,128)(2,1)S(1)} fusion(f32[384,4096]{1,0:T(8,128)S(1)} %fusion.12, bf16[384,384]{1,0:T(8,128)(2,1)S(1)} %get-tuple-element.99, bf16[1,384,4096]{2,1,0:T(8,128)(2,1)S(1)} %copy-done), kind=kOutput, calls=%fused_computation.5 | convolution fusion | flops 1211105280 | bytes 12877824 | tf_op jit(solution)/shard_map/rf,fd->rd/dot_general | solution.py:158
  113.8 3.2 %collective-permute-done.28 = bf16[24,4096]{1,0:T(8,128)(2,1)S(1)} collective-permute-done((bf16[24,4096]{1,0:T(8,128)(2,1)S(1)}, bf16[24,4096]{1,0:T(8,128)(2,1)S(1)}, u32[]{:S(2)}, u32[]{:S(2)}) %collective-permute-start.28) | collective-permute-done | bytes 196640 | tf_op jit(solution)/shard_map/ppermute | solution.py:101
  124.0 2.2 %collective-permute-done.33 = bf16[24,2048]{1,0:T(8,128)(2,1)S(1)} collective-permute-done((bf16[24,2048]{1,0:T(8,128)(2,1)S(1)}, bf16[24,2048]{1,0:T(8,128)(2,1)S(1)}, u32[]{:S(2)}, u32[]{:S(2)}) %collective-permute-start.33) | collective-permute-done | bytes 98336 | tf_op jit(solution)/shard_map/ppermute | solution.py:101
  127.0 4.0 %fusion.7 = bf16[1,384,4096]{2,1,0:T(8,128)(2,1)} fusion(bf16[384,4096]{1,0:T(8,128)(2,1)S(1)} %slice.510, bf16[384,4096]{1,0:T(8,128)(2,1)S(1)} %slice.496, bf16[384,384]{1,0:T(8,128)(2,1)S(1)} %copy-done.9, bf16[384,384]{1,0:T(8,128)(2,1)S(1)} %copy-done.7), kind=kOutput, calls=%fused_computation.10 | convolution fusion | flops 2431254528 | bytes 10027008 | tf_op jit(solution)/shard_map/rf,rd->fd/dot_general | solution.py:244
  131.1 2.0 %collective-permute-done.34 = bf16[24,4096]{1,0:T(8,128)(2,1)S(1)} collective-permute-done((bf16[24,4096]{1,0:T(8,128)(2,1)S(1)}, bf16[24,4096]{1,0:T(8,128)(2,1)S(1)}, u32[]{:S(2)}, u32[]{:S(2)}) %collective-permute-start.34) | collective-permute-done | bytes 196640 | tf_op jit(solution)/shard_map/ppermute | solution.py:101
  135.3 4.0 %fusion.8 = bf16[1,384,4096]{2,1,0:T(8,128)(2,1)} fusion(bf16[384,4096]{1,0:T(8,128)(2,1)S(1)} %slice.510, bf16[384,4096]{1,0:T(8,128)(2,1)S(1)} %slice.496, bf16[384,384]{1,0:T(8,128)(2,1)S(1)} %get-tuple-element.99, bf16[384,384]{1,0:T(8,128)(2,1)S(1)} %copy-done.5), kind=kOutput, calls=%fused_computation.11 | convolution fusion | flops 2431254528 | bytes 10027008 | tf_op jit(solution)/shard_map/rf,rd->fd/dot_general | solution.py:244
  141.4 2.8 %collective-permute-start.39 = (bf16[24,4096]{1,0:T(8,128)(2,1)S(1)}, bf16[24,4096]{1,0:T(8,128)(2,1)S(1)}, u32[]{:S(2)}, u32[]{:S(2)}) collective-permute-start(bf16[24,4096]{1,0:T(8,128)(2,1)S(1)} %add_convert_fusion.3), channel_id=1, source_target_pairs={{0,8},{1,9},{2,10},{3,11},{4,12},{5,13},{6,14},{7,15},{8,0},{9,1},... | collective-permute-start | bytes 589832 | tf_op jit(solution)/shard_map/ppermute | solution.py:101
  144.3 4.0 %fusion.9 = bf16[1,384,4096]{2,1,0:T(8,128)(2,1)} fusion(bf16[384,4096]{1,0:T(8,128)(2,1)S(1)} %slice.508, bf16[384,4096]{1,0:T(8,128)(2,1)S(1)} %slice.493, bf16[384,384]{1,0:T(8,128)(2,1)S(1)} %copy-done.17, bf16[384,384]{1,0:T(8,128)(2,1)S(1)} %copy-done.16), kind=kOutput, calls=%fused_computation.12 | convolution fusion | flops 2431254528 | bytes 10027008 | tf_op jit(solution)/shard_map/rf,rd->fd/dot_general | solution.py:244
  148.3 1.9 %collective-permute-done.39 = bf16[24,4096]{1,0:T(8,128)(2,1)S(1)} collective-permute-done((bf16[24,4096]{1,0:T(8,128)(2,1)S(1)}, bf16[24,4096]{1,0:T(8,128)(2,1)S(1)}, u32[]{:S(2)}, u32[]{:S(2)}) %collective-permute-start.39) | collective-permute-done | bytes 196640 | tf_op jit(solution)/shard_map/ppermute | solution.py:101
  150.2 1.8 %add_convert_fusion.2 = bf16[24,4096]{1,0:T(8,128)(2,1)} fusion(bf16[24,4096]{1,0:T(8,128)(2,1)S(1)} %collective-permute-done.39, bf16[24,4096]{1,0:T(8,128)(2,1)S(1)} %copy-done.13, bf16[24,4096]{1,0:T(8,128)(2,1)S(1)} %copy-done.11, bf16[24,4096]{1,0:T(8,128)(2,1)S(1)} %collective-permute-done.27, bf16[8,24,4096]{2,1,0:T(8,128)(2,1)} %copy-done.3, ...), kind=kLoop, calls=%fused_computation.120 | loop fusion | flops 1572864 | bytes 1376256 | tf_op jit(solution)/shard_map/convert_element_type | solution.py:122
  (189 shorter events, 51.8 us)
Async XLA Ops:
  4.1 18.8 %collective-permute-start.2 = (bf16[2,24,4224]{2,1,0:T(8,128)(2,1)}, bf16[2,24,4224]{2,1,0:T(8,128)(2,1)}, u32[]{:S(2)}, u32[]{:S(2)}) collective-permute-start(bf16[2,24,4224]{2,1,0:T(8,128)(2,1)} %pad_maximum_fusion.10), channel_id=1, source_target_pairs={{0,4},{1,5},{2,6},{3,7},{4,0},{5,1},{6,2},{7,3},{8,12},{9,13},{10,... | collective-permute-start | bytes 1216520 | tf_op jit(solution)/shard_map/ppermute | solution.py:101
  7.1 15.8 %collective-permute-start.1 = (bf16[2,24,4224]{2,1,0:T(8,128)(2,1)}, bf16[2,24,4224]{2,1,0:T(8,128)(2,1)}, u32[]{:S(2)}, u32[]{:S(2)}) collective-permute-start(bf16[2,24,4224]{2,1,0:T(8,128)(2,1)} %pad_maximum_fusion.10), channel_id=1, source_target_pairs={{0,16},{16,0},{1,17},{17,1},{2,18},{18,2},{3,19},{19,3},{4,20},{20... | collective-permute-start | bytes 1216520 | tf_op jit(solution)/shard_map/ppermute | solution.py:101
  8.6 14.3 %collective-permute-start = (bf16[2,24,4224]{2,1,0:T(8,128)(2,1)}, bf16[2,24,4224]{2,1,0:T(8,128)(2,1)}, u32[]{:S(2)}, u32[]{:S(2)}) collective-permute-start(bf16[2,24,4224]{2,1,0:T(8,128)(2,1)} %pad_maximum_fusion.10), channel_id=1, source_target_pairs={{0,2},{1,3},{2,0},{3,1},{4,6},{5,7},{6,4},{7,5},{8,10},{9,11},{10,... | collective-permute-start | bytes 1216520 | tf_op jit(solution)/shard_map/ppermute | solution.py:101
  10.1 22.8 %collective-permute-start.7 = (bf16[2,24,4224]{2,1,0:T(8,128)(2,1)}, bf16[2,24,4224]{2,1,0:T(8,128)(2,1)}, u32[]{:S(2)}, u32[]{:S(2)}) collective-permute-start(bf16[2,24,4224]{2,1,0:T(8,128)(2,1)} %pad_maximum_fusion.10), channel_id=1, source_target_pairs={{0,8},{1,9},{2,10},{3,11},{4,12},{5,13},{6,14},{7,15},{8,0},{9,1},... | collective-permute-start | bytes 1216520 | tf_op jit(solution)/shard_map/ppermute | solution.py:101
  27.2 15.3 %collective-permute-start.6 = (bf16[2,96,4224]{2,1,0:T(8,128)(2,1)S(1)}, bf16[2,96,4224]{2,1,0:T(8,128)(2,1)S(1)}, u32[]{:S(2)}, u32[]{:S(2)}) collective-permute-start(bf16[2,96,4224]{2,1,0:T(8,128)(2,1)S(1)} %pad_maximum_fusion.3), channel_id=1, source_target_pairs={{0,1},{1,0},{2,3},{3,2},{4,5},{5,4},{6,7},{7,6},{8,9},{9,8},{10,11... | collective-permute-start | bytes 4866056 | tf_op jit(solution)/shard_map/ppermute | solution.py:101
  27.5 11.8 %collective-permute-start.5 = (bf16[2,24,4224]{2,1,0:T(8,128)(2,1)S(1)}, bf16[2,24,4224]{2,1,0:T(8,128)(2,1)S(1)}, u32[]{:S(2)}, u32[]{:S(2)}) collective-permute-start(bf16[2,24,4224]{2,1,0:T(8,128)(2,1)S(1)} %get-tuple-element.123), channel_id=1, source_target_pairs={{0,4},{1,5},{2,6},{3,7},{4,0},{5,1},{6,2},{7,3},{8,12},{9,13},{10,... | collective-permute-start | bytes 1216520 | tf_op jit(solution)/shard_map/ppermute | solution.py:101
  27.5 12.7 %collective-permute-start.3 = (bf16[2,24,4224]{2,1,0:T(8,128)(2,1)S(1)}, bf16[2,24,4224]{2,1,0:T(8,128)(2,1)S(1)}, u32[]{:S(2)}, u32[]{:S(2)}) collective-permute-start(bf16[2,24,4224]{2,1,0:T(8,128)(2,1)S(1)} %get-tuple-element.124), channel_id=1, source_target_pairs={{0,2},{1,3},{2,0},{3,1},{4,6},{5,7},{6,4},{7,5},{8,10},{9,11},{10,... | collective-permute-start | bytes 1216520 | tf_op jit(solution)/shard_map/ppermute | solution.py:101
  30.2 12.3 %collective-permute-start.4 = (bf16[2,24,4224]{2,1,0:T(8,128)(2,1)S(1)}, bf16[2,24,4224]{2,1,0:T(8,128)(2,1)S(1)}, u32[]{:S(2)}, u32[]{:S(2)}) collective-permute-start(bf16[2,24,4224]{2,1,0:T(8,128)(2,1)S(1)} %get-tuple-element.125), channel_id=1, source_target_pairs={{0,16},{16,0},{1,17},{17,1},{2,18},{18,2},{3,19},{19,3},{4,20},{20... | collective-permute-start | bytes 1216520 | tf_op jit(solution)/shard_map/ppermute | solution.py:101
  42.5 17.8 %collective-permute-start.10 = (bf16[2,24,4224]{2,1,0:T(8,128)(2,1)}, bf16[2,24,4224]{2,1,0:T(8,128)(2,1)S(1)}, u32[]{:S(2)}, u32[]{:S(2)}) collective-permute-start(bf16[2,24,4224]{2,1,0:T(8,128)(2,1)} %collective-permute-done.7), channel_id=1, source_target_pairs={{0,4},{1,5},{2,6},{3,7},{4,0},{5,1},{6,2},{7,3},{8,12},{9,13},{10,... | collective-permute-start | bytes 1216520 | tf_op jit(solution)/shard_map/ppermute | solution.py:101
  44.2 16.1 %collective-permute-start.9 = (bf16[2,24,4224]{2,1,0:T(8,128)(2,1)}, bf16[2,24,4224]{2,1,0:T(8,128)(2,1)S(1)}, u32[]{:S(2)}, u32[]{:S(2)}) collective-permute-start(bf16[2,24,4224]{2,1,0:T(8,128)(2,1)} %collective-permute-done.7), channel_id=1, source_target_pairs={{0,16},{16,0},{1,17},{17,1},{2,18},{18,2},{3,19},{19,3},{4,20},{20... | collective-permute-start | bytes 1216520 | tf_op jit(solution)/shard_map/ppermute | solution.py:101
  45.9 14.4 %collective-permute-start.8 = (bf16[2,24,4224]{2,1,0:T(8,128)(2,1)}, bf16[2,24,4224]{2,1,0:T(8,128)(2,1)S(1)}, u32[]{:S(2)}, u32[]{:S(2)}) collective-permute-start(bf16[2,24,4224]{2,1,0:T(8,128)(2,1)} %collective-permute-done.7), channel_id=1, source_target_pairs={{0,2},{1,3},{2,0},{3,1},{4,6},{5,7},{6,4},{7,5},{8,10},{9,11},{10,... | collective-permute-start | bytes 1216520 | tf_op jit(solution)/shard_map/ppermute | solution.py:101
  46.2 12.9 %collective-permute-start.12 = (bf16[24,4224]{1,0:T(8,128)(2,1)S(1)}, bf16[24,4224]{1,0:T(8,128)(2,1)S(1)}, u32[]{:S(2)}, u32[]{:S(2)}) collective-permute-start(bf16[24,4224]{1,0:T(8,128)(2,1)S(1)} %get-tuple-element.116), channel_id=1, source_target_pairs={{0,16},{16,0},{1,17},{17,1},{2,18},{18,2},{3,19},{19,3},{4,20},{20... | collective-permute-start | bytes 608264 | tf_op jit(solution)/shard_map/ppermute | solution.py:101
  46.6 13.7 %collective-permute-start.11 = (bf16[24,4224]{1,0:T(8,128)(2,1)S(1)}, bf16[24,4224]{1,0:T(8,128)(2,1)S(1)}, u32[]{:S(2)}, u32[]{:S(2)}) collective-permute-start(bf16[24,4224]{1,0:T(8,128)(2,1)S(1)} %get-tuple-element.117), channel_id=1, source_target_pairs={{0,2},{1,3},{2,0},{3,1},{4,6},{5,7},{6,4},{7,5},{8,10},{9,11},{10,... | collective-permute-start | bytes 608264 | tf_op jit(solution)/shard_map/ppermute | solution.py:101
  60.5 17.4 %collective-permute-start.16 = (bf16[2,96,4224]{2,1,0:T(8,128)(2,1)S(1)}, bf16[2,96,4224]{2,1,0:T(8,128)(2,1)S(1)}, u32[]{:S(2)}, u32[]{:S(2)}) collective-permute-start(bf16[2,96,4224]{2,1,0:T(8,128)(2,1)S(1)} %constant_dynamic-update-slice_fusion), channel_id=1, source_target_pairs={{0,1},{1,0},{2,3},{3,2},{4,5},{5,4},{6,7},{7,6},{8,9},{9,8},{10,11... | collective-permute-start | bytes 4866056 | tf_op jit(solution)/shard_map/ppermute | solution.py:101
  61.7 16.2 %collective-permute-start.15 = (bf16[2,24,4224]{2,1,0:T(8,128)(2,1)}, bf16[2,24,4224]{2,1,0:T(8,128)(2,1)S(1)}, u32[]{:S(2)}, u32[]{:S(2)}) collective-permute-start(bf16[2,24,4224]{2,1,0:T(8,128)(2,1)} %get-tuple-element.120), channel_id=1, source_target_pairs={{0,4},{1,5},{2,6},{3,7},{4,0},{5,1},{6,2},{7,3},{8,12},{9,13},{10,... | collective-permute-start | bytes 1216520 | tf_op jit(solution)/shard_map/ppermute | solution.py:101
  62.4 15.5 %collective-permute-start.13 = (bf16[2,24,4224]{2,1,0:T(8,128)(2,1)}, bf16[2,24,4224]{2,1,0:T(8,128)(2,1)S(1)}, u32[]{:S(2)}, u32[]{:S(2)}) collective-permute-start(bf16[2,24,4224]{2,1,0:T(8,128)(2,1)} %get-tuple-element.121), channel_id=1, source_target_pairs={{0,2},{1,3},{2,0},{3,1},{4,6},{5,7},{6,4},{7,5},{8,10},{9,11},{10,... | collective-permute-start | bytes 1216520 | tf_op jit(solution)/shard_map/ppermute | solution.py:101
  63.1 14.8 %collective-permute-start.14 = (bf16[2,24,4224]{2,1,0:T(8,128)(2,1)S(1)}, bf16[2,24,4224]{2,1,0:T(8,128)(2,1)S(1)}, u32[]{:S(2)}, u32[]{:S(2)}) collective-permute-start(bf16[2,24,4224]{2,1,0:T(8,128)(2,1)S(1)} %get-tuple-element.122), channel_id=1, source_target_pairs={{0,16},{16,0},{1,17},{17,1},{2,18},{18,2},{3,19},{19,3},{4,20},{20... | collective-permute-start | bytes 1216520 | tf_op jit(solution)/shard_map/ppermute | solution.py:101
  78.1 7.1 %collective-permute-start.19 = (bf16[24,4224]{1,0:T(8,128)(2,1)S(1)}, bf16[24,4224]{1,0:T(8,128)(2,1)S(1)}, u32[]{:S(2)}, u32[]{:S(2)}) collective-permute-start(bf16[24,4224]{1,0:T(8,128)(2,1)S(1)} %get-tuple-element.106), channel_id=1, source_target_pairs={{0,16},{16,0},{1,17},{17,1},{2,18},{18,2},{3,19},{19,3},{4,20},{20... | collective-permute-start | bytes 608264 | tf_op jit(solution)/shard_map/ppermute | solution.py:101
  79.7 6.8 %collective-permute-start.18 = (bf16[24,4224]{1,0:T(8,128)(2,1)S(1)}, bf16[24,4224]{1,0:T(8,128)(2,1)S(1)}, u32[]{:S(2)}, u32[]{:S(2)}) collective-permute-start(bf16[24,4224]{1,0:T(8,128)(2,1)S(1)} %get-tuple-element.107), channel_id=1, source_target_pairs={{0,2},{1,3},{2,0},{3,1},{4,6},{5,7},{6,4},{7,5},{8,10},{9,11},{10,... | collective-permute-start | bytes 608264 | tf_op jit(solution)/shard_map/ppermute | solution.py:101
  87.0 6.4 %collective-permute-start.24 = (bf16[24,2048]{1,0:T(8,128)(2,1)S(1)}, bf16[24,2048]{1,0:T(8,128)(2,1)S(1)}, u32[]{:S(2)}, u32[]{:S(2)}) collective-permute-start(bf16[24,2048]{1,0:T(8,128)(2,1)S(1)} %get-tuple-element.138), channel_id=1, source_target_pairs={{0,16},{16,0},{1,17},{17,1},{2,18},{18,2},{3,19},{19,3},{4,20},{20... | collective-permute-start | bytes 294920 | tf_op jit(solution)/shard_map/ppermute | solution.py:101
  89.7 18.5 %collective-permute-start.21 = (bf16[2,24,2048]{2,1,0:T(8,128)(2,1)}, bf16[2,24,2048]{2,1,0:T(8,128)(2,1)}, u32[]{:S(2)}, u32[]{:S(2)}) collective-permute-start(bf16[2,24,2048]{2,1,0:T(8,128)(2,1)} %pad_maximum_fusion.13), channel_id=1, source_target_pairs={{0,2},{1,3},{2,0},{3,1},{4,6},{5,7},{6,4},{7,5},{8,10},{9,11},{10,... | collective-permute-start | bytes 589832 | tf_op jit(solution)/shard_map/ppermute | solution.py:101
  91.0 17.2 %collective-permute-start.22 = (bf16[2,24,2048]{2,1,0:T(8,128)(2,1)}, bf16[2,24,2048]{2,1,0:T(8,128)(2,1)}, u32[]{:S(2)}, u32[]{:S(2)}) collective-permute-start(bf16[2,24,2048]{2,1,0:T(8,128)(2,1)} %pad_maximum_fusion.14), channel_id=1, source_target_pairs={{0,16},{16,0},{1,17},{17,1},{2,18},{18,2},{3,19},{19,3},{4,20},{20... | collective-permute-start | bytes 589832 | tf_op jit(solution)/shard_map/ppermute | solution.py:101
  96.8 11.4 %collective-permute-start.26 = (bf16[24,4096]{1,0:T(8,128)(2,1)S(1)}, bf16[24,4096]{1,0:T(8,128)(2,1)S(1)}, u32[]{:S(2)}, u32[]{:S(2)}) collective-permute-start(bf16[24,4096]{1,0:T(8,128)(2,1)S(1)} %pad_maximum_fusion.15), channel_id=1, source_target_pairs={{0,4},{1,5},{2,6},{3,7},{4,0},{5,1},{6,2},{7,3},{8,12},{9,13},{10,... | collective-permute-start | bytes 589832 | tf_op jit(solution)/shard_map/ppermute | solution.py:101
  108.4 10.3 %collective-permute-start.30 = (bf16[8,24,4096]{2,1,0:T(8,128)(2,1)S(1)}, bf16[8,24,4096]{2,1,0:T(8,128)(2,1)S(1)}, u32[]{:S(2)}, u32[]{:S(2)}) collective-permute-start(bf16[8,24,4096]{2,1,0:T(8,128)(2,1)S(1)} %slice_bitcast_fusion), channel_id=1, source_target_pairs={{0,1},{1,0},{2,3},{3,2},{4,5},{5,4},{6,7},{7,6},{8,9},{9,8},{10,11... | collective-permute-start | bytes 4718600 | tf_op jit(solution)/shard_map/ppermute | solution.py:101
  109.7 7.4 %collective-permute-start.28 = (bf16[24,4096]{1,0:T(8,128)(2,1)S(1)}, bf16[24,4096]{1,0:T(8,128)(2,1)S(1)}, u32[]{:S(2)}, u32[]{:S(2)}) collective-permute-start(bf16[24,4096]{1,0:T(8,128)(2,1)S(1)} %pad_maximum_fusion.17), channel_id=1, source_target_pairs={{0,16},{16,0},{1,17},{17,1},{2,18},{18,2},{3,19},{19,3},{4,20},{20... | collective-permute-start | bytes 589832 | tf_op jit(solution)/shard_map/ppermute | solution.py:101
  110.3 7.1 %collective-permute-start.27 = (bf16[24,4096]{1,0:T(8,128)(2,1)S(1)}, bf16[24,4096]{1,0:T(8,128)(2,1)S(1)}, u32[]{:S(2)}, u32[]{:S(2)}) collective-permute-start(bf16[24,4096]{1,0:T(8,128)(2,1)S(1)} %pad_maximum_fusion.16), channel_id=1, source_target_pairs={{0,2},{1,3},{2,0},{3,1},{4,6},{5,7},{6,4},{7,5},{8,10},{9,11},{10,... | collective-permute-start | bytes 589832 | tf_op jit(solution)/shard_map/ppermute | solution.py:101
  111.8 6.8 %collective-permute-start.29 = (bf16[24,4096]{1,0:T(8,128)(2,1)S(1)}, bf16[24,4096]{1,0:T(8,128)(2,1)S(1)}, u32[]{:S(2)}, u32[]{:S(2)}) collective-permute-start(bf16[24,4096]{1,0:T(8,128)(2,1)S(1)} %pad_maximum_fusion.18), channel_id=1, source_target_pairs={{0,4},{1,5},{2,6},{3,7},{4,0},{5,1},{6,2},{7,3},{8,12},{9,13},{10,... | collective-permute-start | bytes 589832 | tf_op jit(solution)/shard_map/ppermute | solution.py:101
  121.3 9.8 %collective-permute-start.36 = (bf16[2,24,2048]{2,1,0:T(8,128)(2,1)S(1)}, bf16[2,24,2048]{2,1,0:T(8,128)(2,1)S(1)}, u32[]{:S(2)}, u32[]{:S(2)}) collective-permute-start(bf16[2,24,2048]{2,1,0:T(8,128)(2,1)S(1)} %pad_maximum_fusion.22), channel_id=1, source_target_pairs={{0,2},{1,3},{2,0},{3,1},{4,6},{5,7},{6,4},{7,5},{8,10},{9,11},{10,... | collective-permute-start | bytes 589832 | tf_op jit(solution)/shard_map/ppermute | solution.py:101
  122.8 8.3 %collective-permute-start.31 = (bf16[2,24,2048]{2,1,0:T(8,128)(2,1)S(1)}, bf16[2,24,2048]{2,1,0:T(8,128)(2,1)S(1)}, u32[]{:S(2)}, u32[]{:S(2)}) collective-permute-start(bf16[2,24,2048]{2,1,0:T(8,128)(2,1)S(1)} %pad_maximum_fusion.19), channel_id=1, source_target_pairs={{0,16},{16,0},{1,17},{17,1},{2,18},{18,2},{3,19},{19,3},{4,20},{20... | collective-permute-start | bytes 589832 | tf_op jit(solution)/shard_map/ppermute | solution.py:101
  126.3 6.8 %collective-permute-start.34 = (bf16[24,4096]{1,0:T(8,128)(2,1)S(1)}, bf16[24,4096]{1,0:T(8,128)(2,1)S(1)}, u32[]{:S(2)}, u32[]{:S(2)}) collective-permute-start(bf16[24,4096]{1,0:T(8,128)(2,1)S(1)} %pad_maximum_fusion.20), channel_id=1, source_target_pairs={{0,4},{1,5},{2,6},{3,7},{4,0},{5,1},{6,2},{7,3},{8,12},{9,13},{10,... | collective-permute-start | bytes 589832 | tf_op jit(solution)/shard_map/ppermute | solution.py:101
  133.2 6.6 %collective-permute-start.38 = (bf16[24,4096]{1,0:T(8,128)(2,1)S(1)}, bf16[24,4096]{1,0:T(8,128)(2,1)S(1)}, u32[]{:S(2)}, u32[]{:S(2)}) collective-permute-start(bf16[24,4096]{1,0:T(8,128)(2,1)S(1)} %pad_maximum_fusion.24), channel_id=1, source_target_pairs={{0,4},{1,5},{2,6},{3,7},{4,0},{5,1},{6,2},{7,3},{8,12},{9,13},{10,... | collective-permute-start | bytes 589832 | tf_op jit(solution)/shard_map/ppermute | solution.py:101
  141.4 8.7 %collective-permute-start.39 = (bf16[24,4096]{1,0:T(8,128)(2,1)S(1)}, bf16[24,4096]{1,0:T(8,128)(2,1)S(1)}, u32[]{:S(2)}, u32[]{:S(2)}) collective-permute-start(bf16[24,4096]{1,0:T(8,128)(2,1)S(1)} %add_convert_fusion.3), channel_id=1, source_target_pairs={{0,8},{1,9},{2,10},{3,11},{4,12},{5,13},{6,14},{7,15},{8,0},{9,1},... | collective-permute-start | bytes 589832 | tf_op jit(solution)/shard_map/ppermute | solution.py:101
  (26 other events, 206.9 us)

commit v3 on v2

--- a/solution.py
+++ b/solution.py
@@ -138,9 +138,9 @@
     gate_w, up_w, down_w = w_gate[0], w_up[0], w_down[0]
     own = jnp.arange(LANES, dtype=jnp.int32) == lax.axis_index("expert")
 
-    def expert_rows(near, far, near_other, far_other):
-        x_rows = rows_of(near[0], far[0], near_other[0], far_other[0])[:, :features]
-        g_rows = rows_of(near[1], far[1], near_other[1], far_other[1])
+    def expert_rows(lane, other):
+        x_rows = rows_of(lane[0], other[0])[:, :features]
+        g_rows = rows_of(lane[1], other[1])
         scale = g_rows[:, features:].astype(jnp.float32)
         scale = jnp.sum(jnp.where(own, scale, 0.0), axis=-1, keepdims=True)
         g_rows = g_rows[:, :features]
@@ -156,7 +156,7 @@
         ).astype(jnp.bfloat16)
         part = jnp.einsum("rf,fd->rd", d_gate_act, gate_w, preferred_element_type=jnp.float32)
         part = part + jnp.einsum("rf,fd->rd", d_up_act, up_w, preferred_element_type=jnp.float32)
-        part = part.astype(jnp.bfloat16).reshape(2, 8, rows, features)
+        part = part.astype(jnp.bfloat16).reshape(2, 4, rows, features)
         return part, (x_rows, g_rows, hidden, d_gate_act, d_up_act)
 
     def near_of(mine, from_x, from_y, from_z):
@@ -186,65 +186,87 @@
     scales = gate_of_expert(routes, gates, experts)
     scales = jnp.pad(scales, ((0, 0), (0, LANES - experts)))
     mine = jnp.stack([jnp.pad(tokens, ((0, 0), (0, LANES))), jnp.concatenate([out_grad, scales], axis=1)])
-    first = firsts(mine)
+    from_x, from_y, from_z = firsts(mine)
     distant = over_far_z(mine)
-    first = together(first)
-    second = seconds(*first)
-    near = near_of(mine, *first)
+    from_x, from_y = together((from_x, from_y))
+    g_far, t_far = over_x(from_y[1]), over_y(from_x[0])
+    from_z, g_far, t_far = together((from_z, g_far, t_far))
+    z_x, z_y = over_x(from_z), over_y(from_z)
+    near = near_of(mine, from_x, from_y, from_z)
     near_other = over_core(near)
-    second, near_other, distant = together((second, near_other, distant))
+    z_x, z_y, near_other, distant = together((z_x, z_y, near_other, distant))
     first2 = firsts(distant)
-    third = thirds(second[2])
-    first2, third = together((first2, third))
+    third = over_x(z_y[1]), over_y(z_x[0])
+    part_near, kept_near = expert_rows(near, near_other)
+    first2, third, part_near = together((first2, third, part_near))
     second2 = seconds(*first2)
-    far = far_of(*second, *third)
+    far = jnp.stack(
+        [rows_of(t_far, z_y[0], z_x[0], third[1]), rows_of(g_far, z_y[1], z_x[1], third[0])]
+    )
     far_other = over_core(far)
     near2 = near_of(distant, *first2)
     near2_other = over_core(near2)
-    part, kept = expert_rows(near, far, near_other, far_other)
-    second2, near2_other, part = together((second2, near2_other, part))
+    part_far, kept_far = expert_rows(far, far_other)
+    second2, near2_other, part_far = together((second2, near2_other, part_far))
     third2 = thirds(second2[2])
-    part_other = over_core(part[1])
-    third2, part_other = together((third2, part_other))
+    others = over_core(part_near[1]), over_core(part_far[1])
+    part_near2, kept_near2 = expert_rows(near2, near2_other)
+    third2, others, part_near2 = together((third2, others, part_near2))
     far2 = far_of(*second2, *third2)
     far2_other = over_core(far2)
 
-    def lane_sums(part, part_other):
-        own, x, y, z, xy, yz, xz, xyz = (summed(part[i], part_other[i]) for i in range(8))
-        opening = over_x(xyz[:, half:]), over_y(xyz[:, :half])
-        middle = over_x(jnp.stack([xy[:, half:], xz[:, half:]])), over_y(jnp.stack([xy[:, :half], yz[:, :half]]))
-        return (own, x, y, z, yz[:, half:], xz[:, :half]), opening, middle
+    def lane_sums(near_part, far_part, near_part_other, far_part_other):
+        return tuple(summed(near_part[i], near_part_other[i]) for i in range(4)) + tuple(
+            summed(far_part[i], far_part_other[i]) for i in range(4)
+        )
+
+    def opening_sends(sums):
+        return over_x(sums[7][:, half:]), over_y(sums[7][:, :half])
+
+    def middle_sends(sums):
+        _, _, _, _, xy, yz, xz, _ = sums
+        return over_x(jnp.stack([xy[:, half:], xz[:, half:]])), over_y(jnp.stack([xy[:, :half], yz[:, :half]]))
+
+    def early_sends(sums):
+        _, _, _, _, xy, yz, xz, xyz = sums
+        in_x = over_x(jnp.stack([xyz[:, half:], xy[:, half:], xz[:, half:]]))
+        in_y = over_y(jnp.stack([xyz[:, :half], xy[:, :half], yz[:, :half]]))
+        return in_x, in_y
 
     def sent_z(sums, opening):
-        return over_z(jnp.concatenate([summed(sums[5], opening[1]), summed(sums[4], opening[0])], axis=1))
+        _, _, _, _, _, yz, xz, _ = sums
+        return over_z(jnp.concatenate([summed(xz[:, :half], opening[1]), summed(yz[:, half:], opening[0])], axis=1))
 
     def last_sends(sums, middle, from_z):
-        _, x, y, z, _, _ = sums
+        _, x, y, z, _, _, _, _ = sums
         from_x, from_y = middle
         x = jnp.concatenate([summed(x[:, :half], from_y[0], from_z[:, :half]), x[:, half:]], axis=1)
         y = jnp.concatenate([y[:, :half], summed(y[:, half:], from_x[0], from_z[:, half:])], axis=1)
         z = jnp.concatenate([summed(z[:, :half], from_y[1]), summed(z[:, half:], from_x[1])], axis=1)
         return over_x(x), over_y(y), over_z(z)
 
-    sums, opening, middle = lane_sums(part[0], part_other)
-    opening, far2_other = together((opening, far2_other))
-    from_z = sent_z(sums, opening)
-    part2, kept2 = expert_rows(near2, far2, near2_other, far2_other)
-    middle, from_z, part2 = together((middle, from_z, part2))
-    part2_other = over_core(part2[1])
-    last = last_sends(sums, middle, from_z)
-    last, part2_other = together((last, part2_other))
-    near_total = summed(sums[0], *last)
-    sums2, opening2, middle2 = lane_sums(part2[0], part2_other)
+    sums = lane_sums(part_near[0], part_far[0], *others)
+    in_x, in_y = early_sends(sums)
+    part_far2, kept_far2 = expert_rows(far2, far2_other)
+    part_far2, in_x, in_y = together((part_far2, in_x, in_y))
+    others2 = over_core(part_near2[1]), over_core(part_far2[1])
+    middle = in_x[1:], in_y[1:]
+    from_z = sent_z(sums, (in_x[0], in_y[0]))
+    sums2 = lane_sums(part_near2[0], part_far2[0], *others2)
+    opening2, middle2 = opening_sends(sums2), middle_sends(sums2)
     from_z2 = sent_z(sums2, opening2)
     last2 = last_sends(sums2, middle2, from_z2)
-    d_tokens = summed(near_total, over_far_z(summed(sums2[0], *last2)))
+    sums, middle, from_z, last2 = together((sums, middle, from_z, last2))
+    returned = over_far_z(summed(sums2[0], *last2))
+    last = last_sends(sums, middle, from_z)
+    d_tokens = summed(sums[0], *last, returned)
 
     def weight_grad(at, side):
+        kept = (kept_near, kept_far, kept_near2, kept_far2)
         return jnp.einsum(
             "rf,rd->fd",
-            rows_of(kept[at], kept2[at]),
-            rows_of(kept[side], kept2[side]),
+            rows_of(*(held[at] for held in kept)),
+            rows_of(*(held[side] for held in kept)),
             preferred_element_type=jnp.float32,
         ).astype(jnp.bfloat16)[None]
 

time: 152 us -> 134 us (0.88)
  waiting for transfers between devices: 53.9 us -> 35 us
  matrix products: 32 us -> 35.2 us
  other arithmetic: 12.7 us -> 10.3 us
  starting transfers between devices: 43.4 us -> 41.8 us
    ppermute x40 -> x41, waiting for transfers between devices: 53.9 us -> 35 us  [swapped(): return lax.ppermute(x, axis, [(i, i ^ bits) for i in range(count)])]
    unnamed x58 -> x31, local copies, waits for them, and re-layouts: 2.93 us -> 6.41 us
    convert_element_type x10 -> x12, other arithmetic: 5 us -> 2.22 us  [summed(): return total.astype(jnp.bfloat16)]
    squeeze x2 -> x12, local copies, waits for them, and re-layouts: 0.25 us -> 2.17 us  [the longest x2 1.44 us: dense_plan(): g_far, t_far = (over_x(from_y[1]), over_y(from_x[0]))]
    ppermute x40 -> x41, starting transfers between devices: 43.4 us -> 41.8 us  [swapped(): return lax.ppermute(x, axis, [(i, i ^ bits) for i in range(count)])]
    dot_general x2 -> x4, matrix products: 3.6 us -> 4.71 us  [expert_rows(): jnp.einsum('rd,fd->rf', x_rows, gate_w, preferred_element_type=jnp.float32)]
    dot_general x2 -> x4, matrix products: 3.62 us -> 4.71 us  [expert_rows(): jnp.einsum('rd,fd->rf', g_rows, down_w, preferred_element_type=jnp.float32)]
    dot_general x2 -> x4, matrix products: 3.73 us -> 4.53 us  [expert_rows(): jnp.einsum('rf,fd->rd', d_up_act, up_w, preferred_element_type=jnp.float32)]
  transfers between devices with their start and end apart: 40 -> 41, of which waited for: 18 -> 15; matrix products, arithmetic and copies ran while one was open for 30% -> 36% of each run, Pallas kernels for 0% -> 0%
where the time goes in v3:
time: 134 us
  starting transfers between devices  41.8 us (31%)
  matrix products  35.2 us (26%)
  waiting for transfers between devices  35 us (26%)
  other arithmetic  10.3 us (8%)
  local copies, waits for them, and re-layouts  10 us (7%)
  between operations  1.55 us (1%)
    ppermute x41, starting transfers between devices, swapped(): return lax.ppermute(x, axis, [(i, i ^ bits) for i in range(count)])  41.8 us
    ppermute x41, waiting for transfers between devices, swapped(): return lax.ppermute(x, axis, [(i, i ^ bits) for i in range(count)])  35 us
    dot_general x3, matrix products, weight_grad(): jnp.einsum('rf,rd->fd', rows_of(*(held[at] for held in kept)), rows_of(*(...  12.1 us
    unnamed x31, local copies, waits for them, and re-layouts  6.41 us
    dot_general x4, matrix products, expert_rows(): jnp.einsum('rd,fd->rf', x_rows, up_w, preferred_element_type=jnp.float32)  5.08 us
    dot_general x4, matrix products, expert_rows(): jnp.einsum('rd,fd->rf', x_rows, gate_w, preferred_element_type=jnp.float32)  4.71 us
    dot_general x4, matrix products, expert_rows(): jnp.einsum('rd,fd->rf', g_rows, down_w, preferred_element_type=jnp.float32)  4.71 us
    dot_general x4, matrix products, expert_rows(): jnp.einsum('rf,fd->rd', d_up_act, up_w, preferred_element_type=jnp.float32)  4.53 us
  transfers between devices with their start and end apart: 41, of which 15 were waited for; matrix products, arithmetic and copies ran while one was open for 36% of the time, Pallas kernels for 0%

profile of v3, /device:TPU:0, one launch (start us, length us, event | category | flops | bytes accessed | tf_op | source)
XLA Modules:
  0.0 133.8 jit_solution(4464370746768708689)
XLA Ops:
  4.1 2.9 %collective-permute-start.1 = (bf16[2,24,4224]{2,1,0:T(8,128)(2,1)}, bf16[2,24,4224]{2,1,0:T(8,128)(2,1)S(1)}, u32[]{:S(2)}, u32[]{:S(2)}) collective-permute-start(bf16[2,24,4224]{2,1,0:T(8,128)(2,1)} %pad_maximum_fusion.12), channel_id=1, source_target_pairs={{0,2},{1,3},{2,0},{3,1},{4,6},{5,7},{6,4},{7,5},{8,10},{9,11},{10,... | collective-permute-start | bytes 1216520 | tf_op jit(solution)/shard_map/ppermute | solution.py:101
  7.0 1.5 %collective-permute-start.2 = (bf16[2,24,4224]{2,1,0:T(8,128)(2,1)}, bf16[2,24,4224]{2,1,0:T(8,128)(2,1)S(1)}, u32[]{:S(2)}, u32[]{:S(2)}) collective-permute-start(bf16[2,24,4224]{2,1,0:T(8,128)(2,1)} %pad_maximum_fusion.12), channel_id=1, source_target_pairs={{0,16},{16,0},{1,17},{17,1},{2,18},{18,2},{3,19},{19,3},{4,20},{20... | collective-permute-start | bytes 1216520 | tf_op jit(solution)/shard_map/ppermute | solution.py:101
  8.5 1.6 %collective-permute-start = (bf16[2,24,4224]{2,1,0:T(8,128)(2,1)}, bf16[2,24,4224]{2,1,0:T(8,128)(2,1)}, u32[]{:S(2)}, u32[]{:S(2)}) collective-permute-start(bf16[2,24,4224]{2,1,0:T(8,128)(2,1)} %pad_maximum_fusion.12), channel_id=1, source_target_pairs={{0,4},{1,5},{2,6},{3,7},{4,0},{5,1},{6,2},{7,3},{8,12},{9,13},{10,... | collective-permute-start | bytes 1216520 | tf_op jit(solution)/shard_map/ppermute | solution.py:101
  10.1 6.5 %collective-permute-done.1 = bf16[2,24,4224]{2,1,0:T(8,128)(2,1)S(1)} collective-permute-done((bf16[2,24,4224]{2,1,0:T(8,128)(2,1)}, bf16[2,24,4224]{2,1,0:T(8,128)(2,1)S(1)}, u32[]{:S(2)}, u32[]{:S(2)}) %collective-permute-start.1) | collective-permute-done | bytes 405536 | tf_op jit(solution)/shard_map/ppermute | solution.py:101
  16.6 1.5 %collective-permute-done.2 = bf16[2,24,4224]{2,1,0:T(8,128)(2,1)S(1)} collective-permute-done((bf16[2,24,4224]{2,1,0:T(8,128)(2,1)}, bf16[2,24,4224]{2,1,0:T(8,128)(2,1)S(1)}, u32[]{:S(2)}, u32[]{:S(2)}) %collective-permute-start.2) | collective-permute-done | bytes 405536 | tf_op jit(solution)/shard_map/ppermute | solution.py:101
  19.9 1.6 %collective-permute-start.4 = (bf16[24,4224]{1,0:T(8,128)(2,1)}, bf16[24,4224]{1,0:T(8,128)(2,1)}, u32[]{:S(2)}, u32[]{:S(2)}) collective-permute-start(bf16[24,4224]{1,0:T(8,128)(2,1)} %slice_bitcast_fusion.26), channel_id=1, source_target_pairs={{0,16},{16,0},{1,17},{17,1},{2,18},{18,2},{3,19},{19,3},{4,20},{20... | collective-permute-start | bytes 608264 | tf_op jit(solution)/shard_map/ppermute | solution.py:101
  21.6 2.6 %collective-permute-start.8 = (bf16[2,24,4224]{2,1,0:T(8,128)(2,1)}, bf16[2,24,4224]{2,1,0:T(8,128)(2,1)}, u32[]{:S(2)}, u32[]{:S(2)}) collective-permute-start(bf16[2,24,4224]{2,1,0:T(8,128)(2,1)} %pad_maximum_fusion.12), channel_id=1, source_target_pairs={{0,8},{1,9},{2,10},{3,11},{4,12},{5,13},{6,14},{7,15},{8,0},{9,1},... | collective-permute-start | bytes 1216520 | tf_op jit(solution)/shard_map/ppermute | solution.py:101
  26.0 1.6 %collective-permute-start.5 = (bf16[2,24,4224]{2,1,0:T(8,128)(2,1)}, bf16[2,24,4224]{2,1,0:T(8,128)(2,1)S(1)}, u32[]{:S(2)}, u32[]{:S(2)}) collective-permute-start(bf16[2,24,4224]{2,1,0:T(8,128)(2,1)} %collective-permute-done), channel_id=1, source_target_pairs={{0,2},{1,3},{2,0},{3,1},{4,6},{5,7},{6,4},{7,5},{8,10},{9,11},{10,... | collective-permute-start | bytes 1216520 | tf_op jit(solution)/shard_map/ppermute | solution.py:101
  27.6 1.5 %collective-permute-start.6 = (bf16[2,24,4224]{2,1,0:T(8,128)(2,1)}, bf16[2,24,4224]{2,1,0:T(8,128)(2,1)S(1)}, u32[]{:S(2)}, u32[]{:S(2)}) collective-permute-start(bf16[2,24,4224]{2,1,0:T(8,128)(2,1)} %collective-permute-done), channel_id=1, source_target_pairs={{0,16},{16,0},{1,17},{17,1},{2,18},{18,2},{3,19},{19,3},{4,20},{20... | collective-permute-start | bytes 1216520 | tf_op jit(solution)/shard_map/ppermute | solution.py:101
  29.1 1.4 %pad_maximum_fusion.1 = bf16[2,96,4224]{2,1,0:T(8,128)(2,1)S(1)} fusion(bf16[2,24,4224]{2,1,0:T(8,128)(2,1)} %collective-permute-done, bf16[2,24,4224]{2,1,0:T(8,128)(2,1)} %copy-done.4, bf16[2,24,4224]{2,1,0:T(8,128)(2,1)} %copy-done.3, bf16[1,24,4224]{2,1,0:T(8,128)(2,1)S(1)} %get-tuple-element.156, bf16[1,24,4224]{2,1,0:T(8,128)(2,1)S(1)} %get-tuple-element.157), kind=kLoop, calls=%fused_computation.59 | loop fusion | flops 8110080 | bytes 3244032 | tf_op jit(solution)/shard_map/concatenate | solution.py:163
  32.6 8.4 %collective-permute-done.8 = bf16[2,24,4224]{2,1,0:T(8,128)(2,1)} collective-permute-done((bf16[2,24,4224]{2,1,0:T(8,128)(2,1)}, bf16[2,24,4224]{2,1,0:T(8,128)(2,1)}, u32[]{:S(2)}, u32[]{:S(2)}) %collective-permute-start.8) | collective-permute-done | bytes 405536 | tf_op jit(solution)/shard_map/ppermute | solution.py:101
  41.0 1.5 %collective-permute-start.9 = (bf16[2,24,4224]{2,1,0:T(8,128)(2,1)}, bf16[2,24,4224]{2,1,0:T(8,128)(2,1)S(1)}, u32[]{:S(2)}, u32[]{:S(2)}) collective-permute-start(bf16[2,24,4224]{2,1,0:T(8,128)(2,1)} %collective-permute-done.8), channel_id=1, source_target_pairs={{0,2},{1,3},{2,0},{3,1},{4,6},{5,7},{6,4},{7,5},{8,10},{9,11},{10,... | collective-permute-start | bytes 1216520 | tf_op jit(solution)/shard_map/ppermute | solution.py:101
  45.5 1.6 %collective-permute-start.13 = (bf16[24,4224]{1,0:T(8,128)(2,1)S(1)}, bf16[24,4224]{1,0:T(8,128)(2,1)S(1)}, u32[]{:S(2)}, u32[]{:S(2)}) collective-permute-start(bf16[24,4224]{1,0:T(8,128)(2,1)S(1)} %get-tuple-element.134), channel_id=1, source_target_pairs={{0,16},{16,0},{1,17},{17,1},{2,18},{18,2},{3,19},{19,3},{4,20},{20... | collective-permute-start | bytes 608264 | tf_op jit(solution)/shard_map/ppermute | solution.py:101
  47.6 1.7 %copy-done.1 = bf16[1,384,4096]{2,1,0:T(8,128)(2,1)S(1)} copy-done((bf16[1,384,4096]{2,1,0:T(8,128)(2,1)S(1)}, bf16[1,384,4096]{2,1,0:T(8,128)(2,1)}, u32[]{:S(2)}) %copy-start.1) | copy-done | bytes 3145752
  52.4 1.3 multiply_convert_fusion.3
  58.7 1.5 %collective-permute-start.16 = (bf16[2,24,4224]{2,1,0:T(8,128)(2,1)S(1)}, bf16[2,24,4224]{2,1,0:T(8,128)(2,1)S(1)}, u32[]{:S(2)}, u32[]{:S(2)}) collective-permute-start(bf16[2,24,4224]{2,1,0:T(8,128)(2,1)S(1)} %get-tuple-element.137), channel_id=1, source_target_pairs={{0,4},{1,5},{2,6},{3,7},{4,0},{5,1},{6,2},{7,3},{8,12},{9,13},{10,... | collective-permute-start | bytes 1216520 | tf_op jit(solution)/shard_map/ppermute | solution.py:101
  63.3 2.9 %collective-permute-done.18 = bf16[2,96,4224]{2,1,0:T(8,128)(2,1)S(1)} collective-permute-done((bf16[2,96,4224]{2,1,0:T(8,128)(2,1)S(1)}, bf16[2,96,4224]{2,1,0:T(8,128)(2,1)S(1)}, u32[]{:S(2)}, u32[]{:S(2)}) %collective-permute-start.18) | collective-permute-done | bytes 1622048 | tf_op jit(solution)/shard_map/ppermute | solution.py:101
  73.5 1.5 %collective-permute-start.19 = (bf16[24,4224]{1,0:T(8,128)(2,1)S(1)}, bf16[24,4224]{1,0:T(8,128)(2,1)S(1)}, u32[]{:S(2)}, u32[]{:S(2)}) collective-permute-start(bf16[24,4224]{1,0:T(8,128)(2,1)S(1)} %get-tuple-element.126), channel_id=1, source_target_pairs={{0,2},{1,3},{2,0},{3,1},{4,6},{5,7},{6,4},{7,5},{8,10},{9,11},{10,... | collective-permute-start | bytes 608264 | tf_op jit(solution)/shard_map/ppermute | solution.py:101
  75.0 1.5 %collective-permute-start.20 = (bf16[24,4224]{1,0:T(8,128)(2,1)S(1)}, bf16[24,4224]{1,0:T(8,128)(2,1)S(1)}, u32[]{:S(2)}, u32[]{:S(2)}) collective-permute-start(bf16[24,4224]{1,0:T(8,128)(2,1)S(1)} %get-tuple-element.125), channel_id=1, source_target_pairs={{0,16},{16,0},{1,17},{17,1},{2,18},{18,2},{3,19},{19,3},{4,20},{20... | collective-permute-start | bytes 608264 | tf_op jit(solution)/shard_map/ppermute | solution.py:101
  79.3 1.3 multiply_convert_fusion.1
  85.9 2.7 %collective-permute-done.27 = bf16[4,24,4096]{2,1,0:T(8,128)(2,1)S(1)} collective-permute-done((bf16[4,24,4096]{2,1,0:T(8,128)(2,1)S(1)}, bf16[4,24,4096]{2,1,0:T(8,128)(2,1)S(1)}, u32[]{:S(2)}, u32[]{:S(2)}) %collective-permute-start.27) | collective-permute-done | bytes 786464 | tf_op jit(solution)/shard_map/ppermute | solution.py:101
  96.1 1.5 %collective-permute-done.28 = bf16[4,24,4096]{2,1,0:T(8,128)(2,1)S(1)} collective-permute-done((bf16[4,24,4096]{2,1,0:T(8,128)(2,1)S(1)}, bf16[4,24,4096]{2,1,0:T(8,128)(2,1)S(1)}, u32[]{:S(2)}, u32[]{:S(2)}) %collective-permute-start.28) | collective-permute-done | bytes 786464 | tf_op jit(solution)/shard_map/ppermute | solution.py:101
  100.8 1.5 %collective-permute-start.30 = (bf16[24,2048]{1,0:T(8,128)(2,1)S(1)}, bf16[24,2048]{1,0:T(8,128)(2,1)S(1)}, u32[]{:S(2)}, u32[]{:S(2)}) collective-permute-start(bf16[24,2048]{1,0:T(8,128)(2,1)S(1)} %get-tuple-element.150), channel_id=1, source_target_pairs={{0,16},{16,0},{1,17},{17,1},{2,18},{18,2},{3,19},{19,3},{4,20},{20... | collective-permute-start | bytes 294920 | tf_op jit(solution)/shard_map/ppermute | solution.py:101
  102.4 2.0 %collective-permute-done.31 = bf16[24,2048]{1,0:T(8,128)(2,1)S(1)} collective-permute-done((bf16[24,2048]{1,0:T(8,128)(2,1)S(1)}, bf16[24,2048]{1,0:T(8,128)(2,1)S(1)}, u32[]{:S(2)}, u32[]{:S(2)}) %collective-permute-start.31) | collective-permute-done | bytes 98336 | tf_op jit(solution)/shard_map/ppermute | solution.py:101
  104.4 3.0 %collective-permute-done.30 = bf16[24,2048]{1,0:T(8,128)(2,1)S(1)} collective-permute-done((bf16[24,2048]{1,0:T(8,128)(2,1)S(1)}, bf16[24,2048]{1,0:T(8,128)(2,1)S(1)}, u32[]{:S(2)}, u32[]{:S(2)}) %collective-permute-start.30) | collective-permute-done | bytes 98336 | tf_op jit(solution)/shard_map/ppermute | solution.py:101
  107.8 4.0 %fusion.11 = bf16[1,384,4096]{2,1,0:T(8,128)(2,1)} fusion(bf16[192,4096]{1,0:T(8,128)(2,1)S(1)} %slice.535, bf16[192,4096]{1,0:T(8,128)(2,1)S(1)} %pad_maximum_fusion.4, bf16[192,4096]{1,0:T(8,128)(2,1)S(1)} %slice.528, bf16[192,4096]{1,0:T(8,128)(2,1)S(1)} %pad_maximum_fusion.6, bf16[192,384]{1,0:T(8,128)(2,1)S(1)} %get-tuple-element.117, ...), kind=kOutput, calls=%fused_computation.16 | convolution fusion | flops 2445017088 | bytes 10027008 | tf_op jit(solution)/shard_map/rf,rd->fd/dot_general | solution.py:266
  111.9 2.0 %collective-permute-done.32 = bf16[24,4096]{1,0:T(8,128)(2,1)S(1)} collective-permute-done((bf16[24,4096]{1,0:T(8,128)(2,1)S(1)}, bf16[24,4096]{1,0:T(8,128)(2,1)S(1)}, u32[]{:S(2)}, u32[]{:S(2)}) %collective-permute-start.32) | collective-permute-done | bytes 196640 | tf_op jit(solution)/shard_map/ppermute | solution.py:101
  115.7 4.0 %fusion.12 = bf16[1,384,4096]{2,1,0:T(8,128)(2,1)} fusion(bf16[192,4096]{1,0:T(8,128)(2,1)S(1)} %slice.535, bf16[192,4096]{1,0:T(8,128)(2,1)S(1)} %pad_maximum_fusion.4, bf16[192,4096]{1,0:T(8,128)(2,1)S(1)} %slice.528, bf16[192,4096]{1,0:T(8,128)(2,1)S(1)} %pad_maximum_fusion.6, bf16[192,384]{1,0:T(8,128)(2,1)S(1)} %get-tuple-element.118, ...), kind=kOutput, calls=%fused_computation.17 | convolution fusion | flops 2445017088 | bytes 10027008 | tf_op jit(solution)/shard_map/rf,rd->fd/dot_general | solution.py:266
  121.2 4.2 %collective-permute-start.40 = (bf16[24,4096]{1,0:T(8,128)(2,1)S(1)}, bf16[24,4096]{1,0:T(8,128)(2,1)S(1)}, u32[]{:S(2)}, u32[]{:S(2)}) collective-permute-start(bf16[24,4096]{1,0:T(8,128)(2,1)S(1)} %add_convert_fusion.1), channel_id=1, source_target_pairs={{0,8},{1,9},{2,10},{3,11},{4,12},{5,13},{6,14},{7,15},{8,0},{9,1},... | collective-permute-start | bytes 589832 | tf_op jit(solution)/shard_map/ppermute | solution.py:101
  125.7 1.6 %collective-permute-start.38 = (bf16[24,4096]{1,0:T(8,128)(2,1)S(1)}, bf16[24,4096]{1,0:T(8,128)(2,1)S(1)}, u32[]{:S(2)}, u32[]{:S(2)}) collective-permute-start(bf16[24,4096]{1,0:T(8,128)(2,1)S(1)} %pad_maximum_fusion.24), channel_id=1, source_target_pairs={{0,16},{16,0},{1,17},{17,1},{2,18},{18,2},{3,19},{19,3},{4,20},{20... | collective-permute-start | bytes 589832 | tf_op jit(solution)/shard_map/ppermute | solution.py:101
  127.3 1.3 collective-permute-start.37
  128.6 4.0 %fusion.13 = bf16[1,384,4096]{2,1,0:T(8,128)(2,1)} fusion(bf16[192,4096]{1,0:T(8,128)(2,1)S(1)} %slice.533, bf16[192,4096]{1,0:T(8,128)(2,1)S(1)} %pad_maximum_fusion.5, bf16[192,4096]{1,0:T(8,128)(2,1)S(1)} %slice.526, bf16[192,4096]{1,0:T(8,128)(2,1)S(1)} %pad_maximum_fusion.7, bf16[192,384]{1,0:T(8,128)(2,1)S(1)} %get-tuple-element.116, ...), kind=kOutput, calls=%fused_computation.18 | convolution fusion | flops 2445017088 | bytes 10027008 | tf_op jit(solution)/shard_map/rf,rd->fd/dot_general | solution.py:266
  (189 shorter events, 54.4 us)
Async XLA Ops:
  4.1 12.5 %collective-permute-start.1 = (bf16[2,24,4224]{2,1,0:T(8,128)(2,1)}, bf16[2,24,4224]{2,1,0:T(8,128)(2,1)S(1)}, u32[]{:S(2)}, u32[]{:S(2)}) collective-permute-start(bf16[2,24,4224]{2,1,0:T(8,128)(2,1)} %pad_maximum_fusion.12), channel_id=1, source_target_pairs={{0,2},{1,3},{2,0},{3,1},{4,6},{5,7},{6,4},{7,5},{8,10},{9,11},{10,... | collective-permute-start | bytes 1216520 | tf_op jit(solution)/shard_map/ppermute | solution.py:101
  7.0 11.0 %collective-permute-start.2 = (bf16[2,24,4224]{2,1,0:T(8,128)(2,1)}, bf16[2,24,4224]{2,1,0:T(8,128)(2,1)S(1)}, u32[]{:S(2)}, u32[]{:S(2)}) collective-permute-start(bf16[2,24,4224]{2,1,0:T(8,128)(2,1)} %pad_maximum_fusion.12), channel_id=1, source_target_pairs={{0,16},{16,0},{1,17},{17,1},{2,18},{18,2},{3,19},{19,3},{4,20},{20... | collective-permute-start | bytes 1216520 | tf_op jit(solution)/shard_map/ppermute | solution.py:101
  8.5 15.6 %collective-permute-start = (bf16[2,24,4224]{2,1,0:T(8,128)(2,1)}, bf16[2,24,4224]{2,1,0:T(8,128)(2,1)}, u32[]{:S(2)}, u32[]{:S(2)}) collective-permute-start(bf16[2,24,4224]{2,1,0:T(8,128)(2,1)} %pad_maximum_fusion.12), channel_id=1, source_target_pairs={{0,4},{1,5},{2,6},{3,7},{4,0},{5,1},{6,2},{7,3},{8,12},{9,13},{10,... | collective-permute-start | bytes 1216520 | tf_op jit(solution)/shard_map/ppermute | solution.py:101
  18.8 6.1 %collective-permute-start.3 = (bf16[24,4224]{1,0:T(8,128)(2,1)}, bf16[24,4224]{1,0:T(8,128)(2,1)}, u32[]{:S(2)}, u32[]{:S(2)}) collective-permute-start(bf16[24,4224]{1,0:T(8,128)(2,1)} %slice_bitcast_fusion.27), channel_id=1, source_target_pairs={{0,2},{1,3},{2,0},{3,1},{4,6},{5,7},{6,4},{7,5},{8,10},{9,11},{10,... | collective-permute-start | bytes 608264 | tf_op jit(solution)/shard_map/ppermute | solution.py:101
  19.9 6.1 %collective-permute-start.4 = (bf16[24,4224]{1,0:T(8,128)(2,1)}, bf16[24,4224]{1,0:T(8,128)(2,1)}, u32[]{:S(2)}, u32[]{:S(2)}) collective-permute-start(bf16[24,4224]{1,0:T(8,128)(2,1)} %slice_bitcast_fusion.26), channel_id=1, source_target_pairs={{0,16},{16,0},{1,17},{17,1},{2,18},{18,2},{3,19},{19,3},{4,20},{20... | collective-permute-start | bytes 608264 | tf_op jit(solution)/shard_map/ppermute | solution.py:101
  21.6 19.4 %collective-permute-start.8 = (bf16[2,24,4224]{2,1,0:T(8,128)(2,1)}, bf16[2,24,4224]{2,1,0:T(8,128)(2,1)}, u32[]{:S(2)}, u32[]{:S(2)}) collective-permute-start(bf16[2,24,4224]{2,1,0:T(8,128)(2,1)} %pad_maximum_fusion.12), channel_id=1, source_target_pairs={{0,8},{1,9},{2,10},{3,11},{4,12},{5,13},{6,14},{7,15},{8,0},{9,1},... | collective-permute-start | bytes 1216520 | tf_op jit(solution)/shard_map/ppermute | solution.py:101
  26.0 15.0 %collective-permute-start.5 = (bf16[2,24,4224]{2,1,0:T(8,128)(2,1)}, bf16[2,24,4224]{2,1,0:T(8,128)(2,1)S(1)}, u32[]{:S(2)}, u32[]{:S(2)}) collective-permute-start(bf16[2,24,4224]{2,1,0:T(8,128)(2,1)} %collective-permute-done), channel_id=1, source_target_pairs={{0,2},{1,3},{2,0},{3,1},{4,6},{5,7},{6,4},{7,5},{8,10},{9,11},{10,... | collective-permute-start | bytes 1216520 | tf_op jit(solution)/shard_map/ppermute | solution.py:101
  27.6 13.4 %collective-permute-start.6 = (bf16[2,24,4224]{2,1,0:T(8,128)(2,1)}, bf16[2,24,4224]{2,1,0:T(8,128)(2,1)S(1)}, u32[]{:S(2)}, u32[]{:S(2)}) collective-permute-start(bf16[2,24,4224]{2,1,0:T(8,128)(2,1)} %collective-permute-done), channel_id=1, source_target_pairs={{0,16},{16,0},{1,17},{17,1},{2,18},{18,2},{3,19},{19,3},{4,20},{20... | collective-permute-start | bytes 1216520 | tf_op jit(solution)/shard_map/ppermute | solution.py:101
  30.5 10.5 %collective-permute-start.7 = (bf16[2,96,4224]{2,1,0:T(8,128)(2,1)S(1)}, bf16[2,96,4224]{2,1,0:T(8,128)(2,1)S(1)}, u32[]{:S(2)}, u32[]{:S(2)}) collective-permute-start(bf16[2,96,4224]{2,1,0:T(8,128)(2,1)S(1)} %pad_maximum_fusion.1), channel_id=1, source_target_pairs={{0,1},{1,0},{2,3},{3,2},{4,5},{5,4},{6,7},{7,6},{8,9},{9,8},{10,11... | collective-permute-start | bytes 4866056 | tf_op jit(solution)/shard_map/ppermute | solution.py:101
  41.0 16.0 %collective-permute-start.9 = (bf16[2,24,4224]{2,1,0:T(8,128)(2,1)}, bf16[2,24,4224]{2,1,0:T(8,128)(2,1)S(1)}, u32[]{:S(2)}, u32[]{:S(2)}) collective-permute-start(bf16[2,24,4224]{2,1,0:T(8,128)(2,1)} %collective-permute-done.8), channel_id=1, source_target_pairs={{0,2},{1,3},{2,0},{3,1},{4,6},{5,7},{6,4},{7,5},{8,10},{9,11},{10,... | collective-permute-start | bytes 1216520 | tf_op jit(solution)/shard_map/ppermute | solution.py:101
  42.5 14.5 %collective-permute-start.10 = (bf16[2,24,4224]{2,1,0:T(8,128)(2,1)}, bf16[2,24,4224]{2,1,0:T(8,128)(2,1)S(1)}, u32[]{:S(2)}, u32[]{:S(2)}) collective-permute-start(bf16[2,24,4224]{2,1,0:T(8,128)(2,1)} %collective-permute-done.8), channel_id=1, source_target_pairs={{0,16},{16,0},{1,17},{17,1},{2,18},{18,2},{3,19},{19,3},{4,20},{20... | collective-permute-start | bytes 1216520 | tf_op jit(solution)/shard_map/ppermute | solution.py:101
  43.0 14.0 %collective-permute-start.11 = (bf16[2,24,4224]{2,1,0:T(8,128)(2,1)}, bf16[2,24,4224]{2,1,0:T(8,128)(2,1)S(1)}, u32[]{:S(2)}, u32[]{:S(2)}) collective-permute-start(bf16[2,24,4224]{2,1,0:T(8,128)(2,1)} %collective-permute-done.8), channel_id=1, source_target_pairs={{0,4},{1,5},{2,6},{3,7},{4,0},{5,1},{6,2},{7,3},{8,12},{9,13},{10,... | collective-permute-start | bytes 1216520 | tf_op jit(solution)/shard_map/ppermute | solution.py:101
  44.8 11.1 %collective-permute-start.12 = (bf16[24,4224]{1,0:T(8,128)(2,1)S(1)}, bf16[24,4224]{1,0:T(8,128)(2,1)S(1)}, u32[]{:S(2)}, u32[]{:S(2)}) collective-permute-start(bf16[24,4224]{1,0:T(8,128)(2,1)S(1)} %get-tuple-element.132), channel_id=1, source_target_pairs={{0,2},{1,3},{2,0},{3,1},{4,6},{5,7},{6,4},{7,5},{8,10},{9,11},{10,... | collective-permute-start | bytes 608264 | tf_op jit(solution)/shard_map/ppermute | solution.py:101
  45.5 11.5 %collective-permute-start.13 = (bf16[24,4224]{1,0:T(8,128)(2,1)S(1)}, bf16[24,4224]{1,0:T(8,128)(2,1)S(1)}, u32[]{:S(2)}, u32[]{:S(2)}) collective-permute-start(bf16[24,4224]{1,0:T(8,128)(2,1)S(1)} %get-tuple-element.134), channel_id=1, source_target_pairs={{0,16},{16,0},{1,17},{17,1},{2,18},{18,2},{3,19},{19,3},{4,20},{20... | collective-permute-start | bytes 608264 | tf_op jit(solution)/shard_map/ppermute | solution.py:101
  57.3 15.6 %collective-permute-start.14 = (bf16[2,24,4224]{2,1,0:T(8,128)(2,1)S(1)}, bf16[2,24,4224]{2,1,0:T(8,128)(2,1)S(1)}, u32[]{:S(2)}, u32[]{:S(2)}) collective-permute-start(bf16[2,24,4224]{2,1,0:T(8,128)(2,1)S(1)} %get-tuple-element.138), channel_id=1, source_target_pairs={{0,2},{1,3},{2,0},{3,1},{4,6},{5,7},{6,4},{7,5},{8,10},{9,11},{10,... | collective-permute-start | bytes 1216520 | tf_op jit(solution)/shard_map/ppermute | solution.py:101
  57.9 14.9 %collective-permute-start.15 = (bf16[2,24,4224]{2,1,0:T(8,128)(2,1)S(1)}, bf16[2,24,4224]{2,1,0:T(8,128)(2,1)S(1)}, u32[]{:S(2)}, u32[]{:S(2)}) collective-permute-start(bf16[2,24,4224]{2,1,0:T(8,128)(2,1)S(1)} %get-tuple-element.139), channel_id=1, source_target_pairs={{0,16},{16,0},{1,17},{17,1},{2,18},{18,2},{3,19},{19,3},{4,20},{20... | collective-permute-start | bytes 1216520 | tf_op jit(solution)/shard_map/ppermute | solution.py:101
  58.7 14.2 %collective-permute-start.16 = (bf16[2,24,4224]{2,1,0:T(8,128)(2,1)S(1)}, bf16[2,24,4224]{2,1,0:T(8,128)(2,1)S(1)}, u32[]{:S(2)}, u32[]{:S(2)}) collective-permute-start(bf16[2,24,4224]{2,1,0:T(8,128)(2,1)S(1)} %get-tuple-element.137), channel_id=1, source_target_pairs={{0,4},{1,5},{2,6},{3,7},{4,0},{5,1},{6,2},{7,3},{8,12},{9,13},{10,... | collective-permute-start | bytes 1216520 | tf_op jit(solution)/shard_map/ppermute | solution.py:101
  60.3 12.6 %collective-permute-start.17 = (bf16[2,96,4224]{2,1,0:T(8,128)(2,1)S(1)}, bf16[2,96,4224]{2,1,0:T(8,128)(2,1)S(1)}, u32[]{:S(2)}, u32[]{:S(2)}) collective-permute-start(bf16[2,96,4224]{2,1,0:T(8,128)(2,1)S(1)} %constant_dynamic-update-slice_fusion), channel_id=1, source_target_pairs={{0,1},{1,0},{2,3},{3,2},{4,5},{5,4},{6,7},{7,6},{8,9},{9,8},{10,11... | collective-permute-start | bytes 4866056 | tf_op jit(solution)/shard_map/ppermute | solution.py:101
  66.2 16.9 %collective-permute-start.21 = (bf16[4,24,4096]{2,1,0:T(8,128)(2,1)S(1)}, bf16[4,24,4096]{2,1,0:T(8,128)(2,1)S(1)}, u32[]{:S(2)}, u32[]{:S(2)}) collective-permute-start(bf16[4,24,4096]{2,1,0:T(8,128)(2,1)S(1)} %slice_bitcast_fusion.15), channel_id=1, source_target_pairs={{0,1},{1,0},{2,3},{3,2},{4,5},{5,4},{6,7},{7,6},{8,9},{9,8},{10,11... | collective-permute-start | bytes 2359304 | tf_op jit(solution)/shard_map/ppermute | solution.py:101
  73.5 9.6 %collective-permute-start.19 = (bf16[24,4224]{1,0:T(8,128)(2,1)S(1)}, bf16[24,4224]{1,0:T(8,128)(2,1)S(1)}, u32[]{:S(2)}, u32[]{:S(2)}) collective-permute-start(bf16[24,4224]{1,0:T(8,128)(2,1)S(1)} %get-tuple-element.126), channel_id=1, source_target_pairs={{0,2},{1,3},{2,0},{3,1},{4,6},{5,7},{6,4},{7,5},{8,10},{9,11},{10,... | collective-permute-start | bytes 608264 | tf_op jit(solution)/shard_map/ppermute | solution.py:101
  75.0 8.1 %collective-permute-start.20 = (bf16[24,4224]{1,0:T(8,128)(2,1)S(1)}, bf16[24,4224]{1,0:T(8,128)(2,1)S(1)}, u32[]{:S(2)}, u32[]{:S(2)}) collective-permute-start(bf16[24,4224]{1,0:T(8,128)(2,1)S(1)} %get-tuple-element.125), channel_id=1, source_target_pairs={{0,16},{16,0},{1,17},{17,1},{2,18},{18,2},{3,19},{19,3},{4,20},{20... | collective-permute-start | bytes 608264 | tf_op jit(solution)/shard_map/ppermute | solution.py:101
  76.5 6.5 %collective-permute-start.22 = (bf16[4,24,4096]{2,1,0:T(8,128)(2,1)S(1)}, bf16[4,24,4096]{2,1,0:T(8,128)(2,1)S(1)}, u32[]{:S(2)}, u32[]{:S(2)}) collective-permute-start(bf16[4,24,4096]{2,1,0:T(8,128)(2,1)S(1)} %slice_bitcast_fusion.14), channel_id=1, source_target_pairs={{0,1},{1,0},{2,3},{3,2},{4,5},{5,4},{6,7},{7,6},{8,9},{9,8},{10,11... | collective-permute-start | bytes 2359304 | tf_op jit(solution)/shard_map/ppermute | solution.py:101
  84.5 10.6 %collective-permute-start.24 = (bf16[3,24,2048]{2,1,0:T(8,128)(2,1)S(1)}, bf16[3,24,2048]{2,1,0:T(8,128)(2,1)S(1)}, u32[]{:S(2)}, u32[]{:S(2)}) collective-permute-start(bf16[3,24,2048]{2,1,0:T(8,128)(2,1)S(1)} %pad_maximum_fusion.14), channel_id=1, source_target_pairs={{0,2},{1,3},{2,0},{3,1},{4,6},{5,7},{6,4},{7,5},{8,10},{9,11},{10,... | collective-permute-start | bytes 884744 | tf_op jit(solution)/shard_map/ppermute | solution.py:101
  85.3 9.8 %collective-permute-start.25 = (bf16[3,24,2048]{2,1,0:T(8,128)(2,1)S(1)}, bf16[3,24,2048]{2,1,0:T(8,128)(2,1)S(1)}, u32[]{:S(2)}, u32[]{:S(2)}) collective-permute-start(bf16[3,24,2048]{2,1,0:T(8,128)(2,1)S(1)} %pad_maximum_fusion.15), channel_id=1, source_target_pairs={{0,16},{16,0},{1,17},{17,1},{2,18},{18,2},{3,19},{19,3},{4,20},{20... | collective-permute-start | bytes 884744 | tf_op jit(solution)/shard_map/ppermute | solution.py:101
  95.7 24.2 %collective-permute-start.26 = (bf16[24,4096]{1,0:T(8,128)(2,1)S(1)}, bf16[24,4096]{1,0:T(8,128)(2,1)S(1)}, u32[]{:S(2)}, u32[]{:S(2)}) collective-permute-start(bf16[24,4096]{1,0:T(8,128)(2,1)S(1)} %pad_maximum_fusion.16), channel_id=1, source_target_pairs={{0,4},{1,5},{2,6},{3,7},{4,0},{5,1},{6,2},{7,3},{8,12},{9,13},{10,... | collective-permute-start | bytes 589832 | tf_op jit(solution)/shard_map/ppermute | solution.py:101
  98.1 13.8 %collective-permute-start.29 = (bf16[2,24,2048]{2,1,0:T(8,128)(2,1)S(1)}, bf16[2,24,2048]{2,1,0:T(8,128)(2,1)S(1)}, u32[]{:S(2)}, u32[]{:S(2)}) collective-permute-start(bf16[2,24,2048]{2,1,0:T(8,128)(2,1)S(1)} %pad_maximum_fusion.17), channel_id=1, source_target_pairs={{0,16},{16,0},{1,17},{17,1},{2,18},{18,2},{3,19},{19,3},{4,20},{20... | collective-permute-start | bytes 589832 | tf_op jit(solution)/shard_map/ppermute | solution.py:101
  99.9 12.0 %collective-permute-start.34 = (bf16[2,24,2048]{2,1,0:T(8,128)(2,1)S(1)}, bf16[2,24,2048]{2,1,0:T(8,128)(2,1)S(1)}, u32[]{:S(2)}, u32[]{:S(2)}) collective-permute-start(bf16[2,24,2048]{2,1,0:T(8,128)(2,1)S(1)} %pad_maximum_fusion.20), channel_id=1, source_target_pairs={{0,2},{1,3},{2,0},{3,1},{4,6},{5,7},{6,4},{7,5},{8,10},{9,11},{10,... | collective-permute-start | bytes 589832 | tf_op jit(solution)/shard_map/ppermute | solution.py:101
  100.8 6.6 %collective-permute-start.30 = (bf16[24,2048]{1,0:T(8,128)(2,1)S(1)}, bf16[24,2048]{1,0:T(8,128)(2,1)S(1)}, u32[]{:S(2)}, u32[]{:S(2)}) collective-permute-start(bf16[24,2048]{1,0:T(8,128)(2,1)S(1)} %get-tuple-element.150), channel_id=1, source_target_pairs={{0,16},{16,0},{1,17},{17,1},{2,18},{18,2},{3,19},{19,3},{4,20},{20... | collective-permute-start | bytes 294920 | tf_op jit(solution)/shard_map/ppermute | solution.py:101
  107.5 6.4 %collective-permute-start.32 = (bf16[24,4096]{1,0:T(8,128)(2,1)S(1)}, bf16[24,4096]{1,0:T(8,128)(2,1)S(1)}, u32[]{:S(2)}, u32[]{:S(2)}) collective-permute-start(bf16[24,4096]{1,0:T(8,128)(2,1)S(1)} %pad_maximum_fusion.18), channel_id=1, source_target_pairs={{0,4},{1,5},{2,6},{3,7},{4,0},{5,1},{6,2},{7,3},{8,12},{9,13},{10,... | collective-permute-start | bytes 589832 | tf_op jit(solution)/shard_map/ppermute | solution.py:101
  121.2 11.4 %collective-permute-start.40 = (bf16[24,4096]{1,0:T(8,128)(2,1)S(1)}, bf16[24,4096]{1,0:T(8,128)(2,1)S(1)}, u32[]{:S(2)}, u32[]{:S(2)}) collective-permute-start(bf16[24,4096]{1,0:T(8,128)(2,1)S(1)} %add_convert_fusion.1), channel_id=1, source_target_pairs={{0,8},{1,9},{2,10},{3,11},{4,12},{5,13},{6,14},{7,15},{8,0},{9,1},... | collective-permute-start | bytes 589832 | tf_op jit(solution)/shard_map/ppermute | solution.py:101
  125.6 7.1 %collective-permute-start.39 = (bf16[24,4096]{1,0:T(8,128)(2,1)S(1)}, bf16[24,4096]{1,0:T(8,128)(2,1)S(1)}, u32[]{:S(2)}, u32[]{:S(2)}) collective-permute-start(bf16[24,4096]{1,0:T(8,128)(2,1)S(1)} %pad_maximum_fusion.25), channel_id=1, source_target_pairs={{0,4},{1,5},{2,6},{3,7},{4,0},{5,1},{6,2},{7,3},{8,12},{9,13},{10,... | collective-permute-start | bytes 589832 | tf_op jit(solution)/shard_map/ppermute | solution.py:101
  125.7 7.0 %collective-permute-start.38 = (bf16[24,4096]{1,0:T(8,128)(2,1)S(1)}, bf16[24,4096]{1,0:T(8,128)(2,1)S(1)}, u32[]{:S(2)}, u32[]{:S(2)}) collective-permute-start(bf16[24,4096]{1,0:T(8,128)(2,1)S(1)} %pad_maximum_fusion.24), channel_id=1, source_target_pairs={{0,16},{16,0},{1,17},{17,1},{2,18},{18,2},{3,19},{19,3},{4,20},{20... | collective-permute-start | bytes 589832 | tf_op jit(solution)/shard_map/ppermute | solution.py:101
  (18 other events, 164.0 us)

commit v4 on v3

--- a/solution.py
+++ b/solution.py
@@ -185,16 +185,21 @@
 
     scales = gate_of_expert(routes, gates, experts)
     scales = jnp.pad(scales, ((0, 0), (0, LANES - experts)))
-    mine = jnp.stack([jnp.pad(tokens, ((0, 0), (0, LANES))), jnp.concatenate([out_grad, scales], axis=1)])
+    tail = ((0, 0), (0, LANES))
+    grad_rows = jnp.concatenate([out_grad, scales], axis=1)
+    mine = jnp.stack([jnp.pad(tokens, tail), grad_rows])
     from_x, from_y, from_z = firsts(mine)
-    distant = over_far_z(mine)
+    distant_t = over_far_z(tokens)
+    mine, distant_t = together((mine, distant_t))
+    distant_g = over_far_z(mine[1])
     from_x, from_y = together((from_x, from_y))
     g_far, t_far = over_x(from_y[1]), over_y(from_x[0])
     from_z, g_far, t_far = together((from_z, g_far, t_far))
     z_x, z_y = over_x(from_z), over_y(from_z)
     near = near_of(mine, from_x, from_y, from_z)
     near_other = over_core(near)
-    z_x, z_y, near_other, distant = together((z_x, z_y, near_other, distant))
+    z_x, z_y, near_other, distant_t, distant_g = together((z_x, z_y, near_other, distant_t, distant_g))
+    distant = jnp.stack([jnp.pad(distant_t, tail), distant_g])
     first2 = firsts(distant)
     third = over_x(z_y[1]), over_y(z_x[0])
     part_near, kept_near = expert_rows(near, near_other)

time: 134 us -> 127 us (0.948)
  other arithmetic: 10.3 us -> 6.11 us
  waiting for transfers between devices: 35 us -> 31.5 us
    ppermute x41 -> x42, waiting for transfers between devices: 35 us -> 31.5 us  [swapped(): return lax.ppermute(x, axis, [(i, i ^ bits) for i in range(count)])]
    another operation x3, other arithmetic: 2.15 us -> 0.3 us  [dense_plan(): jnp.stack([rows_of(t_far, z_y[0], z_x[0], third[1]), rows_of(g_far, z_y[1...]
    unnamed x31 -> x27, local copies, waits for them, and re-layouts: 6.41 us -> 4.92 us
    ppermute x41 -> x42, starting transfers between devices: 41.8 us -> 41.8 us  [swapped(): return lax.ppermute(x, axis, [(i, i ^ bits) for i in range(count)])]
  transfers between devices with their start and end apart: 41 -> 42, of which waited for: 15 -> 17; matrix products, arithmetic and copies ran while one was open for 36% -> 37% of each run, Pallas kernels for 0% -> 0%
where the time goes in v4:
time: 127 us
  starting transfers between devices  41.8 us (33%)
  matrix products  35.1 us (28%)
  waiting for transfers between devices  31.5 us (25%)
  local copies, waits for them, and re-layouts  10.9 us (9%)
  other arithmetic  6.11 us (5%)
  between operations  1.57 us (1%)
    ppermute x42, starting transfers between devices, swapped(): return lax.ppermute(x, axis, [(i, i ^ bits) for i in range(count)])  41.8 us
    ppermute x42, waiting for transfers between devices, swapped(): return lax.ppermute(x, axis, [(i, i ^ bits) for i in range(count)])  31.5 us
    dot_general x3, matrix products, weight_grad(): jnp.einsum('rf,rd->fd', rows_of(*(held[at] for held in kept)), rows_of(*(...  12.1 us
    dot_general x4, matrix products, expert_rows(): jnp.einsum('rd,fd->rf', x_rows, up_w, preferred_element_type=jnp.float32)  5.08 us
    unnamed x27, local copies, waits for them, and re-layouts  4.92 us
    dot_general x4, matrix products, expert_rows(): jnp.einsum('rd,fd->rf', g_rows, down_w, preferred_element_type=jnp.float32)  4.72 us
    dot_general x4, matrix products, expert_rows(): jnp.einsum('rd,fd->rf', x_rows, gate_w, preferred_element_type=jnp.float32)  4.71 us
    dot_general x4, matrix products, expert_rows(): jnp.einsum('rf,fd->rd', d_up_act, up_w, preferred_element_type=jnp.float32)  4.48 us
  transfers between devices with their start and end apart: 42, of which 17 were waited for; matrix products, arithmetic and copies ran while one was open for 37% of the time, Pallas kernels for 0%

profile of v4, /device:TPU:0, one launch (start us, length us, event | category | flops | bytes accessed | tf_op | source)
XLA Modules:
  0.0 127.0 jit_solution(16779735143247600840)
XLA Ops:
  0.6 4.1 %collective-permute-start.7 = (bf16[24,4096]{1,0:T(8,128)(2,1)}, bf16[24,4096]{1,0:T(8,128)(2,1)}, u32[]{:S(2)}, u32[]{:S(2)}) collective-permute-start(bf16[24,4096]{1,0:T(8,128)(2,1)} %param.7), channel_id=1, source_target_pairs={{0,8},{1,9},{2,10},{3,11},{4,12},{5,13},{6,14},{7,15},{8,0},{9,1},... | collective-permute-start | bytes 589832 | tf_op jit(solution)/shard_map/ppermute | solution.py:101
  6.7 1.6 %collective-permute-start = (bf16[2,24,4224]{2,1,0:T(8,128)(2,1)S(1)}, bf16[2,24,4224]{2,1,0:T(8,128)(2,1)}, u32[]{:S(2)}, u32[]{:S(2)}) collective-permute-start(bf16[2,24,4224]{2,1,0:T(8,128)(2,1)S(1)} %pad_maximum_fusion.12), channel_id=1, source_target_pairs={{0,4},{1,5},{2,6},{3,7},{4,0},{5,1},{6,2},{7,3},{8,12},{9,13},{10,... | collective-permute-start | bytes 1216520 | tf_op jit(solution)/shard_map/ppermute | solution.py:101
  8.3 1.5 %collective-permute-start.1 = (bf16[2,24,4224]{2,1,0:T(8,128)(2,1)S(1)}, bf16[2,24,4224]{2,1,0:T(8,128)(2,1)}, u32[]{:S(2)}, u32[]{:S(2)}) collective-permute-start(bf16[2,24,4224]{2,1,0:T(8,128)(2,1)S(1)} %pad_maximum_fusion.12), channel_id=1, source_target_pairs={{0,2},{1,3},{2,0},{3,1},{4,6},{5,7},{6,4},{7,5},{8,10},{9,11},{10,... | collective-permute-start | bytes 1216520 | tf_op jit(solution)/shard_map/ppermute | solution.py:101
  9.8 1.5 %collective-permute-start.2 = (bf16[2,24,4224]{2,1,0:T(8,128)(2,1)S(1)}, bf16[2,24,4224]{2,1,0:T(8,128)(2,1)}, u32[]{:S(2)}, u32[]{:S(2)}) collective-permute-start(bf16[2,24,4224]{2,1,0:T(8,128)(2,1)S(1)} %pad_maximum_fusion.12), channel_id=1, source_target_pairs={{0,16},{16,0},{1,17},{17,1},{2,18},{18,2},{3,19},{19,3},{4,20},{20... | collective-permute-start | bytes 1216520 | tf_op jit(solution)/shard_map/ppermute | solution.py:101
  11.3 3.0 %collective-permute-done.7 = bf16[24,4096]{1,0:T(8,128)(2,1)} collective-permute-done((bf16[24,4096]{1,0:T(8,128)(2,1)}, bf16[24,4096]{1,0:T(8,128)(2,1)}, u32[]{:S(2)}, u32[]{:S(2)}) %collective-permute-start.7) | collective-permute-done | bytes 196640 | tf_op jit(solution)/shard_map/ppermute | solution.py:101
  14.4 4.5 %collective-permute-done.1 = bf16[2,24,4224]{2,1,0:T(8,128)(2,1)} collective-permute-done((bf16[2,24,4224]{2,1,0:T(8,128)(2,1)S(1)}, bf16[2,24,4224]{2,1,0:T(8,128)(2,1)}, u32[]{:S(2)}, u32[]{:S(2)}) %collective-permute-start.1) | collective-permute-done | bytes 405536 | tf_op jit(solution)/shard_map/ppermute | solution.py:101
  22.7 1.6 %collective-permute-start.4 = (bf16[24,4224]{1,0:T(8,128)(2,1)S(1)}, bf16[24,4224]{1,0:T(8,128)(2,1)S(1)}, u32[]{:S(2)}, u32[]{:S(2)}) collective-permute-start(bf16[24,4224]{1,0:T(8,128)(2,1)S(1)} %slice_bitcast_fusion.27), channel_id=1, source_target_pairs={{0,16},{16,0},{1,17},{17,1},{2,18},{18,2},{3,19},{19,3},{4,20},{20... | collective-permute-start | bytes 608264 | tf_op jit(solution)/shard_map/ppermute | solution.py:101
  26.9 1.5 %collective-permute-done.4 = bf16[24,4224]{1,0:T(8,128)(2,1)S(1)} collective-permute-done((bf16[24,4224]{1,0:T(8,128)(2,1)S(1)}, bf16[24,4224]{1,0:T(8,128)(2,1)S(1)}, u32[]{:S(2)}, u32[]{:S(2)}) %collective-permute-start.4) | collective-permute-done | bytes 202784 | tf_op jit(solution)/shard_map/ppermute | solution.py:101
  28.5 1.5 %collective-permute-start.5 = (bf16[2,24,4224]{2,1,0:T(8,128)(2,1)}, bf16[2,24,4224]{2,1,0:T(8,128)(2,1)S(1)}, u32[]{:S(2)}, u32[]{:S(2)}) collective-permute-start(bf16[2,24,4224]{2,1,0:T(8,128)(2,1)} %collective-permute-done), channel_id=1, source_target_pairs={{0,2},{1,3},{2,0},{3,1},{4,6},{5,7},{6,4},{7,5},{8,10},{9,11},{10,... | collective-permute-start | bytes 1216520 | tf_op jit(solution)/shard_map/ppermute | solution.py:101
  30.0 1.5 %collective-permute-start.6 = (bf16[2,24,4224]{2,1,0:T(8,128)(2,1)}, bf16[2,24,4224]{2,1,0:T(8,128)(2,1)S(1)}, u32[]{:S(2)}, u32[]{:S(2)}) collective-permute-start(bf16[2,24,4224]{2,1,0:T(8,128)(2,1)} %collective-permute-done), channel_id=1, source_target_pairs={{0,16},{16,0},{1,17},{17,1},{2,18},{18,2},{3,19},{19,3},{4,20},{20... | collective-permute-start | bytes 1216520 | tf_op jit(solution)/shard_map/ppermute | solution.py:101
  32.8 4.1 %collective-permute-done.5 = bf16[2,24,4224]{2,1,0:T(8,128)(2,1)S(1)} collective-permute-done((bf16[2,24,4224]{2,1,0:T(8,128)(2,1)}, bf16[2,24,4224]{2,1,0:T(8,128)(2,1)S(1)}, u32[]{:S(2)}, u32[]{:S(2)}) %collective-permute-start.5) | collective-permute-done | bytes 405536 | tf_op jit(solution)/shard_map/ppermute | solution.py:101
  39.7 1.5 %collective-permute-start.11 = (bf16[2,24,4224]{2,1,0:T(8,128)(2,1)S(1)}, bf16[2,24,4224]{2,1,0:T(8,128)(2,1)S(1)}, u32[]{:S(2)}, u32[]{:S(2)}) collective-permute-start(bf16[2,24,4224]{2,1,0:T(8,128)(2,1)S(1)} %pad_maximum_fusion.13), channel_id=1, source_target_pairs={{0,16},{16,0},{1,17},{17,1},{2,18},{18,2},{3,19},{19,3},{4,20},{20... | collective-permute-start | bytes 1216520 | tf_op jit(solution)/shard_map/ppermute | solution.py:101
  44.5 1.7 %copy-done.1 = bf16[1,384,4096]{2,1,0:T(8,128)(2,1)S(1)} copy-done((bf16[1,384,4096]{2,1,0:T(8,128)(2,1)S(1)}, bf16[1,384,4096]{2,1,0:T(8,128)(2,1)}, u32[]{:S(2)}) %copy-start.1) | copy-done | bytes 3145752
  49.3 1.3 %multiply_convert_fusion.3 = (bf16[192,384]{1,0:T(8,128)(2,1)S(1)}, bf16[192,384]{1,0:T(8,128)(2,1)S(1)}, bf16[192,384]{1,0:T(8,128)(2,1)S(1)}) fusion(f32[192]{0:T(256)S(1)} %select_reduce_fusion.3, f32[192,384]{1,0:T(8,128)S(1)} %fusion.34, f32[192,384]{1,0:T(8,128)S(1)} %fusion.56, bf16[192,4096]{1,0:T(8,128)(2,1)S(1)} %pad_maximum_fusion.6, ...), kind=kOutput, calls=%fused_computation.161 | convolution fusion | flops 605159424 | bytes 5751552 | tf_op jit(solution)/shard_map/rd,fd->rf/dot_general | solution.py:148
  53.6 1.6 %collective-permute-start.15 = (bf16[2,24,4224]{2,1,0:T(8,128)(2,1)S(1)}, bf16[2,24,4224]{2,1,0:T(8,128)(2,1)S(1)}, u32[]{:S(2)}, u32[]{:S(2)}) collective-permute-start(bf16[2,24,4224]{2,1,0:T(8,128)(2,1)S(1)} %get-tuple-element.144), channel_id=1, source_target_pairs={{0,2},{1,3},{2,0},{3,1},{4,6},{5,7},{6,4},{7,5},{8,10},{9,11},{10,... | collective-permute-start | bytes 1216520 | tf_op jit(solution)/shard_map/ppermute | solution.py:101
  58.0 4.7 %collective-permute-done.19 = bf16[2,96,4224]{2,1,0:T(8,128)(2,1)S(1)} collective-permute-done((bf16[2,96,4224]{2,1,0:T(8,128)(2,1)S(1)}, bf16[2,96,4224]{2,1,0:T(8,128)(2,1)S(1)}, u32[]{:S(2)}, u32[]{:S(2)}) %collective-permute-start.19) | collective-permute-done | bytes 1622048 | tf_op jit(solution)/shard_map/ppermute | solution.py:101
  67.8 1.3 fusion.17
  69.7 1.6 %collective-permute-start.20 = (bf16[24,4224]{1,0:T(8,128)(2,1)S(1)}, bf16[24,4224]{1,0:T(8,128)(2,1)S(1)}, u32[]{:S(2)}, u32[]{:S(2)}) collective-permute-start(bf16[24,4224]{1,0:T(8,128)(2,1)S(1)} %get-tuple-element.132), channel_id=1, source_target_pairs={{0,2},{1,3},{2,0},{3,1},{4,6},{5,7},{6,4},{7,5},{8,10},{9,11},{10,... | collective-permute-start | bytes 608264 | tf_op jit(solution)/shard_map/ppermute | solution.py:101
  74.5 1.3 %multiply_convert_fusion.1 = (bf16[192,384]{1,0:T(8,128)(2,1)S(1)}, bf16[192,384]{1,0:T(8,128)(2,1)S(1)}, bf16[192,384]{1,0:T(8,128)(2,1)S(1)}) fusion(f32[192]{0:T(256)S(1)} %select_reduce_fusion.1, f32[192,384]{1,0:T(8,128)S(1)} %fusion.26, f32[192,384]{1,0:T(8,128)S(1)} %fusion.62, bf16[192,4096]{1,0:T(8,128)(2,1)S(1)} %pad_maximum_fusion.4, ...), kind=kOutput, calls=%fused_computation.159 | convolution fusion | flops 605159424 | bytes 5751552 | tf_op jit(solution)/shard_map/rd,fd->rf/dot_general | solution.py:148
  80.7 1.4 %collective-permute-start.26 = (bf16[3,24,2048]{2,1,0:T(8,128)(2,1)S(1)}, bf16[3,24,2048]{2,1,0:T(8,128)(2,1)S(1)}, u32[]{:S(2)}, u32[]{:S(2)}) collective-permute-start(bf16[3,24,2048]{2,1,0:T(8,128)(2,1)S(1)} %pad_maximum_fusion.16), channel_id=1, source_target_pairs={{0,16},{16,0},{1,17},{17,1},{2,18},{18,2},{3,19},{19,3},{4,20},{20... | collective-permute-start | bytes 884744 | tf_op jit(solution)/shard_map/ppermute | solution.py:101
  82.1 1.7 %collective-permute-done.28 = bf16[4,24,4096]{2,1,0:T(8,128)(2,1)S(1)} collective-permute-done((bf16[4,24,4096]{2,1,0:T(8,128)(2,1)S(1)}, bf16[4,24,4096]{2,1,0:T(8,128)(2,1)S(1)}, u32[]{:S(2)}, u32[]{:S(2)}) %collective-permute-start.28) | collective-permute-done | bytes 786464 | tf_op jit(solution)/shard_map/ppermute | solution.py:101
  86.9 1.3 multiply_convert_fusion
  90.9 1.4 %collective-permute-start.27 = (bf16[24,4096]{1,0:T(8,128)(2,1)S(1)}, bf16[24,4096]{1,0:T(8,128)(2,1)S(1)}, u32[]{:S(2)}, u32[]{:S(2)}) collective-permute-start(bf16[24,4096]{1,0:T(8,128)(2,1)S(1)} %pad_maximum_fusion.17), channel_id=1, source_target_pairs={{0,4},{1,5},{2,6},{3,7},{4,0},{5,1},{6,2},{7,3},{8,12},{9,13},{10,... | collective-permute-start | bytes 589832 | tf_op jit(solution)/shard_map/ppermute | solution.py:101
  93.0 1.6 %collective-permute-start.30 = (bf16[2,24,2048]{2,1,0:T(8,128)(2,1)S(1)}, bf16[2,24,2048]{2,1,0:T(8,128)(2,1)S(1)}, u32[]{:S(2)}, u32[]{:S(2)}) collective-permute-start(bf16[2,24,2048]{2,1,0:T(8,128)(2,1)S(1)} %pad_maximum_fusion.18), channel_id=1, source_target_pairs={{0,16},{16,0},{1,17},{17,1},{2,18},{18,2},{3,19},{19,3},{4,20},{20... | collective-permute-start | bytes 589832 | tf_op jit(solution)/shard_map/ppermute | solution.py:101
  97.3 3.0 %collective-permute-done.32 = bf16[24,2048]{1,0:T(8,128)(2,1)S(1)} collective-permute-done((bf16[24,2048]{1,0:T(8,128)(2,1)S(1)}, bf16[24,2048]{1,0:T(8,128)(2,1)S(1)}, u32[]{:S(2)}, u32[]{:S(2)}) %collective-permute-start.32) | collective-permute-done | bytes 98336 | tf_op jit(solution)/shard_map/ppermute | solution.py:101
  100.4 2.0 %collective-permute-done.31 = bf16[24,2048]{1,0:T(8,128)(2,1)S(1)} collective-permute-done((bf16[24,2048]{1,0:T(8,128)(2,1)S(1)}, bf16[24,2048]{1,0:T(8,128)(2,1)S(1)}, u32[]{:S(2)}, u32[]{:S(2)}) %collective-permute-start.31) | collective-permute-done | bytes 98336 | tf_op jit(solution)/shard_map/ppermute | solution.py:101
  102.4 1.3 %collective-permute-start.33 = (bf16[24,4096]{1,0:T(8,128)(2,1)S(1)}, bf16[24,4096]{1,0:T(8,128)(2,1)S(1)}, u32[]{:S(2)}, u32[]{:S(2)}) collective-permute-start(bf16[24,4096]{1,0:T(8,128)(2,1)S(1)} %pad_maximum_fusion.19), channel_id=1, source_target_pairs={{0,4},{1,5},{2,6},{3,7},{4,0},{5,1},{6,2},{7,3},{8,12},{9,13},{10,... | collective-permute-start | bytes 589832 | tf_op jit(solution)/shard_map/ppermute | solution.py:101
  103.7 4.0 %fusion.11 = bf16[1,384,4096]{2,1,0:T(8,128)(2,1)} fusion(bf16[192,4096]{1,0:T(8,128)(2,1)S(1)} %slice.539, bf16[192,4096]{1,0:T(8,128)(2,1)S(1)} %pad_maximum_fusion.4, bf16[192,4096]{1,0:T(8,128)(2,1)S(1)} %slice.532, bf16[192,4096]{1,0:T(8,128)(2,1)S(1)} %pad_maximum_fusion.6, bf16[192,384]{1,0:T(8,128)(2,1)S(1)} %get-tuple-element.123, ...), kind=kOutput, calls=%fused_computation.16 | convolution fusion | flops 2445017088 | bytes 10027008 | tf_op jit(solution)/shard_map/rf,rd->fd/dot_general | solution.py:271
  109.8 1.6 %collective-permute-start.36 = (bf16[24,4096]{1,0:T(8,128)(2,1)S(1)}, bf16[24,4096]{1,0:T(8,128)(2,1)S(1)}, u32[]{:S(2)}, u32[]{:S(2)}) collective-permute-start(bf16[24,4096]{1,0:T(8,128)(2,1)S(1)} %pad_maximum_fusion.22), channel_id=1, source_target_pairs={{0,16},{16,0},{1,17},{17,1},{2,18},{18,2},{3,19},{19,3},{4,20},{20... | collective-permute-start | bytes 589832 | tf_op jit(solution)/shard_map/ppermute | solution.py:101
  112.1 4.0 %fusion.12 = bf16[1,384,4096]{2,1,0:T(8,128)(2,1)} fusion(bf16[192,4096]{1,0:T(8,128)(2,1)S(1)} %slice.539, bf16[192,4096]{1,0:T(8,128)(2,1)S(1)} %pad_maximum_fusion.4, bf16[192,4096]{1,0:T(8,128)(2,1)S(1)} %slice.532, bf16[192,4096]{1,0:T(8,128)(2,1)S(1)} %pad_maximum_fusion.6, bf16[192,384]{1,0:T(8,128)(2,1)S(1)} %get-tuple-element.124, ...), kind=kOutput, calls=%fused_computation.17 | convolution fusion | flops 2445017088 | bytes 10027008 | tf_op jit(solution)/shard_map/rf,rd->fd/dot_general | solution.py:271
  118.8 1.5 %collective-permute-start.39 = (bf16[24,4096]{1,0:T(8,128)(2,1)S(1)}, bf16[24,4096]{1,0:T(8,128)(2,1)S(1)}, u32[]{:S(2)}, u32[]{:S(2)}) collective-permute-start(bf16[24,4096]{1,0:T(8,128)(2,1)S(1)} %pad_maximum_fusion.25), channel_id=1, source_target_pairs={{0,16},{16,0},{1,17},{17,1},{2,18},{18,2},{3,19},{19,3},{4,20},{20... | collective-permute-start | bytes 589832 | tf_op jit(solution)/shard_map/ppermute | solution.py:101
  121.0 4.0 %fusion.13 = bf16[1,384,4096]{2,1,0:T(8,128)(2,1)} fusion(bf16[192,4096]{1,0:T(8,128)(2,1)S(1)} %slice.537, bf16[192,4096]{1,0:T(8,128)(2,1)S(1)} %pad_maximum_fusion.5, bf16[192,4096]{1,0:T(8,128)(2,1)S(1)} %slice.530, bf16[192,4096]{1,0:T(8,128)(2,1)S(1)} %pad_maximum_fusion.7, bf16[192,384]{1,0:T(8,128)(2,1)S(1)} %get-tuple-element.122, ...), kind=kOutput, calls=%fused_computation.18 | convolution fusion | flops 2445017088 | bytes 10027008 | tf_op jit(solution)/shard_map/rf,rd->fd/dot_general | solution.py:271
  (190 shorter events, 55.2 us)
Async XLA Ops:
  0.6 13.6 %collective-permute-start.7 = (bf16[24,4096]{1,0:T(8,128)(2,1)}, bf16[24,4096]{1,0:T(8,128)(2,1)}, u32[]{:S(2)}, u32[]{:S(2)}) collective-permute-start(bf16[24,4096]{1,0:T(8,128)(2,1)} %param.7), channel_id=1, source_target_pairs={{0,8},{1,9},{2,10},{3,11},{4,12},{5,13},{6,14},{7,15},{8,0},{9,1},... | collective-permute-start | bytes 589832 | tf_op jit(solution)/shard_map/ppermute | solution.py:101
  6.7 19.7 %collective-permute-start = (bf16[2,24,4224]{2,1,0:T(8,128)(2,1)S(1)}, bf16[2,24,4224]{2,1,0:T(8,128)(2,1)}, u32[]{:S(2)}, u32[]{:S(2)}) collective-permute-start(bf16[2,24,4224]{2,1,0:T(8,128)(2,1)S(1)} %pad_maximum_fusion.12), channel_id=1, source_target_pairs={{0,4},{1,5},{2,6},{3,7},{4,0},{5,1},{6,2},{7,3},{8,12},{9,13},{10,... | collective-permute-start | bytes 1216520 | tf_op jit(solution)/shard_map/ppermute | solution.py:101
  8.3 10.7 %collective-permute-start.1 = (bf16[2,24,4224]{2,1,0:T(8,128)(2,1)S(1)}, bf16[2,24,4224]{2,1,0:T(8,128)(2,1)}, u32[]{:S(2)}, u32[]{:S(2)}) collective-permute-start(bf16[2,24,4224]{2,1,0:T(8,128)(2,1)S(1)} %pad_maximum_fusion.12), channel_id=1, source_target_pairs={{0,2},{1,3},{2,0},{3,1},{4,6},{5,7},{6,4},{7,5},{8,10},{9,11},{10,... | collective-permute-start | bytes 1216520 | tf_op jit(solution)/shard_map/ppermute | solution.py:101
  9.8 10.4 %collective-permute-start.2 = (bf16[2,24,4224]{2,1,0:T(8,128)(2,1)S(1)}, bf16[2,24,4224]{2,1,0:T(8,128)(2,1)}, u32[]{:S(2)}, u32[]{:S(2)}) collective-permute-start(bf16[2,24,4224]{2,1,0:T(8,128)(2,1)S(1)} %pad_maximum_fusion.12), channel_id=1, source_target_pairs={{0,16},{16,0},{1,17},{17,1},{2,18},{18,2},{3,19},{19,3},{4,20},{20... | collective-permute-start | bytes 1216520 | tf_op jit(solution)/shard_map/ppermute | solution.py:101
  14.3 18.5 %collective-permute-start.9 = (bf16[24,4224]{1,0:T(8,128)(2,1)S(1)}, bf16[24,4224]{1,0:T(8,128)(2,1)S(1)}, u32[]{:S(2)}, u32[]{:S(2)}) collective-permute-start(bf16[24,4224]{1,0:T(8,128)(2,1)S(1)} %slice_bitcast_fusion.26), channel_id=1, source_target_pairs={{0,8},{1,9},{2,10},{3,11},{4,12},{5,13},{6,14},{7,15},{8,0},{9,1},... | collective-permute-start | bytes 608264 | tf_op jit(solution)/shard_map/ppermute | solution.py:101
  28.5 8.5 %collective-permute-start.5 = (bf16[2,24,4224]{2,1,0:T(8,128)(2,1)}, bf16[2,24,4224]{2,1,0:T(8,128)(2,1)S(1)}, u32[]{:S(2)}, u32[]{:S(2)}) collective-permute-start(bf16[2,24,4224]{2,1,0:T(8,128)(2,1)} %collective-permute-done), channel_id=1, source_target_pairs={{0,2},{1,3},{2,0},{3,1},{4,6},{5,7},{6,4},{7,5},{8,10},{9,11},{10,... | collective-permute-start | bytes 1216520 | tf_op jit(solution)/shard_map/ppermute | solution.py:101
  30.0 8.1 %collective-permute-start.6 = (bf16[2,24,4224]{2,1,0:T(8,128)(2,1)}, bf16[2,24,4224]{2,1,0:T(8,128)(2,1)S(1)}, u32[]{:S(2)}, u32[]{:S(2)}) collective-permute-start(bf16[2,24,4224]{2,1,0:T(8,128)(2,1)} %collective-permute-done), channel_id=1, source_target_pairs={{0,16},{16,0},{1,17},{17,1},{2,18},{18,2},{3,19},{19,3},{4,20},{20... | collective-permute-start | bytes 1216520 | tf_op jit(solution)/shard_map/ppermute | solution.py:101
  39.1 14.1 %collective-permute-start.10 = (bf16[2,24,4224]{2,1,0:T(8,128)(2,1)S(1)}, bf16[2,24,4224]{2,1,0:T(8,128)(2,1)S(1)}, u32[]{:S(2)}, u32[]{:S(2)}) collective-permute-start(bf16[2,24,4224]{2,1,0:T(8,128)(2,1)S(1)} %pad_maximum_fusion.13), channel_id=1, source_target_pairs={{0,2},{1,3},{2,0},{3,1},{4,6},{5,7},{6,4},{7,5},{8,10},{9,11},{10,... | collective-permute-start | bytes 1216520 | tf_op jit(solution)/shard_map/ppermute | solution.py:101
  39.7 13.4 %collective-permute-start.11 = (bf16[2,24,4224]{2,1,0:T(8,128)(2,1)S(1)}, bf16[2,24,4224]{2,1,0:T(8,128)(2,1)S(1)}, u32[]{:S(2)}, u32[]{:S(2)}) collective-permute-start(bf16[2,24,4224]{2,1,0:T(8,128)(2,1)S(1)} %pad_maximum_fusion.13), channel_id=1, source_target_pairs={{0,16},{16,0},{1,17},{17,1},{2,18},{18,2},{3,19},{19,3},{4,20},{20... | collective-permute-start | bytes 1216520 | tf_op jit(solution)/shard_map/ppermute | solution.py:101
  41.3 11.9 %collective-permute-start.12 = (bf16[2,24,4224]{2,1,0:T(8,128)(2,1)S(1)}, bf16[2,24,4224]{2,1,0:T(8,128)(2,1)S(1)}, u32[]{:S(2)}, u32[]{:S(2)}) collective-permute-start(bf16[2,24,4224]{2,1,0:T(8,128)(2,1)S(1)} %pad_maximum_fusion.13), channel_id=1, source_target_pairs={{0,4},{1,5},{2,6},{3,7},{4,0},{5,1},{6,2},{7,3},{8,12},{9,13},{10,... | collective-permute-start | bytes 1216520 | tf_op jit(solution)/shard_map/ppermute | solution.py:101
  42.2 10.7 %collective-permute-start.13 = (bf16[24,4224]{1,0:T(8,128)(2,1)S(1)}, bf16[24,4224]{1,0:T(8,128)(2,1)S(1)}, u32[]{:S(2)}, u32[]{:S(2)}) collective-permute-start(bf16[24,4224]{1,0:T(8,128)(2,1)S(1)} %get-tuple-element.138), channel_id=1, source_target_pairs={{0,2},{1,3},{2,0},{3,1},{4,6},{5,7},{6,4},{7,5},{8,10},{9,11},{10,... | collective-permute-start | bytes 608264 | tf_op jit(solution)/shard_map/ppermute | solution.py:101
  43.3 9.9 %collective-permute-start.14 = (bf16[24,4224]{1,0:T(8,128)(2,1)S(1)}, bf16[24,4224]{1,0:T(8,128)(2,1)S(1)}, u32[]{:S(2)}, u32[]{:S(2)}) collective-permute-start(bf16[24,4224]{1,0:T(8,128)(2,1)S(1)} %get-tuple-element.140), channel_id=1, source_target_pairs={{0,16},{16,0},{1,17},{17,1},{2,18},{18,2},{3,19},{19,3},{4,20},{20... | collective-permute-start | bytes 608264 | tf_op jit(solution)/shard_map/ppermute | solution.py:101
  53.6 15.5 %collective-permute-start.15 = (bf16[2,24,4224]{2,1,0:T(8,128)(2,1)S(1)}, bf16[2,24,4224]{2,1,0:T(8,128)(2,1)S(1)}, u32[]{:S(2)}, u32[]{:S(2)}) collective-permute-start(bf16[2,24,4224]{2,1,0:T(8,128)(2,1)S(1)} %get-tuple-element.144), channel_id=1, source_target_pairs={{0,2},{1,3},{2,0},{3,1},{4,6},{5,7},{6,4},{7,5},{8,10},{9,11},{10,... | collective-permute-start | bytes 1216520 | tf_op jit(solution)/shard_map/ppermute | solution.py:101
  55.1 14.0 %collective-permute-start.16 = (bf16[2,24,4224]{2,1,0:T(8,128)(2,1)S(1)}, bf16[2,24,4224]{2,1,0:T(8,128)(2,1)S(1)}, u32[]{:S(2)}, u32[]{:S(2)}) collective-permute-start(bf16[2,24,4224]{2,1,0:T(8,128)(2,1)S(1)} %get-tuple-element.145), channel_id=1, source_target_pairs={{0,16},{16,0},{1,17},{17,1},{2,18},{18,2},{3,19},{19,3},{4,20},{20... | collective-permute-start | bytes 1216520 | tf_op jit(solution)/shard_map/ppermute | solution.py:101
  55.8 13.3 %collective-permute-start.17 = (bf16[2,24,4224]{2,1,0:T(8,128)(2,1)S(1)}, bf16[2,24,4224]{2,1,0:T(8,128)(2,1)S(1)}, u32[]{:S(2)}, u32[]{:S(2)}) collective-permute-start(bf16[2,24,4224]{2,1,0:T(8,128)(2,1)S(1)} %get-tuple-element.143), channel_id=1, source_target_pairs={{0,4},{1,5},{2,6},{3,7},{4,0},{5,1},{6,2},{7,3},{8,12},{9,13},{10,... | collective-permute-start | bytes 1216520 | tf_op jit(solution)/shard_map/ppermute | solution.py:101
  56.9 12.2 %collective-permute-start.18 = (bf16[2,96,4224]{2,1,0:T(8,128)(2,1)S(1)}, bf16[2,96,4224]{2,1,0:T(8,128)(2,1)S(1)}, u32[]{:S(2)}, u32[]{:S(2)}) collective-permute-start(bf16[2,96,4224]{2,1,0:T(8,128)(2,1)S(1)} %pad_maximum_fusion.1), channel_id=1, source_target_pairs={{0,1},{1,0},{2,3},{3,2},{4,5},{5,4},{6,7},{7,6},{8,9},{9,8},{10,11... | collective-permute-start | bytes 4866056 | tf_op jit(solution)/shard_map/ppermute | solution.py:101
  62.7 15.6 %collective-permute-start.22 = (bf16[4,24,4096]{2,1,0:T(8,128)(2,1)S(1)}, bf16[4,24,4096]{2,1,0:T(8,128)(2,1)S(1)}, u32[]{:S(2)}, u32[]{:S(2)}) collective-permute-start(bf16[4,24,4096]{2,1,0:T(8,128)(2,1)S(1)} %slice_bitcast_fusion.15), channel_id=1, source_target_pairs={{0,1},{1,0},{2,3},{3,2},{4,5},{5,4},{6,7},{7,6},{8,9},{9,8},{10,11... | collective-permute-start | bytes 2359304 | tf_op jit(solution)/shard_map/ppermute | solution.py:101
  69.7 8.6 %collective-permute-start.20 = (bf16[24,4224]{1,0:T(8,128)(2,1)S(1)}, bf16[24,4224]{1,0:T(8,128)(2,1)S(1)}, u32[]{:S(2)}, u32[]{:S(2)}) collective-permute-start(bf16[24,4224]{1,0:T(8,128)(2,1)S(1)} %get-tuple-element.132), channel_id=1, source_target_pairs={{0,2},{1,3},{2,0},{3,1},{4,6},{5,7},{6,4},{7,5},{8,10},{9,11},{10,... | collective-permute-start | bytes 608264 | tf_op jit(solution)/shard_map/ppermute | solution.py:101
  71.2 7.1 %collective-permute-start.21 = (bf16[24,4224]{1,0:T(8,128)(2,1)S(1)}, bf16[24,4224]{1,0:T(8,128)(2,1)S(1)}, u32[]{:S(2)}, u32[]{:S(2)}) collective-permute-start(bf16[24,4224]{1,0:T(8,128)(2,1)S(1)} %get-tuple-element.131), channel_id=1, source_target_pairs={{0,16},{16,0},{1,17},{17,1},{2,18},{18,2},{3,19},{19,3},{4,20},{20... | collective-permute-start | bytes 608264 | tf_op jit(solution)/shard_map/ppermute | solution.py:101
  71.8 6.5 %collective-permute-start.23 = (bf16[4,24,4096]{2,1,0:T(8,128)(2,1)S(1)}, bf16[4,24,4096]{2,1,0:T(8,128)(2,1)S(1)}, u32[]{:S(2)}, u32[]{:S(2)}) collective-permute-start(bf16[4,24,4096]{2,1,0:T(8,128)(2,1)S(1)} %slice_bitcast_fusion.14), channel_id=1, source_target_pairs={{0,1},{1,0},{2,3},{3,2},{4,5},{5,4},{6,7},{7,6},{8,9},{9,8},{10,11... | collective-permute-start | bytes 2359304 | tf_op jit(solution)/shard_map/ppermute | solution.py:101
  79.7 10.6 %collective-permute-start.25 = (bf16[3,24,2048]{2,1,0:T(8,128)(2,1)S(1)}, bf16[3,24,2048]{2,1,0:T(8,128)(2,1)S(1)}, u32[]{:S(2)}, u32[]{:S(2)}) collective-permute-start(bf16[3,24,2048]{2,1,0:T(8,128)(2,1)S(1)} %pad_maximum_fusion.15), channel_id=1, source_target_pairs={{0,2},{1,3},{2,0},{3,1},{4,6},{5,7},{6,4},{7,5},{8,10},{9,11},{10,... | collective-permute-start | bytes 884744 | tf_op jit(solution)/shard_map/ppermute | solution.py:101
  80.7 9.6 %collective-permute-start.26 = (bf16[3,24,2048]{2,1,0:T(8,128)(2,1)S(1)}, bf16[3,24,2048]{2,1,0:T(8,128)(2,1)S(1)}, u32[]{:S(2)}, u32[]{:S(2)}) collective-permute-start(bf16[3,24,2048]{2,1,0:T(8,128)(2,1)S(1)} %pad_maximum_fusion.16), channel_id=1, source_target_pairs={{0,16},{16,0},{1,17},{17,1},{2,18},{18,2},{3,19},{19,3},{4,20},{20... | collective-permute-start | bytes 884744 | tf_op jit(solution)/shard_map/ppermute | solution.py:101
  90.9 25.4 %collective-permute-start.27 = (bf16[24,4096]{1,0:T(8,128)(2,1)S(1)}, bf16[24,4096]{1,0:T(8,128)(2,1)S(1)}, u32[]{:S(2)}, u32[]{:S(2)}) collective-permute-start(bf16[24,4096]{1,0:T(8,128)(2,1)S(1)} %pad_maximum_fusion.17), channel_id=1, source_target_pairs={{0,4},{1,5},{2,6},{3,7},{4,0},{5,1},{6,2},{7,3},{8,12},{9,13},{10,... | collective-permute-start | bytes 589832 | tf_op jit(solution)/shard_map/ppermute | solution.py:101
  93.0 14.7 %collective-permute-start.30 = (bf16[2,24,2048]{2,1,0:T(8,128)(2,1)S(1)}, bf16[2,24,2048]{2,1,0:T(8,128)(2,1)S(1)}, u32[]{:S(2)}, u32[]{:S(2)}) collective-permute-start(bf16[2,24,2048]{2,1,0:T(8,128)(2,1)S(1)} %pad_maximum_fusion.18), channel_id=1, source_target_pairs={{0,16},{16,0},{1,17},{17,1},{2,18},{18,2},{3,19},{19,3},{4,20},{20... | collective-permute-start | bytes 589832 | tf_op jit(solution)/shard_map/ppermute | solution.py:101
  95.9 11.9 %collective-permute-start.35 = (bf16[2,24,2048]{2,1,0:T(8,128)(2,1)S(1)}, bf16[2,24,2048]{2,1,0:T(8,128)(2,1)S(1)}, u32[]{:S(2)}, u32[]{:S(2)}) collective-permute-start(bf16[2,24,2048]{2,1,0:T(8,128)(2,1)S(1)} %pad_maximum_fusion.21), channel_id=1, source_target_pairs={{0,2},{1,3},{2,0},{3,1},{4,6},{5,7},{6,4},{7,5},{8,10},{9,11},{10,... | collective-permute-start | bytes 589832 | tf_op jit(solution)/shard_map/ppermute | solution.py:101
  102.4 6.4 %collective-permute-start.33 = (bf16[24,4096]{1,0:T(8,128)(2,1)S(1)}, bf16[24,4096]{1,0:T(8,128)(2,1)S(1)}, u32[]{:S(2)}, u32[]{:S(2)}) collective-permute-start(bf16[24,4096]{1,0:T(8,128)(2,1)S(1)} %pad_maximum_fusion.19), channel_id=1, source_target_pairs={{0,4},{1,5},{2,6},{3,7},{4,0},{5,1},{6,2},{7,3},{8,12},{9,13},{10,... | collective-permute-start | bytes 589832 | tf_op jit(solution)/shard_map/ppermute | solution.py:101
  109.0 7.3 %collective-permute-start.34 = (bf16[24,4096]{1,0:T(8,128)(2,1)S(1)}, bf16[24,4096]{1,0:T(8,128)(2,1)S(1)}, u32[]{:S(2)}, u32[]{:S(2)}) collective-permute-start(bf16[24,4096]{1,0:T(8,128)(2,1)S(1)} %pad_maximum_fusion.20), channel_id=1, source_target_pairs={{0,2},{1,3},{2,0},{3,1},{4,6},{5,7},{6,4},{7,5},{8,10},{9,11},{10,... | collective-permute-start | bytes 589832 | tf_op jit(solution)/shard_map/ppermute | solution.py:101
  109.8 6.6 %collective-permute-start.36 = (bf16[24,4096]{1,0:T(8,128)(2,1)S(1)}, bf16[24,4096]{1,0:T(8,128)(2,1)S(1)}, u32[]{:S(2)}, u32[]{:S(2)}) collective-permute-start(bf16[24,4096]{1,0:T(8,128)(2,1)S(1)} %pad_maximum_fusion.22), channel_id=1, source_target_pairs={{0,16},{16,0},{1,17},{17,1},{2,18},{18,2},{3,19},{19,3},{4,20},{20... | collective-permute-start | bytes 589832 | tf_op jit(solution)/shard_map/ppermute | solution.py:101
  117.2 9.0 %collective-permute-start.41 = (bf16[24,4096]{1,0:T(8,128)(2,1)S(1)}, bf16[24,4096]{1,0:T(8,128)(2,1)S(1)}, u32[]{:S(2)}, u32[]{:S(2)}) collective-permute-start(bf16[24,4096]{1,0:T(8,128)(2,1)S(1)} %add_convert_fusion.1), channel_id=1, source_target_pairs={{0,8},{1,9},{2,10},{3,11},{4,12},{5,13},{6,14},{7,15},{8,0},{9,1},... | collective-permute-start | bytes 589832 | tf_op jit(solution)/shard_map/ppermute | solution.py:101
  117.9 8.2 %collective-permute-start.40 = (bf16[24,4096]{1,0:T(8,128)(2,1)S(1)}, bf16[24,4096]{1,0:T(8,128)(2,1)S(1)}, u32[]{:S(2)}, u32[]{:S(2)}) collective-permute-start(bf16[24,4096]{1,0:T(8,128)(2,1)S(1)} %pad_maximum_fusion.26), channel_id=1, source_target_pairs={{0,4},{1,5},{2,6},{3,7},{4,0},{5,1},{6,2},{7,3},{8,12},{9,13},{10,... | collective-permute-start | bytes 589832 | tf_op jit(solution)/shard_map/ppermute | solution.py:101
  118.8 7.4 %collective-permute-start.39 = (bf16[24,4096]{1,0:T(8,128)(2,1)S(1)}, bf16[24,4096]{1,0:T(8,128)(2,1)S(1)}, u32[]{:S(2)}, u32[]{:S(2)}) collective-permute-start(bf16[24,4096]{1,0:T(8,128)(2,1)S(1)} %pad_maximum_fusion.25), channel_id=1, source_target_pairs={{0,16},{16,0},{1,17},{17,1},{2,18},{18,2},{3,19},{19,3},{4,20},{20... | collective-permute-start | bytes 589832 | tf_op jit(solution)/shard_map/ppermute | solution.py:101
  120.3 5.9 %collective-permute-start.38 = (bf16[24,4096]{1,0:T(8,128)(2,1)S(1)}, bf16[24,4096]{1,0:T(8,128)(2,1)S(1)}, u32[]{:S(2)}, u32[]{:S(2)}) collective-permute-start(bf16[24,4096]{1,0:T(8,128)(2,1)S(1)} %pad_maximum_fusion.24), channel_id=1, source_target_pairs={{0,2},{1,3},{2,0},{3,1},{4,6},{5,7},{6,4},{7,5},{8,10},{9,11},{10,... | collective-permute-start | bytes 589832 | tf_op jit(solution)/shard_map/ppermute | solution.py:101
  (17 other events, 157.6 us)

commit v5 on v4

--- a/solution.py
+++ b/solution.py
@@ -196,19 +196,20 @@
     g_far, t_far = over_x(from_y[1]), over_y(from_x[0])
     from_z, g_far, t_far = together((from_z, g_far, t_far))
     z_x, z_y = over_x(from_z), over_y(from_z)
+    corner = over_z(jnp.stack([t_far, g_far]))
     near = near_of(mine, from_x, from_y, from_z)
     near_other = over_core(near)
-    z_x, z_y, near_other, distant_t, distant_g = together((z_x, z_y, near_other, distant_t, distant_g))
+    z_x, z_y, corner, near_other, distant_t, distant_g = together((z_x, z_y, corner, near_other, distant_t, distant_g))
     distant = jnp.stack([jnp.pad(distant_t, tail), distant_g])
     first2 = firsts(distant)
-    third = over_x(z_y[1]), over_y(z_x[0])
     part_near, kept_near = expert_rows(near, near_other)
-    first2, third, part_near = together((first2, third, part_near))
+    far = jnp.stack(
+        [rows_of(t_far, z_y[0], z_x[0], corner[0]), rows_of(g_far, z_y[1], z_x[1], corner[1])]
+    )
+    far_other = over_core(far)
+    first2, part_near, far_other = together((first2, part_near, far_other))
+    part_far, kept_far = expert_rows(far, far_other)
     second2 = seconds(*first2)
-    far = jnp.stack(
-        [rows_of(t_far, z_y[0], z_x[0], third[1]), rows_of(g_far, z_y[1], z_x[1], third[0])]
-    )
-    far_other = over_core(far)
     near2 = near_of(distant, *first2)
     near2_other = over_core(near2)
     part_far, kept_far = expert_rows(far, far_other)
@@ -253,8 +254,9 @@
     sums = lane_sums(part_near[0], part_far[0], *others)
     in_x, in_y = early_sends(sums)
     part_far2, kept_far2 = expert_rows(far2, far2_other)
-    part_far2, in_x, in_y = together((part_far2, in_x, in_y))
-    others2 = over_core(part_near2[1]), over_core(part_far2[1])
+    near2_back = over_core(part_near2[1])
+    part_far2, in_x, in_y, near2_back = together((part_far2, in_x, in_y, near2_back))
+    others2 = near2_back, over_core(part_far2[1])
     middle = in_x[1:], in_y[1:]
     from_z = sent_z(sums, (in_x[0], in_y[0]))
     sums2 = lane_sums(part_near2[0], part_far2[0], *others2)

time: 127 us -> 125 us (0.984)
  starting transfers between devices: 41.8 us -> 39.2 us
    ppermute x42 -> x41, starting transfers between devices: 41.8 us -> 39.2 us  [swapped(): return lax.ppermute(x, axis, [(i, i ^ bits) for i in range(count)])]
    ppermute x42 -> x41, waiting for transfers between devices: 31.5 us -> 30.6 us  [swapped(): return lax.ppermute(x, axis, [(i, i ^ bits) for i in range(count)])]
    unnamed x27 -> x30, local copies, waits for them, and re-layouts: 4.92 us -> 5.4 us
  transfers between devices with their start and end apart: 42 -> 41, of which waited for: 17 -> 18; matrix products, arithmetic and copies ran while one was open for 37% -> 36% of each run, Pallas kernels for 0% -> 0%
where the time goes in v5:
time: 125 us
  starting transfers between devices  39.2 us (31%)
  matrix products  35.1 us (28%)
  waiting for transfers between devices  30.6 us (24%)
  local copies, waits for them, and re-layouts  12.1 us (10%)
  other arithmetic  6.37 us (5%)
  between operations  1.6 us (1%)
    ppermute x41, starting transfers between devices, swapped(): return lax.ppermute(x, axis, [(i, i ^ bits) for i in range(count)])  39.2 us
    ppermute x41, waiting for transfers between devices, swapped(): return lax.ppermute(x, axis, [(i, i ^ bits) for i in range(count)])  30.6 us
    dot_general x3, matrix products, weight_grad(): jnp.einsum('rf,rd->fd', rows_of(*(held[at] for held in kept)), rows_of(*(...  12 us
    unnamed x30, local copies, waits for them, and re-layouts  5.4 us
    dot_general x4, matrix products, expert_rows(): jnp.einsum('rd,fd->rf', x_rows, up_w, preferred_element_type=jnp.float32)  5.09 us
    dot_general x4, matrix products, expert_rows(): jnp.einsum('rd,fd->rf', x_rows, gate_w, preferred_element_type=jnp.float32)  4.73 us
    dot_general x4, matrix products, expert_rows(): jnp.einsum('rd,fd->rf', g_rows, down_w, preferred_element_type=jnp.float32)  4.71 us
    dot_general x4, matrix products, expert_rows(): jnp.einsum('rf,fd->rd', d_up_act, up_w, preferred_element_type=jnp.float32)  4.55 us
  transfers between devices with their start and end apart: 41, of which 18 were waited for; matrix products, arithmetic and copies ran while one was open for 36% of the time, Pallas kernels for 0%

profile of v5, /device:TPU:0, one launch (start us, length us, event | category | flops | bytes accessed | tf_op | source)
XLA Modules:
  0.0 124.9 jit_solution(14639196501688529219)
XLA Ops:
  0.6 4.1 %collective-permute-start.8 = (bf16[24,4096]{1,0:T(8,128)(2,1)}, bf16[24,4096]{1,0:T(8,128)(2,1)}, u32[]{:S(2)}, u32[]{:S(2)}) collective-permute-start(bf16[24,4096]{1,0:T(8,128)(2,1)} %param.7), channel_id=1, source_target_pairs={{0,8},{1,9},{2,10},{3,11},{4,12},{5,13},{6,14},{7,15},{8,0},{9,1},... | collective-permute-start | bytes 589832 | tf_op jit(solution)/shard_map/ppermute | solution.py:101
  6.7 1.6 %collective-permute-start = (bf16[2,24,4224]{2,1,0:T(8,128)(2,1)S(1)}, bf16[2,24,4224]{2,1,0:T(8,128)(2,1)}, u32[]{:S(2)}, u32[]{:S(2)}) collective-permute-start(bf16[2,24,4224]{2,1,0:T(8,128)(2,1)S(1)} %pad_maximum_fusion.12), channel_id=1, source_target_pairs={{0,4},{1,5},{2,6},{3,7},{4,0},{5,1},{6,2},{7,3},{8,12},{9,13},{10,... | collective-permute-start | bytes 1216520 | tf_op jit(solution)/shard_map/ppermute | solution.py:101
  8.3 1.5 %collective-permute-start.1 = (bf16[2,24,4224]{2,1,0:T(8,128)(2,1)S(1)}, bf16[2,24,4224]{2,1,0:T(8,128)(2,1)}, u32[]{:S(2)}, u32[]{:S(2)}) collective-permute-start(bf16[2,24,4224]{2,1,0:T(8,128)(2,1)S(1)} %pad_maximum_fusion.12), channel_id=1, source_target_pairs={{0,2},{1,3},{2,0},{3,1},{4,6},{5,7},{6,4},{7,5},{8,10},{9,11},{10,... | collective-permute-start | bytes 1216520 | tf_op jit(solution)/shard_map/ppermute | solution.py:101
  9.8 1.5 %collective-permute-start.2 = (bf16[2,24,4224]{2,1,0:T(8,128)(2,1)S(1)}, bf16[2,24,4224]{2,1,0:T(8,128)(2,1)}, u32[]{:S(2)}, u32[]{:S(2)}) collective-permute-start(bf16[2,24,4224]{2,1,0:T(8,128)(2,1)S(1)} %pad_maximum_fusion.12), channel_id=1, source_target_pairs={{0,16},{16,0},{1,17},{17,1},{2,18},{18,2},{3,19},{19,3},{4,20},{20... | collective-permute-start | bytes 1216520 | tf_op jit(solution)/shard_map/ppermute | solution.py:101
  11.3 3.0 %collective-permute-done.8 = bf16[24,4096]{1,0:T(8,128)(2,1)} collective-permute-done((bf16[24,4096]{1,0:T(8,128)(2,1)}, bf16[24,4096]{1,0:T(8,128)(2,1)}, u32[]{:S(2)}, u32[]{:S(2)}) %collective-permute-start.8) | collective-permute-done | bytes 196640 | tf_op jit(solution)/shard_map/ppermute | solution.py:101
  14.4 4.5 %collective-permute-done.1 = bf16[2,24,4224]{2,1,0:T(8,128)(2,1)} collective-permute-done((bf16[2,24,4224]{2,1,0:T(8,128)(2,1)S(1)}, bf16[2,24,4224]{2,1,0:T(8,128)(2,1)}, u32[]{:S(2)}, u32[]{:S(2)}) %collective-permute-start.1) | collective-permute-done | bytes 405536 | tf_op jit(solution)/shard_map/ppermute | solution.py:101
  22.7 1.6 %collective-permute-start.4 = (bf16[24,4224]{1,0:T(8,128)(2,1)S(1)}, bf16[24,4224]{1,0:T(8,128)(2,1)S(1)}, u32[]{:S(2)}, u32[]{:S(2)}) collective-permute-start(bf16[24,4224]{1,0:T(8,128)(2,1)S(1)} %slice_bitcast_fusion.27), channel_id=1, source_target_pairs={{0,16},{16,0},{1,17},{17,1},{2,18},{18,2},{3,19},{19,3},{4,20},{20... | collective-permute-start | bytes 608264 | tf_op jit(solution)/shard_map/ppermute | solution.py:101
  26.9 1.5 %collective-permute-done.4 = bf16[24,4224]{1,0:T(8,128)(2,1)S(1)} collective-permute-done((bf16[24,4224]{1,0:T(8,128)(2,1)S(1)}, bf16[24,4224]{1,0:T(8,128)(2,1)S(1)}, u32[]{:S(2)}, u32[]{:S(2)}) %collective-permute-start.4) | collective-permute-done | bytes 202784 | tf_op jit(solution)/shard_map/ppermute | solution.py:101
  28.5 1.5 %collective-permute-start.5 = (bf16[2,24,4224]{2,1,0:T(8,128)(2,1)}, bf16[2,24,4224]{2,1,0:T(8,128)(2,1)S(1)}, u32[]{:S(2)}, u32[]{:S(2)}) collective-permute-start(bf16[2,24,4224]{2,1,0:T(8,128)(2,1)} %collective-permute-done), channel_id=1, source_target_pairs={{0,2},{1,3},{2,0},{3,1},{4,6},{5,7},{6,4},{7,5},{8,10},{9,11},{10,... | collective-permute-start | bytes 1216520 | tf_op jit(solution)/shard_map/ppermute | solution.py:101
  30.0 1.5 %collective-permute-start.6 = (bf16[2,24,4224]{2,1,0:T(8,128)(2,1)}, bf16[2,24,4224]{2,1,0:T(8,128)(2,1)S(1)}, u32[]{:S(2)}, u32[]{:S(2)}) collective-permute-start(bf16[2,24,4224]{2,1,0:T(8,128)(2,1)} %collective-permute-done), channel_id=1, source_target_pairs={{0,16},{16,0},{1,17},{17,1},{2,18},{18,2},{3,19},{19,3},{4,20},{20... | collective-permute-start | bytes 1216520 | tf_op jit(solution)/shard_map/ppermute | solution.py:101
  33.3 3.6 %collective-permute-done.5 = bf16[2,24,4224]{2,1,0:T(8,128)(2,1)S(1)} collective-permute-done((bf16[2,24,4224]{2,1,0:T(8,128)(2,1)}, bf16[2,24,4224]{2,1,0:T(8,128)(2,1)S(1)}, u32[]{:S(2)}, u32[]{:S(2)}) %collective-permute-start.5) | collective-permute-done | bytes 405536 | tf_op jit(solution)/shard_map/ppermute | solution.py:101
  38.1 1.4 %collective-permute-done.7 = bf16[2,24,4224]{2,1,0:T(8,128)(2,1)S(1)} collective-permute-done((bf16[2,24,4224]{2,1,0:T(8,128)(2,1)S(1)}, bf16[2,24,4224]{2,1,0:T(8,128)(2,1)S(1)}, u32[]{:S(2)}, u32[]{:S(2)}) %collective-permute-start.7) | collective-permute-done | bytes 405536 | tf_op jit(solution)/shard_map/ppermute | solution.py:101
  43.4 1.6 %copy-done.1 = bf16[1,384,4096]{2,1,0:T(8,128)(2,1)S(1)} copy-done((bf16[1,384,4096]{2,1,0:T(8,128)(2,1)S(1)}, bf16[1,384,4096]{2,1,0:T(8,128)(2,1)}, u32[]{:S(2)}) %copy-start.1) | copy-done | bytes 3145752
  48.1 1.3 %multiply_convert_fusion.3 = (bf16[192,384]{1,0:T(8,128)(2,1)S(1)}, bf16[192,384]{1,0:T(8,128)(2,1)S(1)}, bf16[192,384]{1,0:T(8,128)(2,1)S(1)}) fusion(f32[192]{0:T(256)S(1)} %select_reduce_fusion.3, f32[192,384]{1,0:T(8,128)S(1)} %fusion.34, f32[192,384]{1,0:T(8,128)S(1)} %fusion.56, bf16[192,4096]{1,0:T(8,128)(2,1)S(1)} %pad_maximum_fusion.6, ...), kind=kOutput, calls=%fused_computation.160 | convolution fusion | flops 605159424 | bytes 5751552 | tf_op jit(solution)/shard_map/rd,fd->rf/dot_general | solution.py:148
  55.2 1.3 %collective-permute-start.15 = (bf16[2,24,4224]{2,1,0:T(8,128)(2,1)S(1)}, bf16[2,24,4224]{2,1,0:T(8,128)(2,1)S(1)}, u32[]{:S(2)}, u32[]{:S(2)}) collective-permute-start(bf16[2,24,4224]{2,1,0:T(8,128)(2,1)S(1)} %get-tuple-element.150), channel_id=1, source_target_pairs={{0,2},{1,3},{2,0},{3,1},{4,6},{5,7},{6,4},{7,5},{8,10},{9,11},{10,... | collective-permute-start | bytes 1216520 | tf_op jit(solution)/shard_map/ppermute | solution.py:101
  56.6 1.5 %collective-permute-start.16 = (bf16[2,24,4224]{2,1,0:T(8,128)(2,1)S(1)}, bf16[2,24,4224]{2,1,0:T(8,128)(2,1)S(1)}, u32[]{:S(2)}, u32[]{:S(2)}) collective-permute-start(bf16[2,24,4224]{2,1,0:T(8,128)(2,1)S(1)} %get-tuple-element.151), channel_id=1, source_target_pairs={{0,16},{16,0},{1,17},{17,1},{2,18},{18,2},{3,19},{19,3},{4,20},{20... | collective-permute-start | bytes 1216520 | tf_op jit(solution)/shard_map/ppermute | solution.py:101
  58.1 1.6 %collective-permute-start.17 = (bf16[2,24,4224]{2,1,0:T(8,128)(2,1)S(1)}, bf16[2,24,4224]{2,1,0:T(8,128)(2,1)S(1)}, u32[]{:S(2)}, u32[]{:S(2)}) collective-permute-start(bf16[2,24,4224]{2,1,0:T(8,128)(2,1)S(1)} %get-tuple-element.149), channel_id=1, source_target_pairs={{0,4},{1,5},{2,6},{3,7},{4,0},{5,1},{6,2},{7,3},{8,12},{9,13},{10,... | collective-permute-start | bytes 1216520 | tf_op jit(solution)/shard_map/ppermute | solution.py:101
  72.4 1.3 %multiply_convert_fusion.1 = (bf16[192,384]{1,0:T(8,128)(2,1)S(1)}, bf16[192,384]{1,0:T(8,128)(2,1)S(1)}, bf16[192,384]{1,0:T(8,128)(2,1)S(1)}) fusion(f32[192]{0:T(256)S(1)} %select_reduce_fusion.1, f32[192,384]{1,0:T(8,128)S(1)} %fusion.26, f32[192,384]{1,0:T(8,128)S(1)} %fusion.62, bf16[192,4096]{1,0:T(8,128)(2,1)S(1)} %pad_maximum_fusion.4, ...), kind=kOutput, calls=%fused_computation.158 | convolution fusion | flops 605159424 | bytes 5751552 | tf_op jit(solution)/shard_map/rd,fd->rf/dot_general | solution.py:148
  77.0 1.3 %collective-permute-start.24 = (bf16[3,24,2048]{2,1,0:T(8,128)(2,1)S(1)}, bf16[3,24,2048]{2,1,0:T(8,128)(2,1)S(1)}, u32[]{:S(2)}, u32[]{:S(2)}) collective-permute-start(bf16[3,24,2048]{2,1,0:T(8,128)(2,1)S(1)} %pad_maximum_fusion.16), channel_id=1, source_target_pairs={{0,2},{1,3},{2,0},{3,1},{4,6},{5,7},{6,4},{7,5},{8,10},{9,11},{10,... | collective-permute-start | bytes 884744 | tf_op jit(solution)/shard_map/ppermute | solution.py:101
  78.4 1.6 %collective-permute-start.25 = (bf16[3,24,2048]{2,1,0:T(8,128)(2,1)S(1)}, bf16[3,24,2048]{2,1,0:T(8,128)(2,1)S(1)}, u32[]{:S(2)}, u32[]{:S(2)}) collective-permute-start(bf16[3,24,2048]{2,1,0:T(8,128)(2,1)S(1)} %pad_maximum_fusion.17), channel_id=1, source_target_pairs={{0,16},{16,0},{1,17},{17,1},{2,18},{18,2},{3,19},{19,3},{4,20},{20... | collective-permute-start | bytes 884744 | tf_op jit(solution)/shard_map/ppermute | solution.py:101
  87.2 1.6 %collective-permute-start.27 = (bf16[24,4096]{1,0:T(8,128)(2,1)S(1)}, bf16[24,4096]{1,0:T(8,128)(2,1)S(1)}, u32[]{:S(2)}, u32[]{:S(2)}) collective-permute-start(bf16[24,4096]{1,0:T(8,128)(2,1)S(1)} %pad_maximum_fusion.18), channel_id=1, source_target_pairs={{0,4},{1,5},{2,6},{3,7},{4,0},{5,1},{6,2},{7,3},{8,12},{9,13},{10,... | collective-permute-start | bytes 589832 | tf_op jit(solution)/shard_map/ppermute | solution.py:101
  89.4 1.9 %collective-permute-done.28 = bf16[4,24,4096]{2,1,0:T(8,128)(2,1)S(1)} collective-permute-done((bf16[4,24,4096]{2,1,0:T(8,128)(2,1)S(1)}, bf16[4,24,4096]{2,1,0:T(8,128)(2,1)S(1)}, u32[]{:S(2)}, u32[]{:S(2)}) %collective-permute-start.28) | collective-permute-done | bytes 786464 | tf_op jit(solution)/shard_map/ppermute | solution.py:101
  91.5 1.6 %collective-permute-start.29 = (bf16[2,24,2048]{2,1,0:T(8,128)(2,1)S(1)}, bf16[2,24,2048]{2,1,0:T(8,128)(2,1)S(1)}, u32[]{:S(2)}, u32[]{:S(2)}) collective-permute-start(bf16[2,24,2048]{2,1,0:T(8,128)(2,1)S(1)} %pad_maximum_fusion.19), channel_id=1, source_target_pairs={{0,16},{16,0},{1,17},{17,1},{2,18},{18,2},{3,19},{19,3},{4,20},{20... | collective-permute-start | bytes 589832 | tf_op jit(solution)/shard_map/ppermute | solution.py:101
  93.8 1.6 %collective-permute-start.34 = (bf16[2,24,2048]{2,1,0:T(8,128)(2,1)S(1)}, bf16[2,24,2048]{2,1,0:T(8,128)(2,1)S(1)}, u32[]{:S(2)}, u32[]{:S(2)}) collective-permute-start(bf16[2,24,2048]{2,1,0:T(8,128)(2,1)S(1)} %pad_maximum_fusion.22), channel_id=1, source_target_pairs={{0,2},{1,3},{2,0},{3,1},{4,6},{5,7},{6,4},{7,5},{8,10},{9,11},{10,... | collective-permute-start | bytes 589832 | tf_op jit(solution)/shard_map/ppermute | solution.py:101
  95.8 3.1 %collective-permute-done.31 = bf16[24,2048]{1,0:T(8,128)(2,1)S(1)} collective-permute-done((bf16[24,2048]{1,0:T(8,128)(2,1)S(1)}, bf16[24,2048]{1,0:T(8,128)(2,1)S(1)}, u32[]{:S(2)}, u32[]{:S(2)}) %collective-permute-start.31) | collective-permute-done | bytes 98336 | tf_op jit(solution)/shard_map/ppermute | solution.py:101
  98.9 1.7 %collective-permute-done.30 = bf16[24,2048]{1,0:T(8,128)(2,1)S(1)} collective-permute-done((bf16[24,2048]{1,0:T(8,128)(2,1)S(1)}, bf16[24,2048]{1,0:T(8,128)(2,1)S(1)}, u32[]{:S(2)}, u32[]{:S(2)}) %collective-permute-start.30) | collective-permute-done | bytes 98336 | tf_op jit(solution)/shard_map/ppermute | solution.py:101
  101.2 4.0 %fusion.11 = bf16[1,384,4096]{2,1,0:T(8,128)(2,1)} fusion(bf16[192,4096]{1,0:T(8,128)(2,1)S(1)} %slice.543, bf16[192,4096]{1,0:T(8,128)(2,1)S(1)} %pad_maximum_fusion.4, bf16[192,4096]{1,0:T(8,128)(2,1)S(1)} %slice.536, bf16[192,4096]{1,0:T(8,128)(2,1)S(1)} %pad_maximum_fusion.6, bf16[192,384]{1,0:T(8,128)(2,1)S(1)} %get-tuple-element.125, ...), kind=kOutput, calls=%fused_computation.16 | convolution fusion | flops 2445017088 | bytes 10027008 | tf_op jit(solution)/shard_map/rf,rd->fd/dot_general | solution.py:273
  105.3 1.6 %collective-permute-done.32 = bf16[24,4096]{1,0:T(8,128)(2,1)S(1)} collective-permute-done((bf16[24,4096]{1,0:T(8,128)(2,1)S(1)}, bf16[24,4096]{1,0:T(8,128)(2,1)S(1)}, u32[]{:S(2)}, u32[]{:S(2)}) %collective-permute-start.32) | collective-permute-done | bytes 196640 | tf_op jit(solution)/shard_map/ppermute | solution.py:101
  107.6 1.6 %collective-permute-start.35 = (bf16[24,4096]{1,0:T(8,128)(2,1)S(1)}, bf16[24,4096]{1,0:T(8,128)(2,1)S(1)}, u32[]{:S(2)}, u32[]{:S(2)}) collective-permute-start(bf16[24,4096]{1,0:T(8,128)(2,1)S(1)} %pad_maximum_fusion.23), channel_id=1, source_target_pairs={{0,16},{16,0},{1,17},{17,1},{2,18},{18,2},{3,19},{19,3},{4,20},{20... | collective-permute-start | bytes 589832 | tf_op jit(solution)/shard_map/ppermute | solution.py:101
  110.0 4.0 %fusion.12 = bf16[1,384,4096]{2,1,0:T(8,128)(2,1)} fusion(bf16[192,4096]{1,0:T(8,128)(2,1)S(1)} %slice.543, bf16[192,4096]{1,0:T(8,128)(2,1)S(1)} %pad_maximum_fusion.4, bf16[192,4096]{1,0:T(8,128)(2,1)S(1)} %slice.536, bf16[192,4096]{1,0:T(8,128)(2,1)S(1)} %pad_maximum_fusion.6, bf16[192,384]{1,0:T(8,128)(2,1)S(1)} %get-tuple-element.126, ...), kind=kOutput, calls=%fused_computation.17 | convolution fusion | flops 2445017088 | bytes 10027008 | tf_op jit(solution)/shard_map/rf,rd->fd/dot_general | solution.py:273
  118.8 4.0 %fusion.13 = bf16[1,384,4096]{2,1,0:T(8,128)(2,1)} fusion(bf16[192,4096]{1,0:T(8,128)(2,1)S(1)} %slice.541, bf16[192,4096]{1,0:T(8,128)(2,1)S(1)} %pad_maximum_fusion.5, bf16[192,4096]{1,0:T(8,128)(2,1)S(1)} %slice.535, bf16[192,4096]{1,0:T(8,128)(2,1)S(1)} %pad_maximum_fusion.7, bf16[192,384]{1,0:T(8,128)(2,1)S(1)} %get-tuple-element.124, ...), kind=kOutput, calls=%fused_computation.18 | convolution fusion | flops 2445017088 | bytes 10027008 | tf_op jit(solution)/shard_map/rf,rd->fd/dot_general | solution.py:273
  122.8 1.3 %collective-permute-done.40 = bf16[24,4096]{1,0:T(8,128)(2,1)S(1)} collective-permute-done((bf16[24,4096]{1,0:T(8,128)(2,1)S(1)}, bf16[24,4096]{1,0:T(8,128)(2,1)S(1)}, u32[]{:S(2)}, u32[]{:S(2)}) %collective-permute-start.40) | collective-permute-done | bytes 196640 | tf_op jit(solution)/shard_map/ppermute | solution.py:101
  (195 shorter events, 56.3 us)
Async XLA Ops:
  0.6 13.6 %collective-permute-start.8 = (bf16[24,4096]{1,0:T(8,128)(2,1)}, bf16[24,4096]{1,0:T(8,128)(2,1)}, u32[]{:S(2)}, u32[]{:S(2)}) collective-permute-start(bf16[24,4096]{1,0:T(8,128)(2,1)} %param.7), channel_id=1, source_target_pairs={{0,8},{1,9},{2,10},{3,11},{4,12},{5,13},{6,14},{7,15},{8,0},{9,1},... | collective-permute-start | bytes 589832 | tf_op jit(solution)/shard_map/ppermute | solution.py:101
  6.7 19.7 %collective-permute-start = (bf16[2,24,4224]{2,1,0:T(8,128)(2,1)S(1)}, bf16[2,24,4224]{2,1,0:T(8,128)(2,1)}, u32[]{:S(2)}, u32[]{:S(2)}) collective-permute-start(bf16[2,24,4224]{2,1,0:T(8,128)(2,1)S(1)} %pad_maximum_fusion.12), channel_id=1, source_target_pairs={{0,4},{1,5},{2,6},{3,7},{4,0},{5,1},{6,2},{7,3},{8,12},{9,13},{10,... | collective-permute-start | bytes 1216520 | tf_op jit(solution)/shard_map/ppermute | solution.py:101
  8.3 10.7 %collective-permute-start.1 = (bf16[2,24,4224]{2,1,0:T(8,128)(2,1)S(1)}, bf16[2,24,4224]{2,1,0:T(8,128)(2,1)}, u32[]{:S(2)}, u32[]{:S(2)}) collective-permute-start(bf16[2,24,4224]{2,1,0:T(8,128)(2,1)S(1)} %pad_maximum_fusion.12), channel_id=1, source_target_pairs={{0,2},{1,3},{2,0},{3,1},{4,6},{5,7},{6,4},{7,5},{8,10},{9,11},{10,... | collective-permute-start | bytes 1216520 | tf_op jit(solution)/shard_map/ppermute | solution.py:101
  9.8 10.4 %collective-permute-start.2 = (bf16[2,24,4224]{2,1,0:T(8,128)(2,1)S(1)}, bf16[2,24,4224]{2,1,0:T(8,128)(2,1)}, u32[]{:S(2)}, u32[]{:S(2)}) collective-permute-start(bf16[2,24,4224]{2,1,0:T(8,128)(2,1)S(1)} %pad_maximum_fusion.12), channel_id=1, source_target_pairs={{0,16},{16,0},{1,17},{17,1},{2,18},{18,2},{3,19},{19,3},{4,20},{20... | collective-permute-start | bytes 1216520 | tf_op jit(solution)/shard_map/ppermute | solution.py:101
  14.3 19.0 %collective-permute-start.10 = (bf16[24,4224]{1,0:T(8,128)(2,1)S(1)}, bf16[24,4224]{1,0:T(8,128)(2,1)S(1)}, u32[]{:S(2)}, u32[]{:S(2)}) collective-permute-start(bf16[24,4224]{1,0:T(8,128)(2,1)S(1)} %slice_bitcast_fusion.26), channel_id=1, source_target_pairs={{0,8},{1,9},{2,10},{3,11},{4,12},{5,13},{6,14},{7,15},{8,0},{9,1},... | collective-permute-start | bytes 608264 | tf_op jit(solution)/shard_map/ppermute | solution.py:101
  28.5 8.5 %collective-permute-start.5 = (bf16[2,24,4224]{2,1,0:T(8,128)(2,1)}, bf16[2,24,4224]{2,1,0:T(8,128)(2,1)S(1)}, u32[]{:S(2)}, u32[]{:S(2)}) collective-permute-start(bf16[2,24,4224]{2,1,0:T(8,128)(2,1)} %collective-permute-done), channel_id=1, source_target_pairs={{0,2},{1,3},{2,0},{3,1},{4,6},{5,7},{6,4},{7,5},{8,10},{9,11},{10,... | collective-permute-start | bytes 1216520 | tf_op jit(solution)/shard_map/ppermute | solution.py:101
  30.0 8.1 %collective-permute-start.6 = (bf16[2,24,4224]{2,1,0:T(8,128)(2,1)}, bf16[2,24,4224]{2,1,0:T(8,128)(2,1)S(1)}, u32[]{:S(2)}, u32[]{:S(2)}) collective-permute-start(bf16[2,24,4224]{2,1,0:T(8,128)(2,1)} %collective-permute-done), channel_id=1, source_target_pairs={{0,16},{16,0},{1,17},{17,1},{2,18},{18,2},{3,19},{19,3},{4,20},{20... | collective-permute-start | bytes 1216520 | tf_op jit(solution)/shard_map/ppermute | solution.py:101
  31.6 8.0 %collective-permute-start.7 = (bf16[2,24,4224]{2,1,0:T(8,128)(2,1)S(1)}, bf16[2,24,4224]{2,1,0:T(8,128)(2,1)S(1)}, u32[]{:S(2)}, u32[]{:S(2)}) collective-permute-start(bf16[2,24,4224]{2,1,0:T(8,128)(2,1)S(1)} %pad_maximum_fusion.13), channel_id=1, source_target_pairs={{0,4},{1,5},{2,6},{3,7},{4,0},{5,1},{6,2},{7,3},{8,12},{9,13},{10,... | collective-permute-start | bytes 1216520 | tf_op jit(solution)/shard_map/ppermute | solution.py:101
  33.1 6.4 %collective-permute-start.9 = (bf16[2,96,4224]{2,1,0:T(8,128)(2,1)S(1)}, bf16[2,96,4224]{2,1,0:T(8,128)(2,1)S(1)}, u32[]{:S(2)}, u32[]{:S(2)}) collective-permute-start(bf16[2,96,4224]{2,1,0:T(8,128)(2,1)S(1)} %constant_dynamic-update-slice_fusion), channel_id=1, source_target_pairs={{0,1},{1,0},{2,3},{3,2},{4,5},{5,4},{6,7},{7,6},{8,9},{9,8},{10,11... | collective-permute-start | bytes 4866056 | tf_op jit(solution)/shard_map/ppermute | solution.py:101
  40.5 11.0 %collective-permute-start.11 = (bf16[2,24,4224]{2,1,0:T(8,128)(2,1)S(1)}, bf16[2,24,4224]{2,1,0:T(8,128)(2,1)S(1)}, u32[]{:S(2)}, u32[]{:S(2)}) collective-permute-start(bf16[2,24,4224]{2,1,0:T(8,128)(2,1)S(1)} %pad_maximum_fusion.14), channel_id=1, source_target_pairs={{0,2},{1,3},{2,0},{3,1},{4,6},{5,7},{6,4},{7,5},{8,10},{9,11},{10,... | collective-permute-start | bytes 1216520 | tf_op jit(solution)/shard_map/ppermute | solution.py:101
  41.1 10.4 %collective-permute-start.12 = (bf16[2,24,4224]{2,1,0:T(8,128)(2,1)S(1)}, bf16[2,24,4224]{2,1,0:T(8,128)(2,1)S(1)}, u32[]{:S(2)}, u32[]{:S(2)}) collective-permute-start(bf16[2,24,4224]{2,1,0:T(8,128)(2,1)S(1)} %pad_maximum_fusion.14), channel_id=1, source_target_pairs={{0,16},{16,0},{1,17},{17,1},{2,18},{18,2},{3,19},{19,3},{4,20},{20... | collective-permute-start | bytes 1216520 | tf_op jit(solution)/shard_map/ppermute | solution.py:101
  41.6 10.0 %collective-permute-start.13 = (bf16[2,24,4224]{2,1,0:T(8,128)(2,1)S(1)}, bf16[2,24,4224]{2,1,0:T(8,128)(2,1)S(1)}, u32[]{:S(2)}, u32[]{:S(2)}) collective-permute-start(bf16[2,24,4224]{2,1,0:T(8,128)(2,1)S(1)} %pad_maximum_fusion.14), channel_id=1, source_target_pairs={{0,4},{1,5},{2,6},{3,7},{4,0},{5,1},{6,2},{7,3},{8,12},{9,13},{10,... | collective-permute-start | bytes 1216520 | tf_op jit(solution)/shard_map/ppermute | solution.py:101
  43.2 8.5 %collective-permute-start.14 = (bf16[2,96,4224]{2,1,0:T(8,128)(2,1)S(1)}, bf16[2,96,4224]{2,1,0:T(8,128)(2,1)S(1)}, u32[]{:S(2)}, u32[]{:S(2)}) collective-permute-start(bf16[2,96,4224]{2,1,0:T(8,128)(2,1)S(1)} %pad_maximum_fusion.1), channel_id=1, source_target_pairs={{0,1},{1,0},{2,3},{3,2},{4,5},{5,4},{6,7},{7,6},{8,9},{9,8},{10,11... | collective-permute-start | bytes 4866056 | tf_op jit(solution)/shard_map/ppermute | solution.py:101
  55.2 10.2 %collective-permute-start.15 = (bf16[2,24,4224]{2,1,0:T(8,128)(2,1)S(1)}, bf16[2,24,4224]{2,1,0:T(8,128)(2,1)S(1)}, u32[]{:S(2)}, u32[]{:S(2)}) collective-permute-start(bf16[2,24,4224]{2,1,0:T(8,128)(2,1)S(1)} %get-tuple-element.150), channel_id=1, source_target_pairs={{0,2},{1,3},{2,0},{3,1},{4,6},{5,7},{6,4},{7,5},{8,10},{9,11},{10,... | collective-permute-start | bytes 1216520 | tf_op jit(solution)/shard_map/ppermute | solution.py:101
  56.6 9.9 %collective-permute-start.16 = (bf16[2,24,4224]{2,1,0:T(8,128)(2,1)S(1)}, bf16[2,24,4224]{2,1,0:T(8,128)(2,1)S(1)}, u32[]{:S(2)}, u32[]{:S(2)}) collective-permute-start(bf16[2,24,4224]{2,1,0:T(8,128)(2,1)S(1)} %get-tuple-element.151), channel_id=1, source_target_pairs={{0,16},{16,0},{1,17},{17,1},{2,18},{18,2},{3,19},{19,3},{4,20},{20... | collective-permute-start | bytes 1216520 | tf_op jit(solution)/shard_map/ppermute | solution.py:101
  58.1 9.6 %collective-permute-start.17 = (bf16[2,24,4224]{2,1,0:T(8,128)(2,1)S(1)}, bf16[2,24,4224]{2,1,0:T(8,128)(2,1)S(1)}, u32[]{:S(2)}, u32[]{:S(2)}) collective-permute-start(bf16[2,24,4224]{2,1,0:T(8,128)(2,1)S(1)} %get-tuple-element.149), channel_id=1, source_target_pairs={{0,4},{1,5},{2,6},{3,7},{4,0},{5,1},{6,2},{7,3},{8,12},{9,13},{10,... | collective-permute-start | bytes 1216520 | tf_op jit(solution)/shard_map/ppermute | solution.py:101
  59.7 8.0 %collective-permute-start.18 = (bf16[2,96,4224]{2,1,0:T(8,128)(2,1)S(1)}, bf16[2,96,4224]{2,1,0:T(8,128)(2,1)S(1)}, u32[]{:S(2)}, u32[]{:S(2)}) collective-permute-start(bf16[2,96,4224]{2,1,0:T(8,128)(2,1)S(1)} %pad_maximum_fusion.2), channel_id=1, source_target_pairs={{0,1},{1,0},{2,3},{3,2},{4,5},{5,4},{6,7},{7,6},{8,9},{9,8},{10,11... | collective-permute-start | bytes 4866056 | tf_op jit(solution)/shard_map/ppermute | solution.py:101
  63.2 12.6 %collective-permute-start.21 = (bf16[4,24,4096]{2,1,0:T(8,128)(2,1)S(1)}, bf16[4,24,4096]{2,1,0:T(8,128)(2,1)S(1)}, u32[]{:S(2)}, u32[]{:S(2)}) collective-permute-start(bf16[4,24,4096]{2,1,0:T(8,128)(2,1)S(1)} %slice_bitcast_fusion.13), channel_id=1, source_target_pairs={{0,1},{1,0},{2,3},{3,2},{4,5},{5,4},{6,7},{7,6},{8,9},{9,8},{10,11... | collective-permute-start | bytes 2359304 | tf_op jit(solution)/shard_map/ppermute | solution.py:101
  68.3 7.5 %collective-permute-start.19 = (bf16[24,4224]{1,0:T(8,128)(2,1)S(1)}, bf16[24,4224]{1,0:T(8,128)(2,1)S(1)}, u32[]{:S(2)}, u32[]{:S(2)}) collective-permute-start(bf16[24,4224]{1,0:T(8,128)(2,1)S(1)} %get-tuple-element.134), channel_id=1, source_target_pairs={{0,2},{1,3},{2,0},{3,1},{4,6},{5,7},{6,4},{7,5},{8,10},{9,11},{10,... | collective-permute-start | bytes 608264 | tf_op jit(solution)/shard_map/ppermute | solution.py:101
  69.1 6.7 %collective-permute-start.20 = (bf16[24,4224]{1,0:T(8,128)(2,1)S(1)}, bf16[24,4224]{1,0:T(8,128)(2,1)S(1)}, u32[]{:S(2)}, u32[]{:S(2)}) collective-permute-start(bf16[24,4224]{1,0:T(8,128)(2,1)S(1)} %get-tuple-element.133), channel_id=1, source_target_pairs={{0,16},{16,0},{1,17},{17,1},{2,18},{18,2},{3,19},{19,3},{4,20},{20... | collective-permute-start | bytes 608264 | tf_op jit(solution)/shard_map/ppermute | solution.py:101
  77.0 9.6 %collective-permute-start.24 = (bf16[3,24,2048]{2,1,0:T(8,128)(2,1)S(1)}, bf16[3,24,2048]{2,1,0:T(8,128)(2,1)S(1)}, u32[]{:S(2)}, u32[]{:S(2)}) collective-permute-start(bf16[3,24,2048]{2,1,0:T(8,128)(2,1)S(1)} %pad_maximum_fusion.16), channel_id=1, source_target_pairs={{0,2},{1,3},{2,0},{3,1},{4,6},{5,7},{6,4},{7,5},{8,10},{9,11},{10,... | collective-permute-start | bytes 884744 | tf_op jit(solution)/shard_map/ppermute | solution.py:101
  78.4 8.7 %collective-permute-start.25 = (bf16[3,24,2048]{2,1,0:T(8,128)(2,1)S(1)}, bf16[3,24,2048]{2,1,0:T(8,128)(2,1)S(1)}, u32[]{:S(2)}, u32[]{:S(2)}) collective-permute-start(bf16[3,24,2048]{2,1,0:T(8,128)(2,1)S(1)} %pad_maximum_fusion.17), channel_id=1, source_target_pairs={{0,16},{16,0},{1,17},{17,1},{2,18},{18,2},{3,19},{19,3},{4,20},{20... | collective-permute-start | bytes 884744 | tf_op jit(solution)/shard_map/ppermute | solution.py:101
  80.0 7.1 %collective-permute-start.26 = (bf16[4,24,4096]{2,1,0:T(8,128)(2,1)S(1)}, bf16[4,24,4096]{2,1,0:T(8,128)(2,1)S(1)}, u32[]{:S(2)}, u32[]{:S(2)}) collective-permute-start(bf16[4,24,4096]{2,1,0:T(8,128)(2,1)S(1)} %slice_bitcast_fusion.11), channel_id=1, source_target_pairs={{0,1},{1,0},{2,3},{3,2},{4,5},{5,4},{6,7},{7,6},{8,9},{9,8},{10,11... | collective-permute-start | bytes 2359304 | tf_op jit(solution)/shard_map/ppermute | solution.py:101
  87.2 27.0 %collective-permute-start.27 = (bf16[24,4096]{1,0:T(8,128)(2,1)S(1)}, bf16[24,4096]{1,0:T(8,128)(2,1)S(1)}, u32[]{:S(2)}, u32[]{:S(2)}) collective-permute-start(bf16[24,4096]{1,0:T(8,128)(2,1)S(1)} %pad_maximum_fusion.18), channel_id=1, source_target_pairs={{0,4},{1,5},{2,6},{3,7},{4,0},{5,1},{6,2},{7,3},{8,12},{9,13},{10,... | collective-permute-start | bytes 589832 | tf_op jit(solution)/shard_map/ppermute | solution.py:101
  91.5 13.7 %collective-permute-start.29 = (bf16[2,24,2048]{2,1,0:T(8,128)(2,1)S(1)}, bf16[2,24,2048]{2,1,0:T(8,128)(2,1)S(1)}, u32[]{:S(2)}, u32[]{:S(2)}) collective-permute-start(bf16[2,24,2048]{2,1,0:T(8,128)(2,1)S(1)} %pad_maximum_fusion.19), channel_id=1, source_target_pairs={{0,16},{16,0},{1,17},{17,1},{2,18},{18,2},{3,19},{19,3},{4,20},{20... | collective-permute-start | bytes 589832 | tf_op jit(solution)/shard_map/ppermute | solution.py:101
  93.8 11.5 %collective-permute-start.34 = (bf16[2,24,2048]{2,1,0:T(8,128)(2,1)S(1)}, bf16[2,24,2048]{2,1,0:T(8,128)(2,1)S(1)}, u32[]{:S(2)}, u32[]{:S(2)}) collective-permute-start(bf16[2,24,2048]{2,1,0:T(8,128)(2,1)S(1)} %pad_maximum_fusion.22), channel_id=1, source_target_pairs={{0,2},{1,3},{2,0},{3,1},{4,6},{5,7},{6,4},{7,5},{8,10},{9,11},{10,... | collective-permute-start | bytes 589832 | tf_op jit(solution)/shard_map/ppermute | solution.py:101
  107.0 7.2 %collective-permute-start.33 = (bf16[24,4096]{1,0:T(8,128)(2,1)S(1)}, bf16[24,4096]{1,0:T(8,128)(2,1)S(1)}, u32[]{:S(2)}, u32[]{:S(2)}) collective-permute-start(bf16[24,4096]{1,0:T(8,128)(2,1)S(1)} %pad_maximum_fusion.21), channel_id=1, source_target_pairs={{0,2},{1,3},{2,0},{3,1},{4,6},{5,7},{6,4},{7,5},{8,10},{9,11},{10,... | collective-permute-start | bytes 589832 | tf_op jit(solution)/shard_map/ppermute | solution.py:101
  107.6 6.6 %collective-permute-start.35 = (bf16[24,4096]{1,0:T(8,128)(2,1)S(1)}, bf16[24,4096]{1,0:T(8,128)(2,1)S(1)}, u32[]{:S(2)}, u32[]{:S(2)}) collective-permute-start(bf16[24,4096]{1,0:T(8,128)(2,1)S(1)} %pad_maximum_fusion.23), channel_id=1, source_target_pairs={{0,16},{16,0},{1,17},{17,1},{2,18},{18,2},{3,19},{19,3},{4,20},{20... | collective-permute-start | bytes 589832 | tf_op jit(solution)/shard_map/ppermute | solution.py:101
  115.1 9.0 %collective-permute-start.40 = (bf16[24,4096]{1,0:T(8,128)(2,1)S(1)}, bf16[24,4096]{1,0:T(8,128)(2,1)S(1)}, u32[]{:S(2)}, u32[]{:S(2)}) collective-permute-start(bf16[24,4096]{1,0:T(8,128)(2,1)S(1)} %add_convert_fusion.1), channel_id=1, source_target_pairs={{0,8},{1,9},{2,10},{3,11},{4,12},{5,13},{6,14},{7,15},{8,0},{9,1},... | collective-permute-start | bytes 589832 | tf_op jit(solution)/shard_map/ppermute | solution.py:101
  115.9 8.2 %collective-permute-start.39 = (bf16[24,4096]{1,0:T(8,128)(2,1)S(1)}, bf16[24,4096]{1,0:T(8,128)(2,1)S(1)}, u32[]{:S(2)}, u32[]{:S(2)}) collective-permute-start(bf16[24,4096]{1,0:T(8,128)(2,1)S(1)} %pad_maximum_fusion.27), channel_id=1, source_target_pairs={{0,4},{1,5},{2,6},{3,7},{4,0},{5,1},{6,2},{7,3},{8,12},{9,13},{10,... | collective-permute-start | bytes 589832 | tf_op jit(solution)/shard_map/ppermute | solution.py:101
  116.6 7.5 %collective-permute-start.38 = (bf16[24,4096]{1,0:T(8,128)(2,1)S(1)}, bf16[24,4096]{1,0:T(8,128)(2,1)S(1)}, u32[]{:S(2)}, u32[]{:S(2)}) collective-permute-start(bf16[24,4096]{1,0:T(8,128)(2,1)S(1)} %pad_maximum_fusion.26), channel_id=1, source_target_pairs={{0,16},{16,0},{1,17},{17,1},{2,18},{18,2},{3,19},{19,3},{4,20},{20... | collective-permute-start | bytes 589832 | tf_op jit(solution)/shard_map/ppermute | solution.py:101
  117.6 6.5 %collective-permute-start.37 = (bf16[24,4096]{1,0:T(8,128)(2,1)S(1)}, bf16[24,4096]{1,0:T(8,128)(2,1)S(1)}, u32[]{:S(2)}, u32[]{:S(2)}) collective-permute-start(bf16[24,4096]{1,0:T(8,128)(2,1)S(1)} %pad_maximum_fusion.25), channel_id=1, source_target_pairs={{0,2},{1,3},{2,0},{3,1},{4,6},{5,7},{6,4},{7,5},{8,10},{9,11},{10,... | collective-permute-start | bytes 589832 | tf_op jit(solution)/shard_map/ppermute | solution.py:101
  (20 other events, 159.6 us)

commit v6 on v5

--- a/solution.py
+++ b/solution.py
@@ -213,7 +213,7 @@
     near2 = near_of(distant, *first2)
     near2_other = over_core(near2)
     part_far, kept_far = expert_rows(far, far_other)
-    second2, near2_other, part_far = together((second2, near2_other, part_far))
+    second2, part_far = together((second2, part_far))
     third2 = thirds(second2[2])
     others = over_core(part_near[1]), over_core(part_far[1])
     part_near2, kept_near2 = expert_rows(near2, near2_other)

time: 125 us -> 125 us (level)
  transfers between devices with their start and end apart: 41 -> 41, of which waited for: 18 -> 17; matrix products, arithmetic and copies ran while one was open for 36% -> 37% of each run, Pallas kernels for 0% -> 0%
where the time goes in v6:
time: 125 us; the launch traced here: 124 us
  starting transfers between devices  39.2 us (31%)
  matrix products  35.1 us (28%)
  waiting for transfers between devices  29.9 us (24%)
  local copies, waits for them, and re-layouts  12.2 us (10%)
  other arithmetic  6.28 us (5%)
  between operations  1.61 us (1%)
    ppermute x41, starting transfers between devices, swapped(): return lax.ppermute(x, axis, [(i, i ^ bits) for i in range(count)])  39.2 us
    ppermute x41, waiting for transfers between devices, swapped(): return lax.ppermute(x, axis, [(i, i ^ bits) for i in range(count)])  29.9 us
    dot_general x3, matrix products, weight_grad(): jnp.einsum('rf,rd->fd', rows_of(*(held[at] for held in kept)), rows_of(*(...  12.1 us
    unnamed x30, local copies, waits for them, and re-layouts  5.4 us
    dot_general x4, matrix products, expert_rows(): jnp.einsum('rd,fd->rf', x_rows, up_w, preferred_element_type=jnp.float32)  5.01 us
    dot_general x4, matrix products, expert_rows(): jnp.einsum('rd,fd->rf', g_rows, down_w, preferred_element_type=jnp.float32)  4.79 us
    dot_general x4, matrix products, expert_rows(): jnp.einsum('rd,fd->rf', x_rows, gate_w, preferred_element_type=jnp.float32)  4.72 us
    dot_general x4, matrix products, expert_rows(): jnp.einsum('rf,fd->rd', d_up_act, up_w, preferred_element_type=jnp.float32)  4.36 us
  transfers between devices with their start and end apart: 41, of which 17 were waited for; matrix products, arithmetic and copies ran while one was open for 37% of the time, Pallas kernels for 0%

profile of v6, /device:TPU:0, one launch (start us, length us, event | category | flops | bytes accessed | tf_op | source)
XLA Modules:
  0.0 124.3 jit_solution(5919227760604792302)
XLA Ops:
  0.6 4.1 %collective-permute-start.8 = (bf16[24,4096]{1,0:T(8,128)(2,1)}, bf16[24,4096]{1,0:T(8,128)(2,1)}, u32[]{:S(2)}, u32[]{:S(2)}) collective-permute-start(bf16[24,4096]{1,0:T(8,128)(2,1)} %param.7), channel_id=1, source_target_pairs={{0,8},{1,9},{2,10},{3,11},{4,12},{5,13},{6,14},{7,15},{8,0},{9,1},... | collective-permute-start | bytes 589832 | tf_op jit(solution)/shard_map/ppermute | solution.py:101
  6.7 1.6 %collective-permute-start = (bf16[2,24,4224]{2,1,0:T(8,128)(2,1)S(1)}, bf16[2,24,4224]{2,1,0:T(8,128)(2,1)}, u32[]{:S(2)}, u32[]{:S(2)}) collective-permute-start(bf16[2,24,4224]{2,1,0:T(8,128)(2,1)S(1)} %pad_maximum_fusion.12), channel_id=1, source_target_pairs={{0,4},{1,5},{2,6},{3,7},{4,0},{5,1},{6,2},{7,3},{8,12},{9,13},{10,... | collective-permute-start | bytes 1216520 | tf_op jit(solution)/shard_map/ppermute | solution.py:101
  8.3 1.5 %collective-permute-start.1 = (bf16[2,24,4224]{2,1,0:T(8,128)(2,1)S(1)}, bf16[2,24,4224]{2,1,0:T(8,128)(2,1)}, u32[]{:S(2)}, u32[]{:S(2)}) collective-permute-start(bf16[2,24,4224]{2,1,0:T(8,128)(2,1)S(1)} %pad_maximum_fusion.12), channel_id=1, source_target_pairs={{0,2},{1,3},{2,0},{3,1},{4,6},{5,7},{6,4},{7,5},{8,10},{9,11},{10,... | collective-permute-start | bytes 1216520 | tf_op jit(solution)/shard_map/ppermute | solution.py:101
  9.8 1.5 %collective-permute-start.2 = (bf16[2,24,4224]{2,1,0:T(8,128)(2,1)S(1)}, bf16[2,24,4224]{2,1,0:T(8,128)(2,1)}, u32[]{:S(2)}, u32[]{:S(2)}) collective-permute-start(bf16[2,24,4224]{2,1,0:T(8,128)(2,1)S(1)} %pad_maximum_fusion.12), channel_id=1, source_target_pairs={{0,16},{16,0},{1,17},{17,1},{2,18},{18,2},{3,19},{19,3},{4,20},{20... | collective-permute-start | bytes 1216520 | tf_op jit(solution)/shard_map/ppermute | solution.py:101
  11.3 3.0 %collective-permute-done.8 = bf16[24,4096]{1,0:T(8,128)(2,1)} collective-permute-done((bf16[24,4096]{1,0:T(8,128)(2,1)}, bf16[24,4096]{1,0:T(8,128)(2,1)}, u32[]{:S(2)}, u32[]{:S(2)}) %collective-permute-start.8) | collective-permute-done | bytes 196640 | tf_op jit(solution)/shard_map/ppermute | solution.py:101
  14.4 4.5 %collective-permute-done.1 = bf16[2,24,4224]{2,1,0:T(8,128)(2,1)} collective-permute-done((bf16[2,24,4224]{2,1,0:T(8,128)(2,1)S(1)}, bf16[2,24,4224]{2,1,0:T(8,128)(2,1)}, u32[]{:S(2)}, u32[]{:S(2)}) %collective-permute-start.1) | collective-permute-done | bytes 405536 | tf_op jit(solution)/shard_map/ppermute | solution.py:101
  22.7 1.6 %collective-permute-start.4 = (bf16[24,4224]{1,0:T(8,128)(2,1)S(1)}, bf16[24,4224]{1,0:T(8,128)(2,1)S(1)}, u32[]{:S(2)}, u32[]{:S(2)}) collective-permute-start(bf16[24,4224]{1,0:T(8,128)(2,1)S(1)} %slice_bitcast_fusion.27), channel_id=1, source_target_pairs={{0,16},{16,0},{1,17},{17,1},{2,18},{18,2},{3,19},{19,3},{4,20},{20... | collective-permute-start | bytes 608264 | tf_op jit(solution)/shard_map/ppermute | solution.py:101
  26.9 1.5 %collective-permute-done.4 = bf16[24,4224]{1,0:T(8,128)(2,1)S(1)} collective-permute-done((bf16[24,4224]{1,0:T(8,128)(2,1)S(1)}, bf16[24,4224]{1,0:T(8,128)(2,1)S(1)}, u32[]{:S(2)}, u32[]{:S(2)}) %collective-permute-start.4) | collective-permute-done | bytes 202784 | tf_op jit(solution)/shard_map/ppermute | solution.py:101
  28.5 1.5 %collective-permute-start.5 = (bf16[2,24,4224]{2,1,0:T(8,128)(2,1)}, bf16[2,24,4224]{2,1,0:T(8,128)(2,1)S(1)}, u32[]{:S(2)}, u32[]{:S(2)}) collective-permute-start(bf16[2,24,4224]{2,1,0:T(8,128)(2,1)} %collective-permute-done), channel_id=1, source_target_pairs={{0,2},{1,3},{2,0},{3,1},{4,6},{5,7},{6,4},{7,5},{8,10},{9,11},{10,... | collective-permute-start | bytes 1216520 | tf_op jit(solution)/shard_map/ppermute | solution.py:101
  30.0 1.5 %collective-permute-start.6 = (bf16[2,24,4224]{2,1,0:T(8,128)(2,1)}, bf16[2,24,4224]{2,1,0:T(8,128)(2,1)S(1)}, u32[]{:S(2)}, u32[]{:S(2)}) collective-permute-start(bf16[2,24,4224]{2,1,0:T(8,128)(2,1)} %collective-permute-done), channel_id=1, source_target_pairs={{0,16},{16,0},{1,17},{17,1},{2,18},{18,2},{3,19},{19,3},{4,20},{20... | collective-permute-start | bytes 1216520 | tf_op jit(solution)/shard_map/ppermute | solution.py:101
  33.3 3.6 %collective-permute-done.5 = bf16[2,24,4224]{2,1,0:T(8,128)(2,1)S(1)} collective-permute-done((bf16[2,24,4224]{2,1,0:T(8,128)(2,1)}, bf16[2,24,4224]{2,1,0:T(8,128)(2,1)S(1)}, u32[]{:S(2)}, u32[]{:S(2)}) %collective-permute-start.5) | collective-permute-done | bytes 405536 | tf_op jit(solution)/shard_map/ppermute | solution.py:101
  38.1 1.4 %collective-permute-done.7 = bf16[2,24,4224]{2,1,0:T(8,128)(2,1)S(1)} collective-permute-done((bf16[2,24,4224]{2,1,0:T(8,128)(2,1)S(1)}, bf16[2,24,4224]{2,1,0:T(8,128)(2,1)S(1)}, u32[]{:S(2)}, u32[]{:S(2)}) %collective-permute-start.7) | collective-permute-done | bytes 405536 | tf_op jit(solution)/shard_map/ppermute | solution.py:101
  43.4 1.6 %copy-done.1 = bf16[1,384,4096]{2,1,0:T(8,128)(2,1)S(1)} copy-done((bf16[1,384,4096]{2,1,0:T(8,128)(2,1)S(1)}, bf16[1,384,4096]{2,1,0:T(8,128)(2,1)}, u32[]{:S(2)}) %copy-start.1) | copy-done | bytes 3145752
  48.1 1.3 %multiply_convert_fusion.3 = (bf16[192,384]{1,0:T(8,128)(2,1)S(1)}, bf16[192,384]{1,0:T(8,128)(2,1)S(1)}, bf16[192,384]{1,0:T(8,128)(2,1)S(1)}) fusion(f32[192]{0:T(256)S(1)} %select_reduce_fusion.3, f32[192,384]{1,0:T(8,128)S(1)} %fusion.34, f32[192,384]{1,0:T(8,128)S(1)} %fusion.56, bf16[192,4096]{1,0:T(8,128)(2,1)S(1)} %pad_maximum_fusion.6, ...), kind=kOutput, calls=%fused_computation.160 | convolution fusion | flops 605159424 | bytes 5751552 | tf_op jit(solution)/shard_map/rd,fd->rf/dot_general | solution.py:148
  55.1 1.3 %collective-permute-start.15 = (bf16[2,24,4224]{2,1,0:T(8,128)(2,1)S(1)}, bf16[2,24,4224]{2,1,0:T(8,128)(2,1)S(1)}, u32[]{:S(2)}, u32[]{:S(2)}) collective-permute-start(bf16[2,24,4224]{2,1,0:T(8,128)(2,1)S(1)} %get-tuple-element.150), channel_id=1, source_target_pairs={{0,2},{1,3},{2,0},{3,1},{4,6},{5,7},{6,4},{7,5},{8,10},{9,11},{10,... | collective-permute-start | bytes 1216520 | tf_op jit(solution)/shard_map/ppermute | solution.py:101
  56.4 1.5 %collective-permute-start.16 = (bf16[2,24,4224]{2,1,0:T(8,128)(2,1)S(1)}, bf16[2,24,4224]{2,1,0:T(8,128)(2,1)S(1)}, u32[]{:S(2)}, u32[]{:S(2)}) collective-permute-start(bf16[2,24,4224]{2,1,0:T(8,128)(2,1)S(1)} %get-tuple-element.151), channel_id=1, source_target_pairs={{0,16},{16,0},{1,17},{17,1},{2,18},{18,2},{3,19},{19,3},{4,20},{20... | collective-permute-start | bytes 1216520 | tf_op jit(solution)/shard_map/ppermute | solution.py:101
  57.9 1.6 %collective-permute-start.17 = (bf16[2,24,4224]{2,1,0:T(8,128)(2,1)S(1)}, bf16[2,24,4224]{2,1,0:T(8,128)(2,1)S(1)}, u32[]{:S(2)}, u32[]{:S(2)}) collective-permute-start(bf16[2,24,4224]{2,1,0:T(8,128)(2,1)S(1)} %get-tuple-element.149), channel_id=1, source_target_pairs={{0,4},{1,5},{2,6},{3,7},{4,0},{5,1},{6,2},{7,3},{8,12},{9,13},{10,... | collective-permute-start | bytes 1216520 | tf_op jit(solution)/shard_map/ppermute | solution.py:101
  61.6 1.4 %collective-permute-done.22 = bf16[2,96,4224]{2,1,0:T(8,128)(2,1)S(1)} collective-permute-done((bf16[2,96,4224]{2,1,0:T(8,128)(2,1)S(1)}, bf16[2,96,4224]{2,1,0:T(8,128)(2,1)S(1)}, u32[]{:S(2)}, u32[]{:S(2)}) %collective-permute-start.22) | collective-permute-done | bytes 1622048 | tf_op jit(solution)/shard_map/ppermute | solution.py:101
  71.8 1.3 %multiply_convert_fusion.1 = (bf16[192,384]{1,0:T(8,128)(2,1)S(1)}, bf16[192,384]{1,0:T(8,128)(2,1)S(1)}, bf16[192,384]{1,0:T(8,128)(2,1)S(1)}) fusion(f32[192]{0:T(256)S(1)} %get-tuple-element.86, f32[192,384]{1,0:T(8,128)S(1)} %fusion.26, f32[192,384]{1,0:T(8,128)S(1)} %fusion.62, bf16[192,4096]{1,0:T(8,128)(2,1)S(1)} %pad_maximum_fusion.4, ...), kind=kOutput, calls=%fused_computation.158 | convolution fusion | flops 605159424 | bytes 5751552 | tf_op jit(solution)/shard_map/rd,fd->rf/dot_general | solution.py:148
  76.4 1.3 %collective-permute-start.24 = (bf16[3,24,2048]{2,1,0:T(8,128)(2,1)S(1)}, bf16[3,24,2048]{2,1,0:T(8,128)(2,1)S(1)}, u32[]{:S(2)}, u32[]{:S(2)}) collective-permute-start(bf16[3,24,2048]{2,1,0:T(8,128)(2,1)S(1)} %pad_maximum_fusion.16), channel_id=1, source_target_pairs={{0,2},{1,3},{2,0},{3,1},{4,6},{5,7},{6,4},{7,5},{8,10},{9,11},{10,... | collective-permute-start | bytes 884744 | tf_op jit(solution)/shard_map/ppermute | solution.py:101
  77.8 1.6 %collective-permute-start.25 = (bf16[3,24,2048]{2,1,0:T(8,128)(2,1)S(1)}, bf16[3,24,2048]{2,1,0:T(8,128)(2,1)S(1)}, u32[]{:S(2)}, u32[]{:S(2)}) collective-permute-start(bf16[3,24,2048]{2,1,0:T(8,128)(2,1)S(1)} %pad_maximum_fusion.17), channel_id=1, source_target_pairs={{0,16},{16,0},{1,17},{17,1},{2,18},{18,2},{3,19},{19,3},{4,20},{20... | collective-permute-start | bytes 884744 | tf_op jit(solution)/shard_map/ppermute | solution.py:101
  86.6 1.6 %collective-permute-start.27 = (bf16[24,4096]{1,0:T(8,128)(2,1)S(1)}, bf16[24,4096]{1,0:T(8,128)(2,1)S(1)}, u32[]{:S(2)}, u32[]{:S(2)}) collective-permute-start(bf16[24,4096]{1,0:T(8,128)(2,1)S(1)} %pad_maximum_fusion.18), channel_id=1, source_target_pairs={{0,4},{1,5},{2,6},{3,7},{4,0},{5,1},{6,2},{7,3},{8,12},{9,13},{10,... | collective-permute-start | bytes 589832 | tf_op jit(solution)/shard_map/ppermute | solution.py:101
  88.8 1.9 %collective-permute-done.28 = bf16[4,24,4096]{2,1,0:T(8,128)(2,1)S(1)} collective-permute-done((bf16[4,24,4096]{2,1,0:T(8,128)(2,1)S(1)}, bf16[4,24,4096]{2,1,0:T(8,128)(2,1)S(1)}, u32[]{:S(2)}, u32[]{:S(2)}) %collective-permute-start.28) | collective-permute-done | bytes 786464 | tf_op jit(solution)/shard_map/ppermute | solution.py:101
  90.9 1.6 %collective-permute-start.29 = (bf16[2,24,2048]{2,1,0:T(8,128)(2,1)S(1)}, bf16[2,24,2048]{2,1,0:T(8,128)(2,1)S(1)}, u32[]{:S(2)}, u32[]{:S(2)}) collective-permute-start(bf16[2,24,2048]{2,1,0:T(8,128)(2,1)S(1)} %pad_maximum_fusion.19), channel_id=1, source_target_pairs={{0,16},{16,0},{1,17},{17,1},{2,18},{18,2},{3,19},{19,3},{4,20},{20... | collective-permute-start | bytes 589832 | tf_op jit(solution)/shard_map/ppermute | solution.py:101
  93.2 1.6 %collective-permute-start.34 = (bf16[2,24,2048]{2,1,0:T(8,128)(2,1)S(1)}, bf16[2,24,2048]{2,1,0:T(8,128)(2,1)S(1)}, u32[]{:S(2)}, u32[]{:S(2)}) collective-permute-start(bf16[2,24,2048]{2,1,0:T(8,128)(2,1)S(1)} %pad_maximum_fusion.22), channel_id=1, source_target_pairs={{0,2},{1,3},{2,0},{3,1},{4,6},{5,7},{6,4},{7,5},{8,10},{9,11},{10,... | collective-permute-start | bytes 589832 | tf_op jit(solution)/shard_map/ppermute | solution.py:101
  95.2 3.1 %collective-permute-done.31 = bf16[24,2048]{1,0:T(8,128)(2,1)S(1)} collective-permute-done((bf16[24,2048]{1,0:T(8,128)(2,1)S(1)}, bf16[24,2048]{1,0:T(8,128)(2,1)S(1)}, u32[]{:S(2)}, u32[]{:S(2)}) %collective-permute-start.31) | collective-permute-done | bytes 98336 | tf_op jit(solution)/shard_map/ppermute | solution.py:101
  98.3 1.7 %collective-permute-done.30 = bf16[24,2048]{1,0:T(8,128)(2,1)S(1)} collective-permute-done((bf16[24,2048]{1,0:T(8,128)(2,1)S(1)}, bf16[24,2048]{1,0:T(8,128)(2,1)S(1)}, u32[]{:S(2)}, u32[]{:S(2)}) %collective-permute-start.30) | collective-permute-done | bytes 98336 | tf_op jit(solution)/shard_map/ppermute | solution.py:101
  100.6 4.0 %fusion.11 = bf16[1,384,4096]{2,1,0:T(8,128)(2,1)} fusion(bf16[192,4096]{1,0:T(8,128)(2,1)S(1)} %slice.545, bf16[192,4096]{1,0:T(8,128)(2,1)S(1)} %pad_maximum_fusion.4, bf16[192,4096]{1,0:T(8,128)(2,1)S(1)} %slice.536, bf16[192,4096]{1,0:T(8,128)(2,1)S(1)} %pad_maximum_fusion.6, bf16[192,384]{1,0:T(8,128)(2,1)S(1)} %get-tuple-element.125, ...), kind=kOutput, calls=%fused_computation.16 | convolution fusion | flops 2445017088 | bytes 10027008 | tf_op jit(solution)/shard_map/rf,rd->fd/dot_general | solution.py:273
  104.7 1.6 %collective-permute-done.32 = bf16[24,4096]{1,0:T(8,128)(2,1)S(1)} collective-permute-done((bf16[24,4096]{1,0:T(8,128)(2,1)S(1)}, bf16[24,4096]{1,0:T(8,128)(2,1)S(1)}, u32[]{:S(2)}, u32[]{:S(2)}) %collective-permute-start.32) | collective-permute-done | bytes 196640 | tf_op jit(solution)/shard_map/ppermute | solution.py:101
  107.1 1.6 %collective-permute-start.35 = (bf16[24,4096]{1,0:T(8,128)(2,1)S(1)}, bf16[24,4096]{1,0:T(8,128)(2,1)S(1)}, u32[]{:S(2)}, u32[]{:S(2)}) collective-permute-start(bf16[24,4096]{1,0:T(8,128)(2,1)S(1)} %pad_maximum_fusion.23), channel_id=1, source_target_pairs={{0,16},{16,0},{1,17},{17,1},{2,18},{18,2},{3,19},{19,3},{4,20},{20... | collective-permute-start | bytes 589832 | tf_op jit(solution)/shard_map/ppermute | solution.py:101
  109.4 4.0 %fusion.12 = bf16[1,384,4096]{2,1,0:T(8,128)(2,1)} fusion(bf16[192,4096]{1,0:T(8,128)(2,1)S(1)} %slice.545, bf16[192,4096]{1,0:T(8,128)(2,1)S(1)} %pad_maximum_fusion.4, bf16[192,4096]{1,0:T(8,128)(2,1)S(1)} %slice.536, bf16[192,4096]{1,0:T(8,128)(2,1)S(1)} %pad_maximum_fusion.6, bf16[192,384]{1,0:T(8,128)(2,1)S(1)} %get-tuple-element.126, ...), kind=kOutput, calls=%fused_computation.17 | convolution fusion | flops 2445017088 | bytes 10027008 | tf_op jit(solution)/shard_map/rf,rd->fd/dot_general | solution.py:273
  118.2 4.0 %fusion.13 = bf16[1,384,4096]{2,1,0:T(8,128)(2,1)} fusion(bf16[192,4096]{1,0:T(8,128)(2,1)S(1)} %slice.543, bf16[192,4096]{1,0:T(8,128)(2,1)S(1)} %pad_maximum_fusion.5, bf16[192,4096]{1,0:T(8,128)(2,1)S(1)} %slice.535, bf16[192,4096]{1,0:T(8,128)(2,1)S(1)} %pad_maximum_fusion.7, bf16[192,384]{1,0:T(8,128)(2,1)S(1)} %get-tuple-element.124, ...), kind=kOutput, calls=%fused_computation.18 | convolution fusion | flops 2445017088 | bytes 10027008 | tf_op jit(solution)/shard_map/rf,rd->fd/dot_general | solution.py:273
  (194 shorter events, 55.6 us)
Async XLA Ops:
  0.6 13.6 %collective-permute-start.8 = (bf16[24,4096]{1,0:T(8,128)(2,1)}, bf16[24,4096]{1,0:T(8,128)(2,1)}, u32[]{:S(2)}, u32[]{:S(2)}) collective-permute-start(bf16[24,4096]{1,0:T(8,128)(2,1)} %param.7), channel_id=1, source_target_pairs={{0,8},{1,9},{2,10},{3,11},{4,12},{5,13},{6,14},{7,15},{8,0},{9,1},... | collective-permute-start | bytes 589832 | tf_op jit(solution)/shard_map/ppermute | solution.py:101
  6.7 19.7 %collective-permute-start = (bf16[2,24,4224]{2,1,0:T(8,128)(2,1)S(1)}, bf16[2,24,4224]{2,1,0:T(8,128)(2,1)}, u32[]{:S(2)}, u32[]{:S(2)}) collective-permute-start(bf16[2,24,4224]{2,1,0:T(8,128)(2,1)S(1)} %pad_maximum_fusion.12), channel_id=1, source_target_pairs={{0,4},{1,5},{2,6},{3,7},{4,0},{5,1},{6,2},{7,3},{8,12},{9,13},{10,... | collective-permute-start | bytes 1216520 | tf_op jit(solution)/shard_map/ppermute | solution.py:101
  8.3 10.7 %collective-permute-start.1 = (bf16[2,24,4224]{2,1,0:T(8,128)(2,1)S(1)}, bf16[2,24,4224]{2,1,0:T(8,128)(2,1)}, u32[]{:S(2)}, u32[]{:S(2)}) collective-permute-start(bf16[2,24,4224]{2,1,0:T(8,128)(2,1)S(1)} %pad_maximum_fusion.12), channel_id=1, source_target_pairs={{0,2},{1,3},{2,0},{3,1},{4,6},{5,7},{6,4},{7,5},{8,10},{9,11},{10,... | collective-permute-start | bytes 1216520 | tf_op jit(solution)/shard_map/ppermute | solution.py:101
  9.8 10.4 %collective-permute-start.2 = (bf16[2,24,4224]{2,1,0:T(8,128)(2,1)S(1)}, bf16[2,24,4224]{2,1,0:T(8,128)(2,1)}, u32[]{:S(2)}, u32[]{:S(2)}) collective-permute-start(bf16[2,24,4224]{2,1,0:T(8,128)(2,1)S(1)} %pad_maximum_fusion.12), channel_id=1, source_target_pairs={{0,16},{16,0},{1,17},{17,1},{2,18},{18,2},{3,19},{19,3},{4,20},{20... | collective-permute-start | bytes 1216520 | tf_op jit(solution)/shard_map/ppermute | solution.py:101
  14.3 19.0 %collective-permute-start.10 = (bf16[24,4224]{1,0:T(8,128)(2,1)S(1)}, bf16[24,4224]{1,0:T(8,128)(2,1)S(1)}, u32[]{:S(2)}, u32[]{:S(2)}) collective-permute-start(bf16[24,4224]{1,0:T(8,128)(2,1)S(1)} %slice_bitcast_fusion.26), channel_id=1, source_target_pairs={{0,8},{1,9},{2,10},{3,11},{4,12},{5,13},{6,14},{7,15},{8,0},{9,1},... | collective-permute-start | bytes 608264 | tf_op jit(solution)/shard_map/ppermute | solution.py:101
  28.5 8.5 %collective-permute-start.5 = (bf16[2,24,4224]{2,1,0:T(8,128)(2,1)}, bf16[2,24,4224]{2,1,0:T(8,128)(2,1)S(1)}, u32[]{:S(2)}, u32[]{:S(2)}) collective-permute-start(bf16[2,24,4224]{2,1,0:T(8,128)(2,1)} %collective-permute-done), channel_id=1, source_target_pairs={{0,2},{1,3},{2,0},{3,1},{4,6},{5,7},{6,4},{7,5},{8,10},{9,11},{10,... | collective-permute-start | bytes 1216520 | tf_op jit(solution)/shard_map/ppermute | solution.py:101
  30.0 8.1 %collective-permute-start.6 = (bf16[2,24,4224]{2,1,0:T(8,128)(2,1)}, bf16[2,24,4224]{2,1,0:T(8,128)(2,1)S(1)}, u32[]{:S(2)}, u32[]{:S(2)}) collective-permute-start(bf16[2,24,4224]{2,1,0:T(8,128)(2,1)} %collective-permute-done), channel_id=1, source_target_pairs={{0,16},{16,0},{1,17},{17,1},{2,18},{18,2},{3,19},{19,3},{4,20},{20... | collective-permute-start | bytes 1216520 | tf_op jit(solution)/shard_map/ppermute | solution.py:101
  31.6 8.0 %collective-permute-start.7 = (bf16[2,24,4224]{2,1,0:T(8,128)(2,1)S(1)}, bf16[2,24,4224]{2,1,0:T(8,128)(2,1)S(1)}, u32[]{:S(2)}, u32[]{:S(2)}) collective-permute-start(bf16[2,24,4224]{2,1,0:T(8,128)(2,1)S(1)} %pad_maximum_fusion.13), channel_id=1, source_target_pairs={{0,4},{1,5},{2,6},{3,7},{4,0},{5,1},{6,2},{7,3},{8,12},{9,13},{10,... | collective-permute-start | bytes 1216520 | tf_op jit(solution)/shard_map/ppermute | solution.py:101
  33.1 6.4 %collective-permute-start.9 = (bf16[2,96,4224]{2,1,0:T(8,128)(2,1)S(1)}, bf16[2,96,4224]{2,1,0:T(8,128)(2,1)S(1)}, u32[]{:S(2)}, u32[]{:S(2)}) collective-permute-start(bf16[2,96,4224]{2,1,0:T(8,128)(2,1)S(1)} %constant_dynamic-update-slice_fusion), channel_id=1, source_target_pairs={{0,1},{1,0},{2,3},{3,2},{4,5},{5,4},{6,7},{7,6},{8,9},{9,8},{10,11... | collective-permute-start | bytes 4866056 | tf_op jit(solution)/shard_map/ppermute | solution.py:101
  40.5 11.0 %collective-permute-start.11 = (bf16[2,24,4224]{2,1,0:T(8,128)(2,1)S(1)}, bf16[2,24,4224]{2,1,0:T(8,128)(2,1)S(1)}, u32[]{:S(2)}, u32[]{:S(2)}) collective-permute-start(bf16[2,24,4224]{2,1,0:T(8,128)(2,1)S(1)} %pad_maximum_fusion.14), channel_id=1, source_target_pairs={{0,2},{1,3},{2,0},{3,1},{4,6},{5,7},{6,4},{7,5},{8,10},{9,11},{10,... | collective-permute-start | bytes 1216520 | tf_op jit(solution)/shard_map/ppermute | solution.py:101
  41.1 10.4 %collective-permute-start.12 = (bf16[2,24,4224]{2,1,0:T(8,128)(2,1)S(1)}, bf16[2,24,4224]{2,1,0:T(8,128)(2,1)S(1)}, u32[]{:S(2)}, u32[]{:S(2)}) collective-permute-start(bf16[2,24,4224]{2,1,0:T(8,128)(2,1)S(1)} %pad_maximum_fusion.14), channel_id=1, source_target_pairs={{0,16},{16,0},{1,17},{17,1},{2,18},{18,2},{3,19},{19,3},{4,20},{20... | collective-permute-start | bytes 1216520 | tf_op jit(solution)/shard_map/ppermute | solution.py:101
  41.6 10.0 %collective-permute-start.13 = (bf16[2,24,4224]{2,1,0:T(8,128)(2,1)S(1)}, bf16[2,24,4224]{2,1,0:T(8,128)(2,1)S(1)}, u32[]{:S(2)}, u32[]{:S(2)}) collective-permute-start(bf16[2,24,4224]{2,1,0:T(8,128)(2,1)S(1)} %pad_maximum_fusion.14), channel_id=1, source_target_pairs={{0,4},{1,5},{2,6},{3,7},{4,0},{5,1},{6,2},{7,3},{8,12},{9,13},{10,... | collective-permute-start | bytes 1216520 | tf_op jit(solution)/shard_map/ppermute | solution.py:101
  43.2 8.5 %collective-permute-start.14 = (bf16[2,96,4224]{2,1,0:T(8,128)(2,1)S(1)}, bf16[2,96,4224]{2,1,0:T(8,128)(2,1)S(1)}, u32[]{:S(2)}, u32[]{:S(2)}) collective-permute-start(bf16[2,96,4224]{2,1,0:T(8,128)(2,1)S(1)} %pad_maximum_fusion.1), channel_id=1, source_target_pairs={{0,1},{1,0},{2,3},{3,2},{4,5},{5,4},{6,7},{7,6},{8,9},{9,8},{10,11... | collective-permute-start | bytes 4866056 | tf_op jit(solution)/shard_map/ppermute | solution.py:101
  55.1 11.9 %collective-permute-start.15 = (bf16[2,24,4224]{2,1,0:T(8,128)(2,1)S(1)}, bf16[2,24,4224]{2,1,0:T(8,128)(2,1)S(1)}, u32[]{:S(2)}, u32[]{:S(2)}) collective-permute-start(bf16[2,24,4224]{2,1,0:T(8,128)(2,1)S(1)} %get-tuple-element.150), channel_id=1, source_target_pairs={{0,2},{1,3},{2,0},{3,1},{4,6},{5,7},{6,4},{7,5},{8,10},{9,11},{10,... | collective-permute-start | bytes 1216520 | tf_op jit(solution)/shard_map/ppermute | solution.py:101
  56.4 10.5 %collective-permute-start.16 = (bf16[2,24,4224]{2,1,0:T(8,128)(2,1)S(1)}, bf16[2,24,4224]{2,1,0:T(8,128)(2,1)S(1)}, u32[]{:S(2)}, u32[]{:S(2)}) collective-permute-start(bf16[2,24,4224]{2,1,0:T(8,128)(2,1)S(1)} %get-tuple-element.151), channel_id=1, source_target_pairs={{0,16},{16,0},{1,17},{17,1},{2,18},{18,2},{3,19},{19,3},{4,20},{20... | collective-permute-start | bytes 1216520 | tf_op jit(solution)/shard_map/ppermute | solution.py:101
  57.9 9.6 %collective-permute-start.17 = (bf16[2,24,4224]{2,1,0:T(8,128)(2,1)S(1)}, bf16[2,24,4224]{2,1,0:T(8,128)(2,1)S(1)}, u32[]{:S(2)}, u32[]{:S(2)}) collective-permute-start(bf16[2,24,4224]{2,1,0:T(8,128)(2,1)S(1)} %get-tuple-element.149), channel_id=1, source_target_pairs={{0,4},{1,5},{2,6},{3,7},{4,0},{5,1},{6,2},{7,3},{8,12},{9,13},{10,... | collective-permute-start | bytes 1216520 | tf_op jit(solution)/shard_map/ppermute | solution.py:101
  59.6 15.6 %collective-permute-start.20 = (bf16[4,24,4096]{2,1,0:T(8,128)(2,1)S(1)}, bf16[4,24,4096]{2,1,0:T(8,128)(2,1)S(1)}, u32[]{:S(2)}, u32[]{:S(2)}) collective-permute-start(bf16[4,24,4096]{2,1,0:T(8,128)(2,1)S(1)} %slice_bitcast_fusion.13), channel_id=1, source_target_pairs={{0,1},{1,0},{2,3},{3,2},{4,5},{5,4},{6,7},{7,6},{8,9},{9,8},{10,11... | collective-permute-start | bytes 2359304 | tf_op jit(solution)/shard_map/ppermute | solution.py:101
  67.7 7.5 %collective-permute-start.18 = (bf16[24,4224]{1,0:T(8,128)(2,1)S(1)}, bf16[24,4224]{1,0:T(8,128)(2,1)S(1)}, u32[]{:S(2)}, u32[]{:S(2)}) collective-permute-start(bf16[24,4224]{1,0:T(8,128)(2,1)S(1)} %get-tuple-element.134), channel_id=1, source_target_pairs={{0,2},{1,3},{2,0},{3,1},{4,6},{5,7},{6,4},{7,5},{8,10},{9,11},{10,... | collective-permute-start | bytes 608264 | tf_op jit(solution)/shard_map/ppermute | solution.py:101
  68.5 6.7 %collective-permute-start.19 = (bf16[24,4224]{1,0:T(8,128)(2,1)S(1)}, bf16[24,4224]{1,0:T(8,128)(2,1)S(1)}, u32[]{:S(2)}, u32[]{:S(2)}) collective-permute-start(bf16[24,4224]{1,0:T(8,128)(2,1)S(1)} %get-tuple-element.133), channel_id=1, source_target_pairs={{0,16},{16,0},{1,17},{17,1},{2,18},{18,2},{3,19},{19,3},{4,20},{20... | collective-permute-start | bytes 608264 | tf_op jit(solution)/shard_map/ppermute | solution.py:101
  76.4 9.6 %collective-permute-start.24 = (bf16[3,24,2048]{2,1,0:T(8,128)(2,1)S(1)}, bf16[3,24,2048]{2,1,0:T(8,128)(2,1)S(1)}, u32[]{:S(2)}, u32[]{:S(2)}) collective-permute-start(bf16[3,24,2048]{2,1,0:T(8,128)(2,1)S(1)} %pad_maximum_fusion.16), channel_id=1, source_target_pairs={{0,2},{1,3},{2,0},{3,1},{4,6},{5,7},{6,4},{7,5},{8,10},{9,11},{10,... | collective-permute-start | bytes 884744 | tf_op jit(solution)/shard_map/ppermute | solution.py:101
  77.8 8.7 %collective-permute-start.25 = (bf16[3,24,2048]{2,1,0:T(8,128)(2,1)S(1)}, bf16[3,24,2048]{2,1,0:T(8,128)(2,1)S(1)}, u32[]{:S(2)}, u32[]{:S(2)}) collective-permute-start(bf16[3,24,2048]{2,1,0:T(8,128)(2,1)S(1)} %pad_maximum_fusion.17), channel_id=1, source_target_pairs={{0,16},{16,0},{1,17},{17,1},{2,18},{18,2},{3,19},{19,3},{4,20},{20... | collective-permute-start | bytes 884744 | tf_op jit(solution)/shard_map/ppermute | solution.py:101
  79.4 7.1 %collective-permute-start.26 = (bf16[4,24,4096]{2,1,0:T(8,128)(2,1)S(1)}, bf16[4,24,4096]{2,1,0:T(8,128)(2,1)S(1)}, u32[]{:S(2)}, u32[]{:S(2)}) collective-permute-start(bf16[4,24,4096]{2,1,0:T(8,128)(2,1)S(1)} %slice_bitcast_fusion.11), channel_id=1, source_target_pairs={{0,1},{1,0},{2,3},{3,2},{4,5},{5,4},{6,7},{7,6},{8,9},{9,8},{10,11... | collective-permute-start | bytes 2359304 | tf_op jit(solution)/shard_map/ppermute | solution.py:101
  86.6 27.0 %collective-permute-start.27 = (bf16[24,4096]{1,0:T(8,128)(2,1)S(1)}, bf16[24,4096]{1,0:T(8,128)(2,1)S(1)}, u32[]{:S(2)}, u32[]{:S(2)}) collective-permute-start(bf16[24,4096]{1,0:T(8,128)(2,1)S(1)} %pad_maximum_fusion.18), channel_id=1, source_target_pairs={{0,4},{1,5},{2,6},{3,7},{4,0},{5,1},{6,2},{7,3},{8,12},{9,13},{10,... | collective-permute-start | bytes 589832 | tf_op jit(solution)/shard_map/ppermute | solution.py:101
  90.9 13.7 %collective-permute-start.29 = (bf16[2,24,2048]{2,1,0:T(8,128)(2,1)S(1)}, bf16[2,24,2048]{2,1,0:T(8,128)(2,1)S(1)}, u32[]{:S(2)}, u32[]{:S(2)}) collective-permute-start(bf16[2,24,2048]{2,1,0:T(8,128)(2,1)S(1)} %pad_maximum_fusion.19), channel_id=1, source_target_pairs={{0,16},{16,0},{1,17},{17,1},{2,18},{18,2},{3,19},{19,3},{4,20},{20... | collective-permute-start | bytes 589832 | tf_op jit(solution)/shard_map/ppermute | solution.py:101
  93.2 11.5 %collective-permute-start.34 = (bf16[2,24,2048]{2,1,0:T(8,128)(2,1)S(1)}, bf16[2,24,2048]{2,1,0:T(8,128)(2,1)S(1)}, u32[]{:S(2)}, u32[]{:S(2)}) collective-permute-start(bf16[2,24,2048]{2,1,0:T(8,128)(2,1)S(1)} %pad_maximum_fusion.22), channel_id=1, source_target_pairs={{0,2},{1,3},{2,0},{3,1},{4,6},{5,7},{6,4},{7,5},{8,10},{9,11},{10,... | collective-permute-start | bytes 589832 | tf_op jit(solution)/shard_map/ppermute | solution.py:101
  100.1 6.2 %collective-permute-start.32 = (bf16[24,4096]{1,0:T(8,128)(2,1)S(1)}, bf16[24,4096]{1,0:T(8,128)(2,1)S(1)}, u32[]{:S(2)}, u32[]{:S(2)}) collective-permute-start(bf16[24,4096]{1,0:T(8,128)(2,1)S(1)} %pad_maximum_fusion.20), channel_id=1, source_target_pairs={{0,4},{1,5},{2,6},{3,7},{4,0},{5,1},{6,2},{7,3},{8,12},{9,13},{10,... | collective-permute-start | bytes 589832 | tf_op jit(solution)/shard_map/ppermute | solution.py:101
  106.4 7.2 %collective-permute-start.33 = (bf16[24,4096]{1,0:T(8,128)(2,1)S(1)}, bf16[24,4096]{1,0:T(8,128)(2,1)S(1)}, u32[]{:S(2)}, u32[]{:S(2)}) collective-permute-start(bf16[24,4096]{1,0:T(8,128)(2,1)S(1)} %pad_maximum_fusion.21), channel_id=1, source_target_pairs={{0,2},{1,3},{2,0},{3,1},{4,6},{5,7},{6,4},{7,5},{8,10},{9,11},{10,... | collective-permute-start | bytes 589832 | tf_op jit(solution)/shard_map/ppermute | solution.py:101
  107.1 6.6 %collective-permute-start.35 = (bf16[24,4096]{1,0:T(8,128)(2,1)S(1)}, bf16[24,4096]{1,0:T(8,128)(2,1)S(1)}, u32[]{:S(2)}, u32[]{:S(2)}) collective-permute-start(bf16[24,4096]{1,0:T(8,128)(2,1)S(1)} %pad_maximum_fusion.23), channel_id=1, source_target_pairs={{0,16},{16,0},{1,17},{17,1},{2,18},{18,2},{3,19},{19,3},{4,20},{20... | collective-permute-start | bytes 589832 | tf_op jit(solution)/shard_map/ppermute | solution.py:101
  114.5 9.0 %collective-permute-start.40 = (bf16[24,4096]{1,0:T(8,128)(2,1)S(1)}, bf16[24,4096]{1,0:T(8,128)(2,1)S(1)}, u32[]{:S(2)}, u32[]{:S(2)}) collective-permute-start(bf16[24,4096]{1,0:T(8,128)(2,1)S(1)} %add_convert_fusion.1), channel_id=1, source_target_pairs={{0,8},{1,9},{2,10},{3,11},{4,12},{5,13},{6,14},{7,15},{8,0},{9,1},... | collective-permute-start | bytes 589832 | tf_op jit(solution)/shard_map/ppermute | solution.py:101
  115.3 8.2 %collective-permute-start.39 = (bf16[24,4096]{1,0:T(8,128)(2,1)S(1)}, bf16[24,4096]{1,0:T(8,128)(2,1)S(1)}, u32[]{:S(2)}, u32[]{:S(2)}) collective-permute-start(bf16[24,4096]{1,0:T(8,128)(2,1)S(1)} %pad_maximum_fusion.27), channel_id=1, source_target_pairs={{0,4},{1,5},{2,6},{3,7},{4,0},{5,1},{6,2},{7,3},{8,12},{9,13},{10,... | collective-permute-start | bytes 589832 | tf_op jit(solution)/shard_map/ppermute | solution.py:101
  116.0 7.5 %collective-permute-start.38 = (bf16[24,4096]{1,0:T(8,128)(2,1)S(1)}, bf16[24,4096]{1,0:T(8,128)(2,1)S(1)}, u32[]{:S(2)}, u32[]{:S(2)}) collective-permute-start(bf16[24,4096]{1,0:T(8,128)(2,1)S(1)} %pad_maximum_fusion.26), channel_id=1, source_target_pairs={{0,16},{16,0},{1,17},{17,1},{2,18},{18,2},{3,19},{19,3},{4,20},{20... | collective-permute-start | bytes 589832 | tf_op jit(solution)/shard_map/ppermute | solution.py:101
  117.0 6.5 %collective-permute-start.37 = (bf16[24,4096]{1,0:T(8,128)(2,1)S(1)}, bf16[24,4096]{1,0:T(8,128)(2,1)S(1)}, u32[]{:S(2)}, u32[]{:S(2)}) collective-permute-start(bf16[24,4096]{1,0:T(8,128)(2,1)S(1)} %pad_maximum_fusion.25), channel_id=1, source_target_pairs={{0,2},{1,3},{2,0},{3,1},{4,6},{5,7},{6,4},{7,5},{8,10},{9,11},{10,... | collective-permute-start | bytes 589832 | tf_op jit(solution)/shard_map/ppermute | solution.py:101
  (20 other events, 156.9 us)
